TPU v7x, 256 devices: a whole 4x4x8 slice. The times are simulated.
256 devices in a mesh: blk: 128 (over x_lo, z, y, core), rep: 2 (over x_hi).
Axes of the slice: x: 4 (x_hi: 2, x_lo: 2; x = x_hi * 2 + x_lo), y: 4, z: 8, core: 2. Of those that a mesh axis runs over, the one named last changes fastest.
Arguments:
- embeddings: bfloat16 [65536, 400], P('blk'), may hold values from -1.8 to 1.8
- relations: bfloat16 [2560, 400], replicated, may hold values from -3 to 3
- heads: int32 [3, 131072], P(None, ('blk', 'rep')), may hold values from 0 to 511
- tails: int32 [3, 131072], P(None, ('blk', 'rep')), may hold values from 0 to 511
- rels: int32 [3, 131072], P(None, ('blk', 'rep')), may hold values from 0 to 2559
- negatives: int32 [3, 512, 256], P(None, ('blk', 'rep')), may hold values from 0 to 511
- live: int32 [3, 256], P(None, ('blk', 'rep')), may hold values from 1 to 2
Outputs:
- gradient: float32 [65536, 400], P('blk')
- mean_loss: float32 [], replicated
All inputs are finite; a program needn't handle non-finite values.
Results may differ from a plain program's by a relative error of at most 0.0027.
Values may be sent and summed in bfloat16 or wider, within the bound.
No kernel may reach another device: no remote copies, remote signals or barrier semaphores. Data moves between devices by JAX's collectives and lax.ppermute only.
A program may use at most 64 MiB of HBM per device.

v0:
```python
import jax
import jax.numpy as jnp
from jax import lax
from jax.experimental import pallas as pl
from jax.experimental.pallas import tpu as pltpu
from jax.sharding import PartitionSpec as P

STEPS = 3
F32 = jnp.float32
BF16 = jnp.bfloat16
NEVER = -1e30
TN = (((0,), (0,)), ((), ()))
NN = (((1,), (0,)), ((), ()))
NT = (((1,), (1,)), ((), ()))


def dot(a, b, dims):
    return lax.dot_general(a, b, dims, preferred_element_type=F32)


def one_hot(row, size):
    hit = lax.broadcasted_iota(jnp.int32, (size, row.shape[1]), 0) == row
    return jnp.where(hit, 1.0, 0.0).astype(BF16)


def gather_relations(rel_t, row, hot_ref):
    block = 256
    low = one_hot(row & (block - 1), block)
    high = row >> 8
    for j in range(rel_t.shape[1] // block):
        here = jnp.where(high == j, 1.0, 0.0).astype(BF16)
        hot_ref[j * block:(j + 1) * block, :] = low * here
    return dot(rel_t[...], hot_ref[...], NN)


def make_query(h_ref, r_ref, q_ref):
    half = h_ref.shape[0] // 2
    step = 40
    for c in range(0, half, step):
        re, im = slice(c, c + step), slice(half + c, half + c + step)
        h_re, h_im, r_re, r_im = h_ref[re, :], h_ref[im, :], r_ref[re, :], r_ref[im, :]
        q_ref[re, :] = h_re * r_re - h_im * r_im
        q_ref[im, :] = h_re * r_im + h_im * r_re


def head_grad(d_ref, r_ref, scale, out_ref):
    half = d_ref.shape[0] // 2
    step = 40
    for c in range(0, half, step):
        re, im = slice(c, c + step), slice(half + c, half + c + step)
        d_re, d_im, r_re, r_im = d_ref[re, :] * scale, d_ref[im, :] * scale, r_ref[re, :], r_ref[im, :]
        out_ref[re, :] = d_re * r_re + d_im * r_im
        out_ref[im, :] = d_im * r_re - d_re * r_im


def halves(row):
    half = row.shape[1] // 2
    return row[:, :half], row[:, half:]


def log_counts(neg_rows, entities, out_ref):
    for g, neg_row in enumerate(neg_rows):
        hot = one_hot(neg_row, entities)
        count = dot(hot, jnp.ones((neg_row.shape[1], 128), BF16), NN)
        out_ref[:, g * 128:(g + 1) * 128] = jnp.where(count > 0.5, jnp.log(jnp.maximum(count, 1.0)), NEVER)


def softmax_terms(s_ref, log_ref, tail_row, q_ref):
    entities, edges = s_ref.shape
    step = 32
    iota = lax.broadcasted_iota(jnp.int32, (step, edges), 0)
    top = jnp.full((8, edges), NEVER, F32)
    pos = jnp.zeros((8, edges), F32)
    for c in range(0, entities, step):
        s = s_ref[c:c + step, :]
        hit = jnp.where(iota == tail_row - c, s, 0.0)
        first, second = log_ref[c:c + step, :128], log_ref[c:c + step, 128:]
        log = jnp.concatenate([first, first, second, second], axis=1)
        s = s + log
        s_ref[c:c + step, :] = s
        for k in range(0, step, 8):
            pos = pos + hit[k:k + 8, :]
            top = jnp.maximum(top, s[k:k + 8, :])
    positive = jnp.sum(pos, axis=0, keepdims=True)
    top = jnp.max(top, axis=0, keepdims=True)
    total = jnp.zeros((8, edges), F32)
    for c in range(0, entities, step):
        e = jnp.exp(s_ref[c:c + step, :] - top)
        s_ref[c:c + step, :] = e
        for k in range(0, step, 8):
            total = total + e[k:k + 8, :]
    total = jnp.sum(total, axis=0, keepdims=True)
    share = 1.0 / total
    for c in range(0, entities, step):
        p = s_ref[c:c + step, :] * share
        q_ref[c:c + step, :] = jnp.where(iota == tail_row - c, p - 1.0, p).astype(BF16)
    gap = jnp.log(total) + top - positive
    low = jnp.exp(-jnp.abs(gap))
    loss = jnp.maximum(gap, 0.0) + jnp.log(1.0 + low)
    miss = jnp.where(gap >= 0.0, 1.0, low) / (1.0 + low)
    return loss, miss


def live_row(count, edges):
    group = jnp.where(lax.broadcasted_iota(jnp.int32, (1, edges), 1) < edges // 2, 0, 1)
    return jnp.where(group < count, 1.0, 0.0)


HEADS, TAILS, RELS, NEGS, LIVE, EXTRA = 0, 1, 2, 3, 16, 32


def unpacked(block, width, kind, step):
    rows = block[width:width + EXTRA, :].astype(F32)
    k = (kind * 2 + step - 1) * 2
    return (rows[k:k + 1, :] * 256.0 + rows[k + 1:k + 2, :]).astype(jnp.int32)


def live_counts(block, width, step):
    k = LIVE + step - 1
    return block[width:width + EXTRA, :].astype(F32)[k:k + 1, :].astype(jnp.int32)


def split(x):
    high = x.astype(BF16)
    return high, (x - high.astype(F32)).astype(BF16)


def pack_kernel(emb_in, heads_in, tails_in, rels_in, negatives_in, live_in, block,
                heads, tails, rels, negatives, live_groups, rows, sems):
    width = emb_in.shape[0]
    pairs = ((heads_in, heads), (tails_in, tails), (rels_in, rels), (negatives_in, negatives), (live_in, live_groups),
             (emb_in, block.at[:width, :]))
    copies = [pltpu.make_async_copy(a, b, sems.at[k]) for k, (a, b) in enumerate(pairs)]
    for copy in copies:
        copy.start()
    for copy in copies[:5]:
        copy.wait()
    edges = heads.shape[1]
    half = edges // 2
    rows[...] = jnp.zeros(rows.shape, F32)
    for step in (1, 2):
        for kind, ref in ((HEADS, heads), (TAILS, tails), (RELS, rels)):
            k = (kind * 2 + step - 1) * 2
            row = ref[step:step + 1, :]
            rows[k:k + 1, :] = (row >> 8).astype(F32)
            rows[k + 1:k + 2, :] = (row & 255).astype(F32)
        k = (NEGS * 2 + step - 1) * 2
        for g in range(2):
            row = negatives[step, g:g + 1, :]
            rows[k:k + 1, g * half:(g + 1) * half] = (row >> 8).astype(F32)
            rows[k + 1:k + 2, g * half:(g + 1) * half] = (row & 255).astype(F32)
        k = LIVE + step - 1
        rows[k:k + 1, :] = jnp.broadcast_to(live_groups[:, step:step + 1], (1, edges)).astype(F32)
    block[width:width + EXTRA, :] = rows[...].astype(BF16)
    copies[5].wait()


def prepare_kernel(emb, rel, heads, tails, rels, negatives, live_groups, grad, sums, q1, q2, r1, r2, log1, log2, hot, hf, rf, qf, sf, qq, log):
    edges, entities = heads.shape[1], emb.shape[1]
    head_hot = one_hot(heads[0:1, :], entities)
    hf[...] = dot(emb[...], head_hot, NN)
    rf[...] = gather_relations(rel, rels[0:1, :], hot)
    make_query(hf, rf, qf)
    q = qf[...].astype(BF16)
    sf[...] = dot(emb[...], q, TN)
    log_counts([negatives[0, g:g + 1, :] for g in range(2)], entities, log)
    loss, miss = softmax_terms(sf, log, tails[0:1, :], qq)
    live = live_row(live_groups[:, 0:1], edges)
    scale = miss * live * (1.0 / 256.0)
    high, low = split(q.astype(F32) * scale)
    g = dot(high, qq[...], NT) + dot(low, qq[...], NT)
    hf[...] = dot(emb[...], qq[...], NN)
    head_grad(hf, rf, scale, qf)
    high, low = split(qf[...])
    grad[...] = g + dot(high, head_hot, NT) + dot(low, head_hot, NT)
    sums[0:1, :] = loss * live
    sums[1:2, :] = live
    for step, q_out, r_out, log_out in ((1, q1, r1, log1), (2, q2, r2, log2)):
        rf[...] = gather_relations(rel, rels[step:step + 1, :], hot)
        hf[...] = dot(emb[...], one_hot(heads[step:step + 1, :], entities), NN)
        make_query(hf, rf, qf)
        log_counts([negatives[step, g:g + 1, :] for g in range(2)], entities, log_out)
        r_out[...] = rf[...].astype(BF16)
        q_out[...] = qf[...].astype(BF16)


def head_bucket(step, tail, q_in, r_in, log, heads, tails, live_groups, acc, hf, rf, qf, sf, qq):
    edges, (width, entities) = heads.shape[1], acc.shape
    sf[...] = dot(tail[:width, :], q_in[...], TN)
    loss, miss = softmax_terms(sf, log, tails[step:step + 1, :], qq)
    live = live_row(live_groups[:, step:step + 1], edges)
    hf[...] = dot(tail[:width, :], qq[...], NN)
    rf[...] = r_in[...].astype(F32)
    head_grad(hf, rf, miss * live * (1.0 / 256.0), qf)
    high, low = split(qf[...])
    head_hot = one_hot(heads[step:step + 1, :], entities)
    acc[...] += dot(high, head_hot, NT) + dot(low, head_hot, NT)
    return loss * live, live


def far_terms(step, rel, block, r_out, log_out, hot):
    width, entities = rel.shape[0], log_out.shape[0]
    r_out[...] = gather_relations(rel, unpacked(block, width, RELS, step), hot)
    log_counts(halves(unpacked(block, width, NEGS, step)), entities, log_out)


def tail_bucket(step, emb, block, rf, log, acc, hf, qf, sf, qq):
    (width, entities), edges = emb.shape, block.shape[1]
    hf[...] = dot(block[:width, :], one_hot(unpacked(block, width, HEADS, step), entities), NN)
    make_query(hf, rf, qf)
    q = qf[...].astype(BF16)
    sf[...] = dot(emb[...], q, TN)
    loss, miss = softmax_terms(sf, log, unpacked(block, width, TAILS, step), qq)
    scale = miss * live_row(live_counts(block, width, step), edges) * (1.0 / 256.0)
    high, low = split(q.astype(F32) * scale)
    acc[...] += dot(high, qq[...], NT) + dot(low, qq[...], NT)


def heads2_kernel(prev2, q2, r2, log2, heads, tails, live_groups, part, sums, grad, sums_out, hf, rf, qf, sf, qq):
    grad[...] = part[...]
    loss, live = head_bucket(2, prev2, q2, r2, log2, heads, tails, live_groups, grad, hf, rf, qf, sf, qq)
    sums_out[0:1, :] = sums[0:1, :] + loss
    sums_out[1:2, :] = sums[1:2, :] + live


def heads1_kernel(sibling, swapped, q1, r1, log1, heads, tails, live_groups, part, sums, grad, row,
                  hf, rf, qf, sf, qq, prev1):
    grad[...] = part[...]
    prev1[...] = jnp.where(lax.axis_index("blk") & 1 == 0, swapped[...], sibling[...])
    loss, live = head_bucket(1, prev1, q1, r1, log1, heads, tails, live_groups, grad, hf, rf, qf, sf, qq)
    loss_all = jnp.sum(sums[0:1, :] + loss, axis=1, keepdims=True)
    live_all = jnp.sum(sums[1:2, :] + live, axis=1, keepdims=True)
    lane = lax.broadcasted_iota(jnp.int32, row.shape, 1)
    row[...] = jnp.where(lane == 0, loss_all, jnp.where(lane == 1, live_all, 0.0))


def after_kernel(block, row, block_out):
    pass


def tails2_kernel(rel, emb, next2, part, grad, hot, hf, rf, qf, sf, qq, log):
    grad[...] = part[...]
    far_terms(2, rel, next2, rf, log, hot)
    tail_bucket(2, emb, next2, rf, log, grad, hf, qf, sf, qq)


def tails1_kernel(rel, emb, sibling, swapped, part, row, core_row, grad, rows, hot, hf, rf, qf, sf, qq, acc, next1, log):
    next1[...] = jnp.where(lax.axis_index("blk") & 1 == 0, sibling[...], swapped[...])
    acc[...] = part[...]
    far_terms(1, rel, next1, rf, log, hot)
    tail_bucket(1, emb, next1, rf, log, acc, hf, qf, sf, qq)
    grad[...] = acc[...].astype(BF16)
    rows[...] = jnp.broadcast_to(row[0:1, :] + core_row[0:1, :], rows.shape)


def finish_kernel(own, other, rows, grad, mean):
    grad[...] = own[...].astype(F32) + other[...].astype(F32)
    total = jnp.sum(rows[...], axis=0, keepdims=True)
    mean[...] = total[:, 0:1] / total[:, 1:2]


def kernel(body, outs, scratch, flops, spaces, mib=48, aliases={}):
    return pl.pallas_call(
        body,
        out_shape=[jax.ShapeDtypeStruct(s, t) for s, t in outs],
        in_specs=[pl.BlockSpec(memory_space=m) for m in spaces],
        input_output_aliases=aliases,
        scratch_shapes=[pltpu.VMEM(*s) if isinstance(s, tuple) else s for s in scratch],
        compiler_params=pltpu.CompilerParams(vmem_limit_bytes=mib * 2**20),
        cost_estimate=pl.CostEstimate(flops=flops, bytes_accessed=4 * 2**20, transcendentals=0),
    )


def shifted(x, by):
    peers = lax.axis_size("blk")
    return lax.ppermute(x, "blk", [(i, (i + by) % peers) for i in range(peers)])


def exchanged(x):
    return lax.ppermute(x, "blk", [(i, i ^ 1) for i in range(lax.axis_size("blk"))])


def per_device(embeddings, relations, heads, tails, rels, negatives, live):
    edges = heads.shape[1]
    entities, width = embeddings.shape
    n_rel = relations.shape[0]
    blocks = lax.axis_size("blk")
    emb = embeddings.T
    rel = relations.T
    here = pltpu.VMEM
    big, grads, logs, rows_of = (width, edges), (width, entities), (entities, 256), (8, 128)
    work = [(big, F32), (big, F32), (big, F32), ((entities, edges), F32), ((entities, edges), BF16)]
    hot = ((n_rel, edges), BF16)
    raw = (heads, tails, rels, negatives, live.T)
    sent = ((width + EXTRA, edges), BF16)
    (block,) = kernel(
        pack_kernel, [sent],
        [(x.shape, x.dtype) for x in raw] + [((EXTRA, edges), F32), pltpu.SemaphoreType.DMA((len(raw) + 1,))],
        2 * 10**9, [pltpu.HBM] * (len(raw) + 1), 56,
    )(emb, *raw)
    prev2 = shifted(block, 2)
    next2 = shifted(block, -2)
    sibling = exchanged(block)
    part, sums, q1, q2, r1, r2, log1, log2 = kernel(
        prepare_kernel,
        [(grads, F32), ((8, edges), F32)] + [(big, BF16)] * 4 + [(logs, F32)] * 2,
        [hot] + work + [(logs, F32)], 20 * 10**9, [here] * 7)(emb, rel, *raw)
    own_lists = (heads, tails, live.T)
    swapped_prev = exchanged(prev2)
    part, sums = kernel(heads2_kernel, [(grads, F32), ((8, edges), F32)], work, 8 * 10**9, [here] * 9)(
        prev2, q2, r2, log2, *own_lists, part, sums)
    part, row = kernel(heads1_kernel, [(grads, F32), (rows_of, F32)], work + [sent], 3 * 10**9, [here] * 10)(
        sibling, swapped_prev, q1, r1, log1, *own_lists, part, sums)
    core_row = exchanged(row)
    (next2,) = kernel(after_kernel, [sent], [], 10**6, [here] * 2, aliases={0: 0})(next2, row)
    swapped_next = exchanged(next2)
    (part,) = kernel(tails2_kernel, [(grads, F32)], [hot] + work + [(logs, F32)], 10 * 10**9, [here] * 4)(
        rel, emb, next2, part)
    own, rows = kernel(
        tails1_kernel, [(grads, BF16), ((blocks, 128), F32)], [hot] + work + [(grads, F32), sent, (logs, F32)],
        3 * 10**9, [here] * 7,
    )(rel, emb, sibling, swapped_next, part, row, core_row)
    other = lax.ppermute(own, "rep", [(0, 1), (1, 0)])
    rows = lax.all_to_all(rows, ("blk", "rep"), 0, 0, tiled=True,
                          axis_index_groups=[[4 * i + 2 * k + r for i in range(blocks // 2) for r in (0, 1)] for k in (0, 1)])
    grad, mean = kernel(finish_kernel, [(grads, F32), ((1, 1), F32)], [], 10**6, [here] * 3)(own, other, rows)
    return grad.T, mean[0, 0]


def solution(mesh):
    placed = (
        P("blk", None),
        P(),
        P(None, ("blk", "rep")),
        P(None, ("blk", "rep")),
        P(None, ("blk", "rep")),
        P(None, ("blk", "rep"), None),
        P(None, ("blk", "rep")),
    )
    return jax.shard_map(
        per_device, mesh=mesh, in_specs=placed, out_specs=(P("blk", None), P()), check_vma=False
    )
```

profile of v0, /device:TPU:1, one launch (start us, length us, event | category | flops | bytes accessed | tf_op | source)
XLA Modules:
  0.0 55.7 jit_solution(3829656220885583817)
XLA Ops:
  0.6 0.0 copy-start
  0.6 0.0 copy-start.1
  0.7 0.0 copy-start.2
  0.7 0.0 copy-start.3
  0.7 0.0 copy-start.4
  0.7 0.0 copy-start.5
  0.7 0.0 copy-start.6
  0.7 2.0 %shard_map.86 = bf16[432,512]{1,0:T(8,128)(2,1)} custom-call(bf16[400,512]{1,0:T(8,128)(2,1)} %bitcast.14, s32[3,512]{1,0:T(4,128)} %heads.5, s32[3,512]{1,0:T(4,128)} %tails.5, s32[3,512]{1,0:T(4,128)} %rels.1, s32[3,2,256]{2,1,0:T(2,128)} %negatives.1, s32[1,3]{1,0:T(1,128)} %bitcast.18), custom_call_target="tpu_custom_call" | custom-call | flops 2000000000 | bytes 4194304 | tf_op jit(solution)/shard_map/pallas_call | solution.py:296
  2.7 2.2 %collective-permute-start.2 = (bf16[432,512]{1,0:T(8,128)(2,1)}, bf16[432,512]{1,0:T(8,128)(2,1)S(1)}, u32[]{:S(2)}, u32[]{:S(2)}) collective-permute-start(bf16[432,512]{1,0:T(8,128)(2,1)} %shard_map.86), channel_id=1, source_target_pairs={{0,4},{2,6},{4,8},{6,10},{8,12},{10,14},{12,16},{14,18},{16,20},{1... | collective-permute-start | bytes 1327112 | tf_op jit(solution)/shard_map/ppermute | solution.py:276
  4.9 1.2 %collective-permute-start = (bf16[432,512]{1,0:T(8,128)(2,1)}, bf16[432,512]{1,0:T(8,128)(2,1)S(1)}, u32[]{:S(2)}, u32[]{:S(2)}) collective-permute-start(bf16[432,512]{1,0:T(8,128)(2,1)} %shard_map.86), channel_id=1, source_target_pairs={{0,2},{2,0},{4,6},{6,4},{8,10},{10,8},{12,14},{14,12},{16,18},{18,... | collective-permute-start | bytes 1327112 | tf_op jit(solution)/shard_map/ppermute | solution.py:280
  6.1 7.2 %collective-permute-start.1 = (bf16[432,512]{1,0:T(8,128)(2,1)}, bf16[432,512]{1,0:T(8,128)(2,1)S(1)}, u32[]{:S(2)}, u32[]{:S(2)}) collective-permute-start(bf16[432,512]{1,0:T(8,128)(2,1)} %shard_map.86), channel_id=1, source_target_pairs={{0,252},{2,254},{4,0},{6,2},{8,4},{10,6},{12,8},{14,10},{16,12},{1... | collective-permute-start | bytes 1327112 | tf_op jit(solution)/shard_map/ppermute | solution.py:276
  13.4 0.0 copy-done
  13.4 0.0 copy-done.1
  13.4 0.0 copy-done.2
  13.4 0.0 copy-done.3
  13.4 0.0 copy-done.4
  13.4 0.0 copy-done.5
  13.4 0.0 copy-done.6
  13.4 7.0 %shard_map.87 = (f32[400,512]{1,0:T(8,128)S(1)}, f32[8,512]{1,0:T(8,128)S(1)}, bf16[400,512]{1,0:T(8,128)(2,1)S(1)}, bf16[400,512]{1,0:T(8,128)(2,1)S(1)}, bf16[...) custom-call(bf16[400,512]{1,0:T(8,128)(2,1)S(1)} %bitcast.15, ...), custom_call_target="tpu_custom_call" | custom-call | flops 20000000000 | bytes 4194304 | tf_op jit(solution)/shard_map/pallas_call | solution.py:304
  20.4 2.2 %collective-permute-done.2.prev2 = bf16[432,512]{1,0:T(8,128)(2,1)S(1)} collective-permute-done((bf16[432,512]{1,0:T(8,128)(2,1)}, bf16[432,512]{1,0:T(8,128)(2,1)S(1)}, u32[]{:S(2)}, u32[]{:S(2)}) %collective-permute-start.2) | collective-permute-done | bytes 442400 | tf_op jit(solution)/shard_map/ppermute | solution.py:276
  22.7 1.2 %collective-permute-start.3 = (bf16[432,512]{1,0:T(8,128)(2,1)S(1)}, bf16[432,512]{1,0:T(8,128)(2,1)S(1)}, u32[]{:S(2)}, u32[]{:S(2)}) collective-permute-start(bf16[432,512]{1,0:T(8,128)(2,1)S(1)} %collective-permute-done.2.prev2), channel_id=1, source_target_pairs={{0,2},{2,0},{4,6},{6,4},{8,10},{10,8},{12,14},{14,12},{16,18},{18,... | collective-permute-start | bytes 1327112 | tf_op jit(solution)/shard_map/ppermute | solution.py:280
  23.9 1.9 %shard_map.88 = (f32[400,512]{1,0:T(8,128)S(1)}, f32[8,512]{1,0:T(8,128)S(1)}) custom-call(bf16[432,512]{1,0:T(8,128)(2,1)S(1)} %collective-permute-done.2.prev2, bf16[400,512]{1,0:T(8,128)(2,1)S(1)} %get-tuple-element.21.q2, bf16[400,512]{1,0:T(8,128)(2,1)S(1)} %get-tuple-element.22.r2, f32[512,256]{1,0:T(8,128)S(1)} %get-tuple-element.23.log2, ...), custom_call_target="tpu_custom_call" | custom-call | flops 8000000000 | bytes 4194304 | tf_op jit(solution)/shard_map/pallas_call | solution.py:310
  25.8 0.0 collective-permute-done.sibling
  25.8 0.0 collective-permute-done.3.swapped
  25.8 1.9 %shard_map.89 = (f32[400,512]{1,0:T(8,128)S(1)}, f32[8,128]{1,0:T(8,128)S(1)}) custom-call(bf16[432,512]{1,0:T(8,128)(2,1)S(1)} %collective-permute-done.sibling, bf16[432,512]{1,0:T(8,128)(2,1)S(1)} %collective-permute-done.3.swapped, bf16[400,512]{1,0:T(8,128)(2,1)S(1)} %get-tuple-element.18.q1, bf16[400,512]{1,0:T(8,128)(2,1)S(1)} %get-tuple-element.19.r1, ...), custom_call_target="tpu_custom_call" | custom-call | flops 3000000000 | bytes 4194304 | tf_op jit(solution)/shard_map/pallas_call | solution.py:312
  27.8 0.1 collective-permute-start.5
  27.9 0.0 collective-permute-done.1.block
  27.9 0.5 collective-permute-start.4
  28.4 3.1 %shard_map.91.part = f32[400,512]{1,0:T(8,128)S(1)} custom-call(bf16[400,2560]{1,0:T(8,128)(2,1)S(1)} %bitcast.12, bf16[400,512]{1,0:T(8,128)(2,1)S(1)} %bitcast.16, bf16[432,512]{1,0:T(8,128)(2,1)S(1)} %shard_map.90.next2, f32[400,512]{1,0:T(8,128)S(1)} %get-tuple-element.29.part), custom_call_target="tpu_custom_call" | custom-call | flops 10000000000 | bytes 4194304 | tf_op jit(solution)/shard_map/pallas_call | solution.py:317
  31.5 0.0 collective-permute-done.5.core_row
  31.5 0.0 collective-permute-done.4.swapped
  31.6 3.2 %shard_map.92 = (bf16[400,512]{1,0:T(8,128)(2,1)S(1)}, f32[128,128]{1,0:T(8,128)S(1)}) custom-call(bf16[400,2560]{1,0:T(8,128)(2,1)S(1)} %bitcast.13, bf16[400,512]{1,0:T(8,128)(2,1)S(1)} %bitcast.17, bf16[432,512]{1,0:T(8,128)(2,1)S(1)} %collective-permute-done.sibling, bf16[432,512]{1,0:T(8,128)(2,1)S(1)} %collective-permute-done.4.swapped, ...), custom_call_target="tpu_custom_call" | custom-call | flops 3000000000 | bytes 4194304 | tf_op jit(solution)/shard_map/pallas_call | solution.py:319
  34.7 2.5 %collective-permute-start.6 = (bf16[400,512]{1,0:T(8,128)(2,1)S(1)}, bf16[400,512]{1,0:T(8,128)(2,1)S(1)}, u32[]{:S(2)}, u32[]{:S(2)}) collective-permute-start(bf16[400,512]{1,0:T(8,128)(2,1)S(1)} %get-tuple-element.30.own), channel_id=1, source_target_pairs={{0,1},{1,0},{2,3},{3,2},{4,5},{5,4},{6,7},{7,6},{8,9},{9,8},{10,11... | collective-permute-start | bytes 1228808 | tf_op jit(solution)/shard_map/ppermute | solution.py:323
  37.3 17.4 %all_to_all.11 = f32[128,1,128]{2,1,0:T(1,128)S(1)} all-to-all(f32[128,1,128]{2,1,0:T(1,128)S(1)} %bitcast.10), channel_id=1, replica_groups={{0,1,4,5,8,9,12,13,16,17,20,21,24,25,28,29,32,33,36,37,40,41,44,45,48,4..., dimensions={0} | all-to-all | bytes 131072 | tf_op jit(solution)/shard_map/all_to_all | solution.py:324
  54.7 0.0 collective-permute-done.6.other
  54.7 1.0 %shard_map.93 = (f32[400,512]{1,0:T(8,128)}, f32[1,1]{1,0:T(1,128)}) custom-call(bf16[400,512]{1,0:T(8,128)(2,1)S(1)} %get-tuple-element.30.own, bf16[400,512]{1,0:T(8,128)(2,1)S(1)} %collective-permute-done.6.other, f32[128,128]{1,0:T(8,128)S(1)} %bitcast.9), custom_call_target="tpu_custom_call" | custom-call | flops 1000000 | bytes 4194304 | tf_op jit(solution)/shard_map/pallas_call | solution.py:326
  (1 shorter events, 0.0 us)
Async XLA Ops:
  0.6 12.7 %copy-start = (bf16[2560,400]{0,1:T(8,128)(2,1)S(1)}, bf16[2560,400]{0,1:T(8,128)(2,1)}, u32[]{:S(2)}) copy-start(bf16[2560,400]{0,1:T(8,128)(2,1)} %param.8) | copy-start | bytes 6144004
  0.6 12.7 %copy-start.1 = (bf16[512,400]{0,1:T(8,128)(2,1)S(1)}, bf16[512,400]{0,1:T(8,128)(2,1)}, u32[]{:S(2)}) copy-start(bf16[512,400]{0,1:T(8,128)(2,1)} %param.7) | copy-start | bytes 1228804
  0.7 12.7 %copy-start.2 = (s32[3,512]{1,0:T(4,128)S(1)}, s32[3,512]{1,0:T(4,128)}, u32[]{:S(2)}) copy-start(s32[3,512]{1,0:T(4,128)} %rels.1) | copy-start | bytes 18436
  0.7 12.7 %copy-start.3 = (s32[3,512]{1,0:T(4,128)S(1)}, s32[3,512]{1,0:T(4,128)}, u32[]{:S(2)}) copy-start(s32[3,512]{1,0:T(4,128)} %heads.5) | copy-start | bytes 18436
  0.7 12.7 %copy-start.4 = (s32[3,512]{1,0:T(4,128)S(1)}, s32[3,512]{1,0:T(4,128)}, u32[]{:S(2)}) copy-start(s32[3,512]{1,0:T(4,128)} %tails.5) | copy-start | bytes 18436
  0.7 12.7 %copy-start.5 = (s32[3,2,256]{2,1,0:T(2,128)S(1)}, s32[3,2,256]{2,1,0:T(2,128)}, u32[]{:S(2)}) copy-start(s32[3,2,256]{2,1,0:T(2,128)} %negatives.1) | copy-start | bytes 18436
  0.7 12.7 %copy-start.6 = (s32[3,1]{0,1:T(1,128)S(1)}, s32[3,1]{0,1:T(1,128)}, u32[]{:S(2)}) copy-start(s32[3,1]{0,1:T(1,128)} %param.13) | copy-start | bytes 40
  2.7 20.0 %collective-permute-start.2 = (bf16[432,512]{1,0:T(8,128)(2,1)}, bf16[432,512]{1,0:T(8,128)(2,1)S(1)}, u32[]{:S(2)}, u32[]{:S(2)}) collective-permute-start(bf16[432,512]{1,0:T(8,128)(2,1)} %shard_map.86), channel_id=1, source_target_pairs={{0,4},{2,6},{4,8},{6,10},{8,12},{10,14},{12,16},{14,18},{16,20},{1... | collective-permute-start | bytes 1327112 | tf_op jit(solution)/shard_map/ppermute | solution.py:276
  4.9 20.9 %collective-permute-start = (bf16[432,512]{1,0:T(8,128)(2,1)}, bf16[432,512]{1,0:T(8,128)(2,1)S(1)}, u32[]{:S(2)}, u32[]{:S(2)}) collective-permute-start(bf16[432,512]{1,0:T(8,128)(2,1)} %shard_map.86), channel_id=1, source_target_pairs={{0,2},{2,0},{4,6},{6,4},{8,10},{10,8},{12,14},{14,12},{16,18},{18,... | collective-permute-start | bytes 1327112 | tf_op jit(solution)/shard_map/ppermute | solution.py:280
  6.1 21.8 %collective-permute-start.1 = (bf16[432,512]{1,0:T(8,128)(2,1)}, bf16[432,512]{1,0:T(8,128)(2,1)S(1)}, u32[]{:S(2)}, u32[]{:S(2)}) collective-permute-start(bf16[432,512]{1,0:T(8,128)(2,1)} %shard_map.86), channel_id=1, source_target_pairs={{0,252},{2,254},{4,0},{6,2},{8,4},{10,6},{12,8},{14,10},{16,12},{1... | collective-permute-start | bytes 1327112 | tf_op jit(solution)/shard_map/ppermute | solution.py:276
  22.7 3.2 %collective-permute-start.3 = (bf16[432,512]{1,0:T(8,128)(2,1)S(1)}, bf16[432,512]{1,0:T(8,128)(2,1)S(1)}, u32[]{:S(2)}, u32[]{:S(2)}) collective-permute-start(bf16[432,512]{1,0:T(8,128)(2,1)S(1)} %collective-permute-done.2.prev2), channel_id=1, source_target_pairs={{0,2},{2,0},{4,6},{6,4},{8,10},{10,8},{12,14},{14,12},{16,18},{18,... | collective-permute-start | bytes 1327112 | tf_op jit(solution)/shard_map/ppermute | solution.py:280
  27.8 3.8 %collective-permute-start.5 = (f32[8,128]{1,0:T(8,128)S(1)}, f32[8,128]{1,0:T(8,128)S(1)}, u32[]{:S(2)}, u32[]{:S(2)}) collective-permute-start(f32[8,128]{1,0:T(8,128)S(1)} %get-tuple-element.28.row), channel_id=1, source_target_pairs={{0,2},{2,0},{4,6},{6,4},{8,10},{10,8},{12,14},{14,12},{16,18},{18,... | collective-permute-start | bytes 12296 | tf_op jit(solution)/shard_map/ppermute | solution.py:280
  27.9 3.6 %collective-permute-start.4 = (bf16[432,512]{1,0:T(8,128)(2,1)S(1)}, bf16[432,512]{1,0:T(8,128)(2,1)S(1)}, u32[]{:S(2)}, u32[]{:S(2)}) collective-permute-start(bf16[432,512]{1,0:T(8,128)(2,1)S(1)} %shard_map.90.next2), channel_id=1, source_target_pairs={{0,2},{2,0},{4,6},{6,4},{8,10},{10,8},{12,14},{14,12},{16,18},{18,... | collective-permute-start | bytes 1327112 | tf_op jit(solution)/shard_map/ppermute | solution.py:280
  34.7 19.9 %collective-permute-start.6 = (bf16[400,512]{1,0:T(8,128)(2,1)S(1)}, bf16[400,512]{1,0:T(8,128)(2,1)S(1)}, u32[]{:S(2)}, u32[]{:S(2)}) collective-permute-start(bf16[400,512]{1,0:T(8,128)(2,1)S(1)} %get-tuple-element.30.own), channel_id=1, source_target_pairs={{0,1},{1,0},{2,3},{3,2},{4,5},{5,4},{6,7},{7,6},{8,9},{9,8},{10,11... | collective-permute-start | bytes 1228808 | tf_op jit(solution)/shard_map/ppermute | solution.py:323
where the time goes:
time: 55.8 us; the launch traced here: 55.7 us
  Pallas kernels  20.2 us (36%)
  blocking collectives  17.4 us (31%)
  starting transfers between devices  15 us (27%)
  waiting for transfers between devices  2.26 us (4%)
  between operations  0.82 us (1%)
    all_to_all x1, blocking collectives, per_device(): lax.all_to_all(rows, ('blk', 'rep'), 0, 0, tiled=True, axis_index_groups=...  17.4 us
    ppermute x2, starting transfers between devices, shifted(): return lax.ppermute(x, 'blk', [(i, (i + by) % peers) for i in range(peers)])  9.43 us
    pallas_call x1, Pallas kernels, per_device(): kernel(prepare_kernel, [(grads, F32), ((8, edges), F32)] + [(big, BF16)]...  7.02 us
    pallas_call x1, Pallas kernels, per_device(): kernel(tails1_kernel, [(grads, BF16), ((blocks, 128), F32)], [hot] + work...  3.18 us
    pallas_call x1, Pallas kernels, per_device(): kernel(tails2_kernel, [(grads, F32)], [hot] + work + [(logs, F32)], 10 *...  3.14 us
    ppermute x4, starting transfers between devices, exchanged(): lax.ppermute(x, 'blk', [(i, i ^ 1) for i in range(lax.axis_size('blk'))])  3.02 us
    ppermute x1, starting transfers between devices, per_device(): other = lax.ppermute(own, 'rep', [(0, 1), (1, 0)])  2.53 us
    ppermute x2, waiting for transfers between devices, shifted(): return lax.ppermute(x, 'blk', [(i, (i + by) % peers) for i in range(peers)])  2.24 us
  transfers between devices with their start and end apart: 7, of which 1 were waited for; matrix products, arithmetic and copies ran while one was open for 0% of the time, Pallas kernels for 25%

commit v1 on v0

--- a/solution.py
+++ b/solution.py
@@ -226,7 +226,7 @@
 def heads1_kernel(sibling, swapped, q1, r1, log1, heads, tails, live_groups, part, sums, grad, row,
                   hf, rf, qf, sf, qq, prev1):
     grad[...] = part[...]
-    prev1[...] = jnp.where(lax.axis_index("blk") & 1 == 0, swapped[...], sibling[...])
+    prev1[...] = jnp.where(lax.axis_index("blk") & 1 == 0, swapped[...], sibling[:prev1.shape[0], :])
     loss, live = head_bucket(1, prev1, q1, r1, log1, heads, tails, live_groups, grad, hf, rf, qf, sf, qq)
     loss_all = jnp.sum(sums[0:1, :] + loss, axis=1, keepdims=True)
     live_all = jnp.sum(sums[1:2, :] + live, axis=1, keepdims=True)
@@ -298,7 +298,7 @@
         [(x.shape, x.dtype) for x in raw] + [((EXTRA, edges), F32), pltpu.SemaphoreType.DMA((len(raw) + 1,))],
         2 * 10**9, [pltpu.HBM] * (len(raw) + 1), 56,
     )(emb, *raw)
-    prev2 = shifted(block, 2)
+    prev2 = shifted(emb, 2)
     next2 = shifted(block, -2)
     sibling = exchanged(block)
     part, sums, q1, q2, r1, r2, log1, log2 = kernel(
@@ -309,7 +309,7 @@
     swapped_prev = exchanged(prev2)
     part, sums = kernel(heads2_kernel, [(grads, F32), ((8, edges), F32)], work, 8 * 10**9, [here] * 9)(
         prev2, q2, r2, log2, *own_lists, part, sums)
-    part, row = kernel(heads1_kernel, [(grads, F32), (rows_of, F32)], work + [sent], 3 * 10**9, [here] * 10)(
+    part, row = kernel(heads1_kernel, [(grads, F32), (rows_of, F32)], work + [(big, BF16)], 3 * 10**9, [here] * 10)(
         sibling, swapped_prev, q1, r1, log1, *own_lists, part, sums)
     core_row = exchanged(row)
     (next2,) = kernel(after_kernel, [sent], [], 10**6, [here] * 2, aliases={0: 0})(next2, row)

time: 55.8 us -> 54.8 us (0.982)
  waiting for transfers between devices: 2.26 us -> 0.02 us
  blocking collectives: 17.4 us -> 19.1 us
    ppermute x2, waiting for transfers between devices: 2.24 us -> 0.01 us  [shifted(): return lax.ppermute(x, 'blk', [(i, (i + by) % peers) for i in range(peers)])]
    all_to_all x1, blocking collectives: 17.4 us -> 19.1 us  [per_device(): lax.all_to_all(rows, ('blk', 'rep'), 0, 0, tiled=True, axis_index_groups=...]
  transfers between devices with their start and end apart: 7 -> 7, of which waited for: 1 -> 0; matrix products, arithmetic and copies ran while one was open for 0% -> 0% of each run, Pallas kernels for 25% -> 29%
where the time goes in v1:
time: 54.8 us; the launch traced here: 54.6 us
  Pallas kernels  20.2 us (37%)
  blocking collectives  19.1 us (35%)
  starting transfers between devices  14.5 us (26%)
  between operations  0.8 us (1%)
    all_to_all x1, blocking collectives, per_device(): lax.all_to_all(rows, ('blk', 'rep'), 0, 0, tiled=True, axis_index_groups=...  19.1 us
    ppermute x2, starting transfers between devices, shifted(): return lax.ppermute(x, 'blk', [(i, (i + by) % peers) for i in range(peers)])  9.43 us
    pallas_call x1, Pallas kernels, per_device(): kernel(prepare_kernel, [(grads, F32), ((8, edges), F32)] + [(big, BF16)]...  7.02 us
    pallas_call x1, Pallas kernels, per_device(): kernel(tails1_kernel, [(grads, BF16), ((blocks, 128), F32)], [hot] + work...  3.18 us
    pallas_call x1, Pallas kernels, per_device(): kernel(tails2_kernel, [(grads, F32)], [hot] + work + [(logs, F32)], 10 *...  3.14 us
    ppermute x1, starting transfers between devices, per_device(): other = lax.ppermute(own, 'rep', [(0, 1), (1, 0)])  2.53 us
    ppermute x4, starting transfers between devices, exchanged(): lax.ppermute(x, 'blk', [(i, i ^ 1) for i in range(lax.axis_size('blk'))])  2.51 us
    pallas_call x1, Pallas kernels, per_device(): kernel(pack_kernel, [sent], [(x.shape, x.dtype) for x in raw] + [((EXTRA,...  1.99 us
  transfers between devices with their start and end apart: 7, of which 0 were waited for; matrix products, arithmetic and copies ran while one was open for 0% of the time, Pallas kernels for 29%

profile of v1, /device:TPU:1, one launch (start us, length us, event | category | flops | bytes accessed | tf_op | source)
XLA Modules:
  0.0 54.6 jit_solution(9293146415848791043)
XLA Ops:
  0.6 2.2 %collective-permute-start.2 = (bf16[400,512]{1,0:T(8,128)(2,1)}, bf16[400,512]{1,0:T(8,128)(2,1)S(1)}, u32[]{:S(2)}, u32[]{:S(2)}) collective-permute-start(bf16[400,512]{1,0:T(8,128)(2,1)} %bitcast.14), channel_id=1, source_target_pairs={{0,4},{2,6},{4,8},{6,10},{8,12},{10,14},{12,16},{14,18},{16,20},{1... | collective-permute-start | bytes 1228808 | tf_op jit(solution)/shard_map/ppermute | solution.py:276
  2.8 0.0 copy-start
  2.8 0.0 copy-start.1
  2.8 0.0 copy-start.2
  2.8 0.0 copy-start.3
  2.8 0.0 copy-start.4
  2.9 0.0 copy-start.5
  2.9 0.0 copy-start.6
  2.9 2.0 %shard_map.86 = bf16[432,512]{1,0:T(8,128)(2,1)} custom-call(bf16[400,512]{1,0:T(8,128)(2,1)} %bitcast.15, s32[3,512]{1,0:T(4,128)} %heads.5, s32[3,512]{1,0:T(4,128)} %tails.5, s32[3,512]{1,0:T(4,128)} %rels.1, s32[3,2,256]{2,1,0:T(2,128)} %negatives.1, s32[1,3]{1,0:T(1,128)} %bitcast.19), custom_call_target="tpu_custom_call" | custom-call | flops 2000000000 | bytes 4194304 | tf_op jit(solution)/shard_map/pallas_call | solution.py:296
  4.9 1.2 %collective-permute-start = (bf16[432,512]{1,0:T(8,128)(2,1)}, bf16[432,512]{1,0:T(8,128)(2,1)S(1)}, u32[]{:S(2)}, u32[]{:S(2)}) collective-permute-start(bf16[432,512]{1,0:T(8,128)(2,1)} %shard_map.86), channel_id=1, source_target_pairs={{0,2},{2,0},{4,6},{6,4},{8,10},{10,8},{12,14},{14,12},{16,18},{18,... | collective-permute-start | bytes 1327112 | tf_op jit(solution)/shard_map/ppermute | solution.py:280
  6.1 7.2 %collective-permute-start.1 = (bf16[432,512]{1,0:T(8,128)(2,1)}, bf16[432,512]{1,0:T(8,128)(2,1)S(1)}, u32[]{:S(2)}, u32[]{:S(2)}) collective-permute-start(bf16[432,512]{1,0:T(8,128)(2,1)} %shard_map.86), channel_id=1, source_target_pairs={{0,252},{2,254},{4,0},{6,2},{8,4},{10,6},{12,8},{14,10},{16,12},{1... | collective-permute-start | bytes 1327112 | tf_op jit(solution)/shard_map/ppermute | solution.py:276
  13.4 0.0 copy-done
  13.4 0.0 copy-done.1
  13.4 0.0 copy-done.2
  13.4 0.0 copy-done.3
  13.4 0.0 copy-done.4
  13.4 0.0 copy-done.5
  13.4 0.0 copy-done.6
  13.4 7.0 %shard_map.87 = (f32[400,512]{1,0:T(8,128)S(1)}, f32[8,512]{1,0:T(8,128)S(1)}, bf16[400,512]{1,0:T(8,128)(2,1)S(1)}, bf16[400,512]{1,0:T(8,128)(2,1)S(1)}, bf16[...) custom-call(bf16[400,512]{1,0:T(8,128)(2,1)S(1)} %bitcast.16, ...), custom_call_target="tpu_custom_call" | custom-call | flops 20000000000 | bytes 4194304 | tf_op jit(solution)/shard_map/pallas_call | solution.py:304
  20.4 0.0 collective-permute-done.2.prev2
  20.4 0.7 %collective-permute-start.3 = (bf16[400,512]{1,0:T(8,128)(2,1)S(1)}, bf16[400,512]{1,0:T(8,128)(2,1)S(1)}, u32[]{:S(2)}, u32[]{:S(2)}) collective-permute-start(bf16[400,512]{1,0:T(8,128)(2,1)S(1)} %collective-permute-done.2.prev2), channel_id=1, source_target_pairs={{0,2},{2,0},{4,6},{6,4},{8,10},{10,8},{12,14},{14,12},{16,18},{18,... | collective-permute-start | bytes 1228808 | tf_op jit(solution)/shard_map/ppermute | solution.py:280
  21.1 1.9 %shard_map.88 = (f32[400,512]{1,0:T(8,128)S(1)}, f32[8,512]{1,0:T(8,128)S(1)}) custom-call(bf16[400,512]{1,0:T(8,128)(2,1)S(1)} %collective-permute-done.2.prev2, bf16[400,512]{1,0:T(8,128)(2,1)S(1)} %get-tuple-element.21.q2, bf16[400,512]{1,0:T(8,128)(2,1)S(1)} %get-tuple-element.22.r2, f32[512,256]{1,0:T(8,128)S(1)} %get-tuple-element.23.log2, ...), custom_call_target="tpu_custom_call" | custom-call | flops 8000000000 | bytes 4194304 | tf_op jit(solution)/shard_map/pallas_call | solution.py:310
  23.0 0.0 collective-permute-done.sibling
  23.1 0.0 collective-permute-done.3.swapped
  23.1 1.9 %shard_map.89 = (f32[400,512]{1,0:T(8,128)S(1)}, f32[8,128]{1,0:T(8,128)S(1)}) custom-call(bf16[432,512]{1,0:T(8,128)(2,1)S(1)} %collective-permute-done.sibling, bf16[400,512]{1,0:T(8,128)(2,1)S(1)} %collective-permute-done.3.swapped, bf16[400,512]{1,0:T(8,128)(2,1)S(1)} %get-tuple-element.18.q1, bf16[400,512]{1,0:T(8,128)(2,1)S(1)} %get-tuple-element.19.r1, ...), custom_call_target="tpu_custom_call" | custom-call | flops 3000000000 | bytes 4194304 | tf_op jit(solution)/shard_map/pallas_call | solution.py:312
  25.0 0.1 collective-permute-start.5
  25.1 0.0 collective-permute-done.1.block
  25.1 0.5 collective-permute-start.4
  25.6 3.1 %shard_map.91.part = f32[400,512]{1,0:T(8,128)S(1)} custom-call(bf16[400,2560]{1,0:T(8,128)(2,1)S(1)} %bitcast.12, bf16[400,512]{1,0:T(8,128)(2,1)S(1)} %bitcast.17, bf16[432,512]{1,0:T(8,128)(2,1)S(1)} %shard_map.90.next2, f32[400,512]{1,0:T(8,128)S(1)} %get-tuple-element.29.part), custom_call_target="tpu_custom_call" | custom-call | flops 10000000000 | bytes 4194304 | tf_op jit(solution)/shard_map/pallas_call | solution.py:317
  28.8 0.0 collective-permute-done.5.core_row
  28.8 0.0 collective-permute-done.4.swapped
  28.8 3.2 %shard_map.92 = (bf16[400,512]{1,0:T(8,128)(2,1)S(1)}, f32[128,128]{1,0:T(8,128)S(1)}) custom-call(bf16[400,2560]{1,0:T(8,128)(2,1)S(1)} %bitcast.13, bf16[400,512]{1,0:T(8,128)(2,1)S(1)} %bitcast.18, bf16[432,512]{1,0:T(8,128)(2,1)S(1)} %collective-permute-done.sibling, bf16[432,512]{1,0:T(8,128)(2,1)S(1)} %collective-permute-done.4.swapped, ...), custom_call_target="tpu_custom_call" | custom-call | flops 3000000000 | bytes 4194304 | tf_op jit(solution)/shard_map/pallas_call | solution.py:319
  32.0 2.5 %collective-permute-start.6 = (bf16[400,512]{1,0:T(8,128)(2,1)S(1)}, bf16[400,512]{1,0:T(8,128)(2,1)S(1)}, u32[]{:S(2)}, u32[]{:S(2)}) collective-permute-start(bf16[400,512]{1,0:T(8,128)(2,1)S(1)} %get-tuple-element.30.own), channel_id=1, source_target_pairs={{0,1},{1,0},{2,3},{3,2},{4,5},{5,4},{6,7},{7,6},{8,9},{9,8},{10,11... | collective-permute-start | bytes 1228808 | tf_op jit(solution)/shard_map/ppermute | solution.py:323
  34.5 19.1 %all_to_all.11 = f32[128,1,128]{2,1,0:T(1,128)S(1)} all-to-all(f32[128,1,128]{2,1,0:T(1,128)S(1)} %bitcast.10), channel_id=1, replica_groups={{0,1,4,5,8,9,12,13,16,17,20,21,24,25,28,29,32,33,36,37,40,41,44,45,48,4..., dimensions={0} | all-to-all | bytes 131072 | tf_op jit(solution)/shard_map/all_to_all | solution.py:324
  53.6 0.0 collective-permute-done.6.other
  53.6 1.0 %shard_map.93 = (f32[400,512]{1,0:T(8,128)}, f32[1,1]{1,0:T(1,128)}) custom-call(bf16[400,512]{1,0:T(8,128)(2,1)S(1)} %get-tuple-element.30.own, bf16[400,512]{1,0:T(8,128)(2,1)S(1)} %collective-permute-done.6.other, f32[128,128]{1,0:T(8,128)S(1)} %bitcast.9), custom_call_target="tpu_custom_call" | custom-call | flops 1000000 | bytes 4194304 | tf_op jit(solution)/shard_map/pallas_call | solution.py:326
  (1 shorter events, 0.0 us)
Async XLA Ops:
  0.6 19.8 %collective-permute-start.2 = (bf16[400,512]{1,0:T(8,128)(2,1)}, bf16[400,512]{1,0:T(8,128)(2,1)S(1)}, u32[]{:S(2)}, u32[]{:S(2)}) collective-permute-start(bf16[400,512]{1,0:T(8,128)(2,1)} %bitcast.14), channel_id=1, source_target_pairs={{0,4},{2,6},{4,8},{6,10},{8,12},{10,14},{12,16},{14,18},{16,20},{1... | collective-permute-start | bytes 1228808 | tf_op jit(solution)/shard_map/ppermute | solution.py:276
  2.8 10.5 %copy-start = (bf16[2560,400]{0,1:T(8,128)(2,1)S(1)}, bf16[2560,400]{0,1:T(8,128)(2,1)}, u32[]{:S(2)}) copy-start(bf16[2560,400]{0,1:T(8,128)(2,1)} %param.8) | copy-start | bytes 6144004
  2.8 10.5 %copy-start.1 = (bf16[512,400]{0,1:T(8,128)(2,1)S(1)}, bf16[512,400]{0,1:T(8,128)(2,1)}, u32[]{:S(2)}) copy-start(bf16[512,400]{0,1:T(8,128)(2,1)} %param.7) | copy-start | bytes 1228804
  2.8 10.5 %copy-start.2 = (s32[3,512]{1,0:T(4,128)S(1)}, s32[3,512]{1,0:T(4,128)}, u32[]{:S(2)}) copy-start(s32[3,512]{1,0:T(4,128)} %rels.1) | copy-start | bytes 18436
  2.8 10.5 %copy-start.3 = (s32[3,512]{1,0:T(4,128)S(1)}, s32[3,512]{1,0:T(4,128)}, u32[]{:S(2)}) copy-start(s32[3,512]{1,0:T(4,128)} %heads.5) | copy-start | bytes 18436
  2.8 10.5 %copy-start.4 = (s32[3,512]{1,0:T(4,128)S(1)}, s32[3,512]{1,0:T(4,128)}, u32[]{:S(2)}) copy-start(s32[3,512]{1,0:T(4,128)} %tails.5) | copy-start | bytes 18436
  2.9 10.5 %copy-start.5 = (s32[3,2,256]{2,1,0:T(2,128)S(1)}, s32[3,2,256]{2,1,0:T(2,128)}, u32[]{:S(2)}) copy-start(s32[3,2,256]{2,1,0:T(2,128)} %negatives.1) | copy-start | bytes 18436
  2.9 10.5 %copy-start.6 = (s32[3,1]{0,1:T(1,128)S(1)}, s32[3,1]{0,1:T(1,128)}, u32[]{:S(2)}) copy-start(s32[3,1]{0,1:T(1,128)} %param.13) | copy-start | bytes 40
  4.9 18.2 %collective-permute-start = (bf16[432,512]{1,0:T(8,128)(2,1)}, bf16[432,512]{1,0:T(8,128)(2,1)S(1)}, u32[]{:S(2)}, u32[]{:S(2)}) collective-permute-start(bf16[432,512]{1,0:T(8,128)(2,1)} %shard_map.86), channel_id=1, source_target_pairs={{0,2},{2,0},{4,6},{6,4},{8,10},{10,8},{12,14},{14,12},{16,18},{18,... | collective-permute-start | bytes 1327112 | tf_op jit(solution)/shard_map/ppermute | solution.py:280
  6.1 19.0 %collective-permute-start.1 = (bf16[432,512]{1,0:T(8,128)(2,1)}, bf16[432,512]{1,0:T(8,128)(2,1)S(1)}, u32[]{:S(2)}, u32[]{:S(2)}) collective-permute-start(bf16[432,512]{1,0:T(8,128)(2,1)} %shard_map.86), channel_id=1, source_target_pairs={{0,252},{2,254},{4,0},{6,2},{8,4},{10,6},{12,8},{14,10},{16,12},{1... | collective-permute-start | bytes 1327112 | tf_op jit(solution)/shard_map/ppermute | solution.py:276
  20.4 2.6 %collective-permute-start.3 = (bf16[400,512]{1,0:T(8,128)(2,1)S(1)}, bf16[400,512]{1,0:T(8,128)(2,1)S(1)}, u32[]{:S(2)}, u32[]{:S(2)}) collective-permute-start(bf16[400,512]{1,0:T(8,128)(2,1)S(1)} %collective-permute-done.2.prev2), channel_id=1, source_target_pairs={{0,2},{2,0},{4,6},{6,4},{8,10},{10,8},{12,14},{14,12},{16,18},{18,... | collective-permute-start | bytes 1228808 | tf_op jit(solution)/shard_map/ppermute | solution.py:280
  25.0 3.8 %collective-permute-start.5 = (f32[8,128]{1,0:T(8,128)S(1)}, f32[8,128]{1,0:T(8,128)S(1)}, u32[]{:S(2)}, u32[]{:S(2)}) collective-permute-start(f32[8,128]{1,0:T(8,128)S(1)} %get-tuple-element.28.row), channel_id=1, source_target_pairs={{0,2},{2,0},{4,6},{6,4},{8,10},{10,8},{12,14},{14,12},{16,18},{18,... | collective-permute-start | bytes 12296 | tf_op jit(solution)/shard_map/ppermute | solution.py:280
  25.1 3.6 %collective-permute-start.4 = (bf16[432,512]{1,0:T(8,128)(2,1)S(1)}, bf16[432,512]{1,0:T(8,128)(2,1)S(1)}, u32[]{:S(2)}, u32[]{:S(2)}) collective-permute-start(bf16[432,512]{1,0:T(8,128)(2,1)S(1)} %shard_map.90.next2), channel_id=1, source_target_pairs={{0,2},{2,0},{4,6},{6,4},{8,10},{10,8},{12,14},{14,12},{16,18},{18,... | collective-permute-start | bytes 1327112 | tf_op jit(solution)/shard_map/ppermute | solution.py:280
  32.0 21.6 %collective-permute-start.6 = (bf16[400,512]{1,0:T(8,128)(2,1)S(1)}, bf16[400,512]{1,0:T(8,128)(2,1)S(1)}, u32[]{:S(2)}, u32[]{:S(2)}) collective-permute-start(bf16[400,512]{1,0:T(8,128)(2,1)S(1)} %get-tuple-element.30.own), channel_id=1, source_target_pairs={{0,1},{1,0},{2,3},{3,2},{4,5},{5,4},{6,7},{7,6},{8,9},{9,8},{10,11... | collective-permute-start | bytes 1228808 | tf_op jit(solution)/shard_map/ppermute | solution.py:323

commit v2 on v1

--- a/solution.py
+++ b/solution.py
@@ -109,15 +109,15 @@
 HEADS, TAILS, RELS, NEGS, LIVE, EXTRA = 0, 1, 2, 3, 16, 32
 
 
-def unpacked(block, width, kind, step):
-    rows = block[width:width + EXTRA, :].astype(F32)
+def unpacked(lists, kind, step):
+    rows = lists[...].astype(F32)
     k = (kind * 2 + step - 1) * 2
     return (rows[k:k + 1, :] * 256.0 + rows[k + 1:k + 2, :]).astype(jnp.int32)
 
 
-def live_counts(block, width, step):
+def live_counts(lists, step):
     k = LIVE + step - 1
-    return block[width:width + EXTRA, :].astype(F32)[k:k + 1, :].astype(jnp.int32)
+    return lists[...].astype(F32)[k:k + 1, :].astype(jnp.int32)
 
 
 def split(x):
@@ -125,15 +125,13 @@
     return high, (x - high.astype(F32)).astype(BF16)
 
 
-def pack_kernel(emb_in, heads_in, tails_in, rels_in, negatives_in, live_in, block,
+def pack_kernel(heads_in, tails_in, rels_in, negatives_in, live_in, packed,
                 heads, tails, rels, negatives, live_groups, rows, sems):
-    width = emb_in.shape[0]
-    pairs = ((heads_in, heads), (tails_in, tails), (rels_in, rels), (negatives_in, negatives), (live_in, live_groups),
-             (emb_in, block.at[:width, :]))
+    pairs = ((heads_in, heads), (tails_in, tails), (rels_in, rels), (negatives_in, negatives), (live_in, live_groups))
     copies = [pltpu.make_async_copy(a, b, sems.at[k]) for k, (a, b) in enumerate(pairs)]
     for copy in copies:
         copy.start()
-    for copy in copies[:5]:
+    for copy in copies:
         copy.wait()
     edges = heads.shape[1]
     half = edges // 2
@@ -151,8 +149,7 @@
             rows[k + 1:k + 2, g * half:(g + 1) * half] = (row & 255).astype(F32)
         k = LIVE + step - 1
         rows[k:k + 1, :] = jnp.broadcast_to(live_groups[:, step:step + 1], (1, edges)).astype(F32)
-    block[width:width + EXTRA, :] = rows[...].astype(BF16)
-    copies[5].wait()
+    packed[...] = rows[...].astype(BF16)
 
 
 def prepare_kernel(emb, rel, heads, tails, rels, negatives, live_groups, grad, sums, q1, q2, r1, r2, log1, log2, hot, hf, rf, qf, sf, qq, log):
@@ -198,20 +195,19 @@
     return loss * live, live
 
 
-def far_terms(step, rel, block, r_out, log_out, hot):
-    width, entities = rel.shape[0], log_out.shape[0]
-    r_out[...] = gather_relations(rel, unpacked(block, width, RELS, step), hot)
-    log_counts(halves(unpacked(block, width, NEGS, step)), entities, log_out)
-
-
-def tail_bucket(step, emb, block, rf, log, acc, hf, qf, sf, qq):
-    (width, entities), edges = emb.shape, block.shape[1]
-    hf[...] = dot(block[:width, :], one_hot(unpacked(block, width, HEADS, step), entities), NN)
+def far_terms(step, rel, lists, r_out, log_out, hot):
+    r_out[...] = gather_relations(rel, unpacked(lists, RELS, step), hot)
+    log_counts(halves(unpacked(lists, NEGS, step)), log_out.shape[0], log_out)
+
+
+def tail_bucket(step, emb, head, lists, rf, log, acc, hf, qf, sf, qq):
+    entities, edges = emb.shape[1], lists.shape[1]
+    hf[...] = dot(head[...], one_hot(unpacked(lists, HEADS, step), entities), NN)
     make_query(hf, rf, qf)
     q = qf[...].astype(BF16)
     sf[...] = dot(emb[...], q, TN)
-    loss, miss = softmax_terms(sf, log, unpacked(block, width, TAILS, step), qq)
-    scale = miss * live_row(live_counts(block, width, step), edges) * (1.0 / 256.0)
+    loss, miss = softmax_terms(sf, log, unpacked(lists, TAILS, step), qq)
+    scale = miss * live_row(live_counts(lists, step), edges) * (1.0 / 256.0)
     high, low = split(q.astype(F32) * scale)
     acc[...] += dot(high, qq[...], NT) + dot(low, qq[...], NT)
 
@@ -226,7 +222,7 @@
 def heads1_kernel(sibling, swapped, q1, r1, log1, heads, tails, live_groups, part, sums, grad, row,
                   hf, rf, qf, sf, qq, prev1):
     grad[...] = part[...]
-    prev1[...] = jnp.where(lax.axis_index("blk") & 1 == 0, swapped[...], sibling[:prev1.shape[0], :])
+    prev1[...] = jnp.where(lax.axis_index("blk") & 1 == 0, swapped[...], sibling[...])
     loss, live = head_bucket(1, prev1, q1, r1, log1, heads, tails, live_groups, grad, hf, rf, qf, sf, qq)
     loss_all = jnp.sum(sums[0:1, :] + loss, axis=1, keepdims=True)
     live_all = jnp.sum(sums[1:2, :] + live, axis=1, keepdims=True)
@@ -238,17 +234,20 @@
     pass
 
 
-def tails2_kernel(rel, emb, next2, part, grad, hot, hf, rf, qf, sf, qq, log):
+def tails2_kernel(rel, emb, next2, lists, part, grad, hot, hf, rf, qf, sf, qq, log):
     grad[...] = part[...]
-    far_terms(2, rel, next2, rf, log, hot)
-    tail_bucket(2, emb, next2, rf, log, grad, hf, qf, sf, qq)
-
-
-def tails1_kernel(rel, emb, sibling, swapped, part, row, core_row, grad, rows, hot, hf, rf, qf, sf, qq, acc, next1, log):
-    next1[...] = jnp.where(lax.axis_index("blk") & 1 == 0, sibling[...], swapped[...])
+    far_terms(2, rel, lists, rf, log, hot)
+    tail_bucket(2, emb, next2, lists, rf, log, grad, hf, qf, sf, qq)
+
+
+def tails1_kernel(rel, emb, sibling, swapped, sibling_lists, swapped_lists, part, row, core_row, grad, rows,
+                  hot, hf, rf, qf, sf, qq, acc, next1, lists, log):
+    even = lax.axis_index("blk") & 1 == 0
+    next1[...] = jnp.where(even, sibling[...], swapped[...])
+    lists[...] = jnp.where(even, sibling_lists[...], swapped_lists[...])
     acc[...] = part[...]
-    far_terms(1, rel, next1, rf, log, hot)
-    tail_bucket(1, emb, next1, rf, log, acc, hf, qf, sf, qq)
+    far_terms(1, rel, lists, rf, log, hot)
+    tail_bucket(1, emb, next1, lists, rf, log, acc, hf, qf, sf, qq)
     grad[...] = acc[...].astype(BF16)
     rows[...] = jnp.broadcast_to(row[0:1, :] + core_row[0:1, :], rows.shape)
 
@@ -292,15 +291,17 @@
     work = [(big, F32), (big, F32), (big, F32), ((entities, edges), F32), ((entities, edges), BF16)]
     hot = ((n_rel, edges), BF16)
     raw = (heads, tails, rels, negatives, live.T)
-    sent = ((width + EXTRA, edges), BF16)
-    (block,) = kernel(
+    prev2 = shifted(emb, 2)
+    next2 = shifted(emb, -2)
+    sibling = exchanged(emb)
+    sent = ((EXTRA, edges), BF16)
+    (lists,) = kernel(
         pack_kernel, [sent],
-        [(x.shape, x.dtype) for x in raw] + [((EXTRA, edges), F32), pltpu.SemaphoreType.DMA((len(raw) + 1,))],
-        2 * 10**9, [pltpu.HBM] * (len(raw) + 1), 56,
-    )(emb, *raw)
-    prev2 = shifted(emb, 2)
-    next2 = shifted(block, -2)
-    sibling = exchanged(block)
+        [(x.shape, x.dtype) for x in raw] + [((EXTRA, edges), F32), pltpu.SemaphoreType.DMA((len(raw),))],
+        2 * 10**9, [pltpu.HBM] * len(raw), 56,
+    )(*raw)
+    next2_lists = shifted(lists, -2)
+    sibling_lists = exchanged(lists)
     part, sums, q1, q2, r1, r2, log1, log2 = kernel(
         prepare_kernel,
         [(grads, F32), ((8, edges), F32)] + [(big, BF16)] * 4 + [(logs, F32)] * 2,
@@ -312,14 +313,15 @@
     part, row = kernel(heads1_kernel, [(grads, F32), (rows_of, F32)], work + [(big, BF16)], 3 * 10**9, [here] * 10)(
         sibling, swapped_prev, q1, r1, log1, *own_lists, part, sums)
     core_row = exchanged(row)
-    (next2,) = kernel(after_kernel, [sent], [], 10**6, [here] * 2, aliases={0: 0})(next2, row)
+    (next2,) = kernel(after_kernel, [(big, BF16)], [], 10**6, [here] * 2, aliases={0: 0})(next2, row)
     swapped_next = exchanged(next2)
-    (part,) = kernel(tails2_kernel, [(grads, F32)], [hot] + work + [(logs, F32)], 10 * 10**9, [here] * 4)(
-        rel, emb, next2, part)
+    swapped_lists = exchanged(next2_lists)
+    (part,) = kernel(tails2_kernel, [(grads, F32)], [hot] + work + [(logs, F32)], 10 * 10**9, [here] * 5)(
+        rel, emb, next2, next2_lists, part)
     own, rows = kernel(
-        tails1_kernel, [(grads, BF16), ((blocks, 128), F32)], [hot] + work + [(grads, F32), sent, (logs, F32)],
-        3 * 10**9, [here] * 7,
-    )(rel, emb, sibling, swapped_next, part, row, core_row)
+        tails1_kernel, [(grads, BF16), ((blocks, 128), F32)],
+        [hot] + work + [(grads, F32), (big, BF16), sent, (logs, F32)], 3 * 10**9, [here] * 9,
+    )(rel, emb, sibling, swapped_next, sibling_lists, swapped_lists, part, row, core_row)
     other = lax.ppermute(own, "rep", [(0, 1), (1, 0)])
     rows = lax.all_to_all(rows, ("blk", "rep"), 0, 0, tiled=True,
                           axis_index_groups=[[4 * i + 2 * k + r for i in range(blocks // 2) for r in (0, 1)] for k in (0, 1)])

time: 54.8 us -> 57.3 us (1.046)
  starting transfers between devices: 14.5 us -> 16.7 us
  blocking collectives: 19.1 us -> 19.8 us
    ppermute x2 -> x3, starting transfers between devices: 9.43 us -> 11.1 us  [shifted(): return lax.ppermute(x, 'blk', [(i, (i + by) % peers) for i in range(peers)])]
    all_to_all x1, blocking collectives: 19.1 us -> 19.8 us  [per_device(): lax.all_to_all(rows, ('blk', 'rep'), 0, 0, tiled=True, axis_index_groups=...]
    ppermute x4 -> x6, starting transfers between devices: 2.51 us -> 2.97 us  [exchanged(): lax.ppermute(x, 'blk', [(i, i ^ 1) for i in range(lax.axis_size('blk'))])]
  transfers between devices with their start and end apart: 7 -> 10, of which waited for: 0 -> 0; matrix products, arithmetic and copies ran while one was open for 0% -> 0% of each run, Pallas kernels for 29% -> 27%
where the time goes in v2:
time: 57.3 us; the launch traced here: 57.2 us
  Pallas kernels  19.8 us (35%)
  blocking collectives  19.8 us (35%)
  starting transfers between devices  16.7 us (29%)
  between operations  0.8 us (1%)
    all_to_all x1, blocking collectives, per_device(): lax.all_to_all(rows, ('blk', 'rep'), 0, 0, tiled=True, axis_index_groups=...  19.8 us
    ppermute x3, starting transfers between devices, shifted(): return lax.ppermute(x, 'blk', [(i, (i + by) % peers) for i in range(peers)])  11.1 us
    pallas_call x1, Pallas kernels, per_device(): kernel(prepare_kernel, [(grads, F32), ((8, edges), F32)] + [(big, BF16)]...  7.02 us
    pallas_call x1, Pallas kernels, per_device(): kernel(tails1_kernel, [(grads, BF16), ((blocks, 128), F32)], [hot] + work...  3.19 us
    pallas_call x1, Pallas kernels, per_device(): kernel(tails2_kernel, [(grads, F32)], [hot] + work + [(logs, F32)], 10 *...  3.15 us
    ppermute x6, starting transfers between devices, exchanged(): lax.ppermute(x, 'blk', [(i, i ^ 1) for i in range(lax.axis_size('blk'))])  2.97 us
    ppermute x1, starting transfers between devices, per_device(): other = lax.ppermute(own, 'rep', [(0, 1), (1, 0)])  2.55 us
    pallas_call x1, Pallas kernels, per_device(): kernel(heads1_kernel, [(grads, F32), (rows_of, F32)], work + [(big, BF16)...  1.93 us
  transfers between devices with their start and end apart: 10, of which 0 were waited for; matrix products, arithmetic and copies ran while one was open for 0% of the time, Pallas kernels for 27%

profile of v2, /device:TPU:1, one launch (start us, length us, event | category | flops | bytes accessed | tf_op | source)
XLA Modules:
  0.0 57.2 jit_solution(15856293923714931103)
XLA Ops:
  0.6 2.2 %collective-permute-start.2 = (bf16[400,512]{1,0:T(8,128)(2,1)}, bf16[400,512]{1,0:T(8,128)(2,1)S(1)}, u32[]{:S(2)}, u32[]{:S(2)}) collective-permute-start(bf16[400,512]{1,0:T(8,128)(2,1)} %bitcast.14), channel_id=1, source_target_pairs={{0,4},{2,6},{4,8},{6,10},{8,12},{10,14},{12,16},{14,18},{16,20},{1... | collective-permute-start | bytes 1228808 | tf_op jit(solution)/shard_map/ppermute | solution.py:275
  2.8 1.2 %collective-permute-start = (bf16[400,512]{1,0:T(8,128)(2,1)}, bf16[400,512]{1,0:T(8,128)(2,1)S(1)}, u32[]{:S(2)}, u32[]{:S(2)}) collective-permute-start(bf16[400,512]{1,0:T(8,128)(2,1)} %bitcast.15), channel_id=1, source_target_pairs={{0,2},{2,0},{4,6},{6,4},{8,10},{10,8},{12,14},{14,12},{16,18},{18,... | collective-permute-start | bytes 1228808 | tf_op jit(solution)/shard_map/ppermute | solution.py:279
  4.0 7.2 %collective-permute-start.1 = (bf16[400,512]{1,0:T(8,128)(2,1)}, bf16[400,512]{1,0:T(8,128)(2,1)S(1)}, u32[]{:S(2)}, u32[]{:S(2)}) collective-permute-start(bf16[400,512]{1,0:T(8,128)(2,1)} %bitcast.16), channel_id=1, source_target_pairs={{0,252},{2,254},{4,0},{6,2},{8,4},{10,6},{12,8},{14,10},{16,12},{1... | collective-permute-start | bytes 1228808 | tf_op jit(solution)/shard_map/ppermute | solution.py:275
  11.3 0.0 copy-start
  11.3 0.0 copy-start.1
  11.3 0.0 copy-start.2
  11.3 0.0 copy-start.3
  11.3 0.0 copy-start.4
  11.3 0.0 copy-start.5
  11.3 0.0 copy-start.6
  11.3 1.6 %shard_map.90 = bf16[32,512]{1,0:T(8,128)(2,1)} custom-call(s32[3,512]{1,0:T(4,128)} %heads_in.1, s32[3,512]{1,0:T(4,128)} %tails_in.1, s32[3,512]{1,0:T(4,128)} %rels_in.1, s32[3,2,256]{2,1,0:T(2,128)} %negatives_in.1, s32[1,3]{1,0:T(1,128)} %bitcast.20), custom_call_target="tpu_custom_call" | custom-call | flops 2000000000 | bytes 4194304 | tf_op jit(solution)/shard_map/pallas_call | solution.py:298
  12.9 1.7 %collective-permute-start.6 = (bf16[32,512]{1,0:T(8,128)(2,1)}, bf16[32,512]{1,0:T(8,128)(2,1)S(1)}, u32[]{:S(2)}, u32[]{:S(2)}) collective-permute-start(bf16[32,512]{1,0:T(8,128)(2,1)} %shard_map.90), channel_id=1, source_target_pairs={{0,252},{2,254},{4,0},{6,2},{8,4},{10,6},{12,8},{14,10},{16,12},{1... | collective-permute-start | bytes 98312 | tf_op jit(solution)/shard_map/ppermute | solution.py:275
  14.6 0.6 collective-permute-start.5
  15.2 0.0 copy-done
  15.2 0.0 copy-done.1
  15.2 0.0 copy-done.2
  15.2 0.0 copy-done.3
  15.2 0.0 copy-done.4
  15.2 0.0 copy-done.5
  15.2 0.0 copy-done.6
  15.3 7.0 %shard_map.86 = (f32[400,512]{1,0:T(8,128)S(1)}, f32[8,512]{1,0:T(8,128)S(1)}, bf16[400,512]{1,0:T(8,128)(2,1)S(1)}, bf16[400,512]{1,0:T(8,128)(2,1)S(1)}, bf16[...) custom-call(bf16[400,512]{1,0:T(8,128)(2,1)S(1)} %bitcast.17, ...), custom_call_target="tpu_custom_call" | custom-call | flops 20000000000 | bytes 4194304 | tf_op jit(solution)/shard_map/pallas_call | solution.py:305
  22.3 0.0 collective-permute-done.6.lists
  22.3 0.1 collective-permute-start.7
  22.4 0.0 collective-permute-done.2.prev2
  22.4 0.5 collective-permute-start.3
  22.9 1.9 %shard_map.87 = (f32[400,512]{1,0:T(8,128)S(1)}, f32[8,512]{1,0:T(8,128)S(1)}) custom-call(bf16[400,512]{1,0:T(8,128)(2,1)S(1)} %collective-permute-done.2.prev2, bf16[400,512]{1,0:T(8,128)(2,1)S(1)} %get-tuple-element.21.q2, bf16[400,512]{1,0:T(8,128)(2,1)S(1)} %get-tuple-element.22.r2, f32[512,256]{1,0:T(8,128)S(1)} %get-tuple-element.23.log2, ...), custom_call_target="tpu_custom_call" | custom-call | flops 8000000000 | bytes 4194304 | tf_op jit(solution)/shard_map/pallas_call | solution.py:311
  24.8 0.0 collective-permute-done.sibling
  24.8 0.0 collective-permute-done.3.swapped
  24.8 1.9 %shard_map.88 = (f32[400,512]{1,0:T(8,128)S(1)}, f32[8,128]{1,0:T(8,128)S(1)}) custom-call(bf16[400,512]{1,0:T(8,128)(2,1)S(1)} %collective-permute-done.sibling, bf16[400,512]{1,0:T(8,128)(2,1)S(1)} %collective-permute-done.3.swapped, bf16[400,512]{1,0:T(8,128)(2,1)S(1)} %get-tuple-element.18.q1, bf16[400,512]{1,0:T(8,128)(2,1)S(1)} %get-tuple-element.19.r1, ...), custom_call_target="tpu_custom_call" | custom-call | flops 3000000000 | bytes 4194304 | tf_op jit(solution)/shard_map/pallas_call | solution.py:313
  26.8 0.4 collective-permute-start.8
  27.2 0.0 collective-permute-done.1.block
  27.2 0.2 collective-permute-start.4
  27.4 3.1 %shard_map.91.part = f32[400,512]{1,0:T(8,128)S(1)} custom-call(bf16[400,2560]{1,0:T(8,128)(2,1)S(1)} %bitcast.12, bf16[400,512]{1,0:T(8,128)(2,1)S(1)} %bitcast.18, bf16[400,512]{1,0:T(8,128)(2,1)S(1)} %shard_map.89.next2, bf16[32,512]{1,0:T(8,128)(2,1)S(1)} %collective-permute-done.6.lists, f32[400,512]{1,0:T(8,128)S(1)} %get-tuple-element.29.part), custom_call_target="tpu_custom_call" | custom-call | flops 10000000000 | bytes 4194304 | tf_op jit(solution)/shard_map/pallas_call | solution.py:319
  30.5 0.0 collective-permute-done.5.sibling_lists
  30.5 0.0 collective-permute-done.7.swapped_lists
  30.6 0.0 collective-permute-done.8.core_row
  30.6 0.0 collective-permute-done.4.swapped
  30.6 3.2 %shard_map.92 = (bf16[400,512]{1,0:T(8,128)(2,1)S(1)}, f32[128,128]{1,0:T(8,128)S(1)}) custom-call(bf16[400,2560]{1,0:T(8,128)(2,1)S(1)} %bitcast.13, bf16[400,512]{1,0:T(8,128)(2,1)S(1)} %bitcast.19, bf16[400,512]{1,0:T(8,128)(2,1)S(1)} %collective-permute-done.sibling, bf16[400,512]{1,0:T(8,128)(2,1)S(1)} %collective-permute-done.4.swapped, ...), custom_call_target="tpu_custom_call" | custom-call | flops 3000000000 | bytes 4194304 | tf_op jit(solution)/shard_map/pallas_call | solution.py:321
  33.8 2.5 %collective-permute-start.9 = (bf16[400,512]{1,0:T(8,128)(2,1)S(1)}, bf16[400,512]{1,0:T(8,128)(2,1)S(1)}, u32[]{:S(2)}, u32[]{:S(2)}) collective-permute-start(bf16[400,512]{1,0:T(8,128)(2,1)S(1)} %get-tuple-element.30.own), channel_id=1, source_target_pairs={{0,1},{1,0},{2,3},{3,2},{4,5},{5,4},{6,7},{7,6},{8,9},{9,8},{10,11... | collective-permute-start | bytes 1228808 | tf_op jit(solution)/shard_map/ppermute | solution.py:325
  36.3 19.8 %all_to_all.11 = f32[128,1,128]{2,1,0:T(1,128)S(1)} all-to-all(f32[128,1,128]{2,1,0:T(1,128)S(1)} %bitcast.10), channel_id=1, replica_groups={{0,1,4,5,8,9,12,13,16,17,20,21,24,25,28,29,32,33,36,37,40,41,44,45,48,4..., dimensions={0} | all-to-all | bytes 131072 | tf_op jit(solution)/shard_map/all_to_all | solution.py:326
  56.1 0.0 collective-permute-done.9.other
  56.1 1.0 %shard_map.93 = (f32[400,512]{1,0:T(8,128)}, f32[1,1]{1,0:T(1,128)}) custom-call(bf16[400,512]{1,0:T(8,128)(2,1)S(1)} %get-tuple-element.30.own, bf16[400,512]{1,0:T(8,128)(2,1)S(1)} %collective-permute-done.9.other, f32[128,128]{1,0:T(8,128)S(1)} %bitcast.9), custom_call_target="tpu_custom_call" | custom-call | flops 1000000 | bytes 4194304 | tf_op jit(solution)/shard_map/pallas_call | solution.py:328
  (1 shorter events, 0.0 us)
Async XLA Ops:
  0.6 21.8 %collective-permute-start.2 = (bf16[400,512]{1,0:T(8,128)(2,1)}, bf16[400,512]{1,0:T(8,128)(2,1)S(1)}, u32[]{:S(2)}, u32[]{:S(2)}) collective-permute-start(bf16[400,512]{1,0:T(8,128)(2,1)} %bitcast.14), channel_id=1, source_target_pairs={{0,4},{2,6},{4,8},{6,10},{8,12},{10,14},{12,16},{14,18},{16,20},{1... | collective-permute-start | bytes 1228808 | tf_op jit(solution)/shard_map/ppermute | solution.py:275
  2.8 22.0 %collective-permute-start = (bf16[400,512]{1,0:T(8,128)(2,1)}, bf16[400,512]{1,0:T(8,128)(2,1)S(1)}, u32[]{:S(2)}, u32[]{:S(2)}) collective-permute-start(bf16[400,512]{1,0:T(8,128)(2,1)} %bitcast.15), channel_id=1, source_target_pairs={{0,2},{2,0},{4,6},{6,4},{8,10},{10,8},{12,14},{14,12},{16,18},{18,... | collective-permute-start | bytes 1228808 | tf_op jit(solution)/shard_map/ppermute | solution.py:279
  4.0 23.1 %collective-permute-start.1 = (bf16[400,512]{1,0:T(8,128)(2,1)}, bf16[400,512]{1,0:T(8,128)(2,1)S(1)}, u32[]{:S(2)}, u32[]{:S(2)}) collective-permute-start(bf16[400,512]{1,0:T(8,128)(2,1)} %bitcast.16), channel_id=1, source_target_pairs={{0,252},{2,254},{4,0},{6,2},{8,4},{10,6},{12,8},{14,10},{16,12},{1... | collective-permute-start | bytes 1228808 | tf_op jit(solution)/shard_map/ppermute | solution.py:275
  11.3 3.9 %copy-start = (bf16[2560,400]{0,1:T(8,128)(2,1)S(1)}, bf16[2560,400]{0,1:T(8,128)(2,1)}, u32[]{:S(2)}) copy-start(bf16[2560,400]{0,1:T(8,128)(2,1)} %param.8) | copy-start | bytes 6144004
  11.3 3.9 %copy-start.1 = (bf16[512,400]{0,1:T(8,128)(2,1)S(1)}, bf16[512,400]{0,1:T(8,128)(2,1)}, u32[]{:S(2)}) copy-start(bf16[512,400]{0,1:T(8,128)(2,1)} %param.7) | copy-start | bytes 1228804
  11.3 3.9 %copy-start.2 = (s32[3,512]{1,0:T(4,128)S(1)}, s32[3,512]{1,0:T(4,128)}, u32[]{:S(2)}) copy-start(s32[3,512]{1,0:T(4,128)} %rels_in.1) | copy-start | bytes 18436
  11.3 3.9 %copy-start.3 = (s32[3,512]{1,0:T(4,128)S(1)}, s32[3,512]{1,0:T(4,128)}, u32[]{:S(2)}) copy-start(s32[3,512]{1,0:T(4,128)} %heads_in.1) | copy-start | bytes 18436
  11.3 3.9 %copy-start.4 = (s32[3,512]{1,0:T(4,128)S(1)}, s32[3,512]{1,0:T(4,128)}, u32[]{:S(2)}) copy-start(s32[3,512]{1,0:T(4,128)} %tails_in.1) | copy-start | bytes 18436
  11.3 3.9 %copy-start.5 = (s32[3,2,256]{2,1,0:T(2,128)S(1)}, s32[3,2,256]{2,1,0:T(2,128)}, u32[]{:S(2)}) copy-start(s32[3,2,256]{2,1,0:T(2,128)} %negatives_in.1) | copy-start | bytes 18436
  11.3 3.9 %copy-start.6 = (s32[3,1]{0,1:T(1,128)S(1)}, s32[3,1]{0,1:T(1,128)}, u32[]{:S(2)}) copy-start(s32[3,1]{0,1:T(1,128)} %param.13) | copy-start | bytes 40
  12.9 9.3 %collective-permute-start.6 = (bf16[32,512]{1,0:T(8,128)(2,1)}, bf16[32,512]{1,0:T(8,128)(2,1)S(1)}, u32[]{:S(2)}, u32[]{:S(2)}) collective-permute-start(bf16[32,512]{1,0:T(8,128)(2,1)} %shard_map.90), channel_id=1, source_target_pairs={{0,252},{2,254},{4,0},{6,2},{8,4},{10,6},{12,8},{14,10},{16,12},{1... | collective-permute-start | bytes 98312 | tf_op jit(solution)/shard_map/ppermute | solution.py:275
  14.6 15.9 %collective-permute-start.5 = (bf16[32,512]{1,0:T(8,128)(2,1)}, bf16[32,512]{1,0:T(8,128)(2,1)S(1)}, u32[]{:S(2)}, u32[]{:S(2)}) collective-permute-start(bf16[32,512]{1,0:T(8,128)(2,1)} %shard_map.90), channel_id=1, source_target_pairs={{0,2},{2,0},{4,6},{6,4},{8,10},{10,8},{12,14},{14,12},{16,18},{18,... | collective-permute-start | bytes 98312 | tf_op jit(solution)/shard_map/ppermute | solution.py:279
  22.3 8.3 %collective-permute-start.7 = (bf16[32,512]{1,0:T(8,128)(2,1)S(1)}, bf16[32,512]{1,0:T(8,128)(2,1)S(1)}, u32[]{:S(2)}, u32[]{:S(2)}) collective-permute-start(bf16[32,512]{1,0:T(8,128)(2,1)S(1)} %collective-permute-done.6.lists), channel_id=1, source_target_pairs={{0,2},{2,0},{4,6},{6,4},{8,10},{10,8},{12,14},{14,12},{16,18},{18,... | collective-permute-start | bytes 98312 | tf_op jit(solution)/shard_map/ppermute | solution.py:279
  22.4 2.4 %collective-permute-start.3 = (bf16[400,512]{1,0:T(8,128)(2,1)S(1)}, bf16[400,512]{1,0:T(8,128)(2,1)S(1)}, u32[]{:S(2)}, u32[]{:S(2)}) collective-permute-start(bf16[400,512]{1,0:T(8,128)(2,1)S(1)} %collective-permute-done.2.prev2), channel_id=1, source_target_pairs={{0,2},{2,0},{4,6},{6,4},{8,10},{10,8},{12,14},{14,12},{16,18},{18,... | collective-permute-start | bytes 1228808 | tf_op jit(solution)/shard_map/ppermute | solution.py:279
  26.8 3.8 %collective-permute-start.8 = (f32[8,128]{1,0:T(8,128)S(1)}, f32[8,128]{1,0:T(8,128)S(1)}, u32[]{:S(2)}, u32[]{:S(2)}) collective-permute-start(f32[8,128]{1,0:T(8,128)S(1)} %get-tuple-element.28.row), channel_id=1, source_target_pairs={{0,2},{2,0},{4,6},{6,4},{8,10},{10,8},{12,14},{14,12},{16,18},{18,... | collective-permute-start | bytes 12296 | tf_op jit(solution)/shard_map/ppermute | solution.py:279
  27.2 3.4 %collective-permute-start.4 = (bf16[400,512]{1,0:T(8,128)(2,1)S(1)}, bf16[400,512]{1,0:T(8,128)(2,1)S(1)}, u32[]{:S(2)}, u32[]{:S(2)}) collective-permute-start(bf16[400,512]{1,0:T(8,128)(2,1)S(1)} %shard_map.89.next2), channel_id=1, source_target_pairs={{0,2},{2,0},{4,6},{6,4},{8,10},{10,8},{12,14},{14,12},{16,18},{18,... | collective-permute-start | bytes 1228808 | tf_op jit(solution)/shard_map/ppermute | solution.py:279
  33.8 22.4 %collective-permute-start.9 = (bf16[400,512]{1,0:T(8,128)(2,1)S(1)}, bf16[400,512]{1,0:T(8,128)(2,1)S(1)}, u32[]{:S(2)}, u32[]{:S(2)}) collective-permute-start(bf16[400,512]{1,0:T(8,128)(2,1)S(1)} %get-tuple-element.30.own), channel_id=1, source_target_pairs={{0,1},{1,0},{2,3},{3,2},{4,5},{5,4},{6,7},{7,6},{8,9},{9,8},{10,11... | collective-permute-start | bytes 1228808 | tf_op jit(solution)/shard_map/ppermute | solution.py:325

commit v3 on v2

--- a/solution.py
+++ b/solution.py
@@ -230,7 +230,7 @@
     row[...] = jnp.where(lane == 0, loss_all, jnp.where(lane == 1, live_all, 0.0))
 
 
-def after_kernel(block, row, block_out):
+def after_kernel(block, lists, row, block_out, lists_out):
     pass
 
 
@@ -313,7 +313,8 @@
     part, row = kernel(heads1_kernel, [(grads, F32), (rows_of, F32)], work + [(big, BF16)], 3 * 10**9, [here] * 10)(
         sibling, swapped_prev, q1, r1, log1, *own_lists, part, sums)
     core_row = exchanged(row)
-    (next2,) = kernel(after_kernel, [(big, BF16)], [], 10**6, [here] * 2, aliases={0: 0})(next2, row)
+    next2, next2_lists = kernel(after_kernel, [(big, BF16), sent], [], 10**6, [here] * 3, aliases={0: 0, 1: 1})(
+        next2, next2_lists, row)
     swapped_next = exchanged(next2)
     swapped_lists = exchanged(next2_lists)
     (part,) = kernel(tails2_kernel, [(grads, F32)], [hot] + work + [(logs, F32)], 10 * 10**9, [here] * 5)(

time: 57.3 us -> 54.8 us (0.956)
  blocking collectives: 19.8 us -> 17.1 us
    all_to_all x1, blocking collectives: 19.8 us -> 17.1 us  [per_device(): lax.all_to_all(rows, ('blk', 'rep'), 0, 0, tiled=True, axis_index_groups=...]
  transfers between devices with their start and end apart: 10 -> 10, of which waited for: 0 -> 0; matrix products, arithmetic and copies ran while one was open for 0% -> 0% of each run, Pallas kernels for 27% -> 29%
where the time goes in v3:
time: 54.8 us; the launch traced here: 54.7 us
  Pallas kernels  19.8 us (36%)
  blocking collectives  17.1 us (31%)
  starting transfers between devices  16.8 us (31%)
  between operations  0.8 us (1%)
    all_to_all x1, blocking collectives, per_device(): lax.all_to_all(rows, ('blk', 'rep'), 0, 0, tiled=True, axis_index_groups=...  17.1 us
    ppermute x3, starting transfers between devices, shifted(): return lax.ppermute(x, 'blk', [(i, (i + by) % peers) for i in range(peers)])  11.1 us
    pallas_call x1, Pallas kernels, per_device(): kernel(prepare_kernel, [(grads, F32), ((8, edges), F32)] + [(big, BF16)]...  7.03 us
    pallas_call x1, Pallas kernels, per_device(): kernel(tails1_kernel, [(grads, BF16), ((blocks, 128), F32)], [hot] + work...  3.19 us
    pallas_call x1, Pallas kernels, per_device(): kernel(tails2_kernel, [(grads, F32)], [hot] + work + [(logs, F32)], 10 *...  3.15 us
    ppermute x6, starting transfers between devices, exchanged(): lax.ppermute(x, 'blk', [(i, i ^ 1) for i in range(lax.axis_size('blk'))])  3.15 us
    ppermute x1, starting transfers between devices, per_device(): other = lax.ppermute(own, 'rep', [(0, 1), (1, 0)])  2.54 us
    pallas_call x1, Pallas kernels, per_device(): kernel(heads1_kernel, [(grads, F32), (rows_of, F32)], work + [(big, BF16)...  1.94 us
  transfers between devices with their start and end apart: 10, of which 0 were waited for; matrix products, arithmetic and copies ran while one was open for 0% of the time, Pallas kernels for 29%

profile of v3, /device:TPU:1, one launch (start us, length us, event | category | flops | bytes accessed | tf_op | source)
XLA Modules:
  0.0 54.7 jit_solution(14589817561601552113)
XLA Ops:
  0.6 2.2 %collective-permute-start.3 = (bf16[400,512]{1,0:T(8,128)(2,1)}, bf16[400,512]{1,0:T(8,128)(2,1)S(1)}, u32[]{:S(2)}, u32[]{:S(2)}) collective-permute-start(bf16[400,512]{1,0:T(8,128)(2,1)} %bitcast.14), channel_id=1, source_target_pairs={{0,4},{2,6},{4,8},{6,10},{8,12},{10,14},{12,16},{14,18},{16,20},{1... | collective-permute-start | bytes 1228808 | tf_op jit(solution)/shard_map/ppermute | solution.py:275
  2.8 1.2 %collective-permute-start = (bf16[400,512]{1,0:T(8,128)(2,1)}, bf16[400,512]{1,0:T(8,128)(2,1)S(1)}, u32[]{:S(2)}, u32[]{:S(2)}) collective-permute-start(bf16[400,512]{1,0:T(8,128)(2,1)} %bitcast.15), channel_id=1, source_target_pairs={{0,2},{2,0},{4,6},{6,4},{8,10},{10,8},{12,14},{14,12},{16,18},{18,... | collective-permute-start | bytes 1228808 | tf_op jit(solution)/shard_map/ppermute | solution.py:279
  4.0 7.2 %collective-permute-start.1 = (bf16[400,512]{1,0:T(8,128)(2,1)}, bf16[400,512]{1,0:T(8,128)(2,1)S(1)}, u32[]{:S(2)}, u32[]{:S(2)}) collective-permute-start(bf16[400,512]{1,0:T(8,128)(2,1)} %bitcast.16), channel_id=1, source_target_pairs={{0,252},{2,254},{4,0},{6,2},{8,4},{10,6},{12,8},{14,10},{16,12},{1... | collective-permute-start | bytes 1228808 | tf_op jit(solution)/shard_map/ppermute | solution.py:275
  11.3 0.0 copy-start
  11.3 0.0 copy-start.1
  11.3 0.0 copy-start.2
  11.3 0.0 copy-start.3
  11.3 0.0 copy-start.4
  11.3 0.0 copy-start.5
  11.3 0.0 copy-start.6
  11.3 1.6 %shard_map.86 = bf16[32,512]{1,0:T(8,128)(2,1)} custom-call(s32[3,512]{1,0:T(4,128)} %heads.5, s32[3,512]{1,0:T(4,128)} %tails.5, s32[3,512]{1,0:T(4,128)} %rels.1, s32[3,2,256]{2,1,0:T(2,128)} %negatives.1, s32[1,3]{1,0:T(1,128)} %bitcast.20), custom_call_target="tpu_custom_call" | custom-call | flops 2000000000 | bytes 4194304 | tf_op jit(solution)/shard_map/pallas_call | solution.py:298
  12.9 1.7 %collective-permute-start.2 = (bf16[32,512]{1,0:T(8,128)(2,1)}, bf16[32,512]{1,0:T(8,128)(2,1)S(1)}, u32[]{:S(2)}, u32[]{:S(2)}) collective-permute-start(bf16[32,512]{1,0:T(8,128)(2,1)} %shard_map.86), channel_id=1, source_target_pairs={{0,252},{2,254},{4,0},{6,2},{8,4},{10,6},{12,8},{14,10},{16,12},{1... | collective-permute-start | bytes 98312 | tf_op jit(solution)/shard_map/ppermute | solution.py:275
  14.6 0.6 %collective-permute-start.6 = (bf16[32,512]{1,0:T(8,128)(2,1)}, bf16[32,512]{1,0:T(8,128)(2,1)S(1)}, u32[]{:S(2)}, u32[]{:S(2)}) collective-permute-start(bf16[32,512]{1,0:T(8,128)(2,1)} %shard_map.86), channel_id=1, source_target_pairs={{0,2},{2,0},{4,6},{6,4},{8,10},{10,8},{12,14},{14,12},{16,18},{18,... | collective-permute-start | bytes 98312 | tf_op jit(solution)/shard_map/ppermute | solution.py:279
  15.2 0.0 copy-done
  15.2 0.0 copy-done.1
  15.2 0.0 copy-done.2
  15.2 0.0 copy-done.3
  15.2 0.0 copy-done.4
  15.2 0.0 copy-done.5
  15.2 0.0 copy-done.6
  15.3 7.0 %shard_map.87 = (f32[400,512]{1,0:T(8,128)S(1)}, f32[8,512]{1,0:T(8,128)S(1)}, bf16[400,512]{1,0:T(8,128)(2,1)S(1)}, bf16[400,512]{1,0:T(8,128)(2,1)S(1)}, bf16[...) custom-call(bf16[400,512]{1,0:T(8,128)(2,1)S(1)} %bitcast.17, ...), custom_call_target="tpu_custom_call" | custom-call | flops 20000000000 | bytes 4194304 | tf_op jit(solution)/shard_map/pallas_call | solution.py:305
  22.3 0.0 collective-permute-done.3.prev2
  22.3 0.3 collective-permute-start.4
  22.6 1.9 %shard_map.88 = (f32[400,512]{1,0:T(8,128)S(1)}, f32[8,512]{1,0:T(8,128)S(1)}) custom-call(bf16[400,512]{1,0:T(8,128)(2,1)S(1)} %collective-permute-done.3.prev2, bf16[400,512]{1,0:T(8,128)(2,1)S(1)} %get-tuple-element.23.q2, bf16[400,512]{1,0:T(8,128)(2,1)S(1)} %get-tuple-element.24.r2, f32[512,256]{1,0:T(8,128)S(1)} %get-tuple-element.25.log2, ...), custom_call_target="tpu_custom_call" | custom-call | flops 8000000000 | bytes 4194304 | tf_op jit(solution)/shard_map/pallas_call | solution.py:311
  24.5 0.0 collective-permute-done.sibling
  24.5 0.0 collective-permute-done.4.swapped
  24.5 1.9 %shard_map.89 = (f32[400,512]{1,0:T(8,128)S(1)}, f32[8,128]{1,0:T(8,128)S(1)}) custom-call(bf16[400,512]{1,0:T(8,128)(2,1)S(1)} %collective-permute-done.sibling, bf16[400,512]{1,0:T(8,128)(2,1)S(1)} %collective-permute-done.4.swapped, bf16[400,512]{1,0:T(8,128)(2,1)S(1)} %get-tuple-element.20.q1, bf16[400,512]{1,0:T(8,128)(2,1)S(1)} %get-tuple-element.21.r1, ...), custom_call_target="tpu_custom_call" | custom-call | flops 3000000000 | bytes 4194304 | tf_op jit(solution)/shard_map/pallas_call | solution.py:313
  26.5 0.6 %collective-permute-start.8 = (f32[8,128]{1,0:T(8,128)S(1)}, f32[8,128]{1,0:T(8,128)S(1)}, u32[]{:S(2)}, u32[]{:S(2)}) collective-permute-start(f32[8,128]{1,0:T(8,128)S(1)} %get-tuple-element.30.row), channel_id=1, source_target_pairs={{0,2},{2,0},{4,6},{6,4},{8,10},{10,8},{12,14},{14,12},{16,18},{18,... | collective-permute-start | bytes 12296 | tf_op jit(solution)/shard_map/ppermute | solution.py:279
  27.0 0.0 collective-permute-done.2.lists
  27.1 0.0 collective-permute-done.1.block
  27.1 0.1 collective-permute-start.5
  27.2 0.4 collective-permute-start.7
  27.6 3.2 %shard_map.91.part = f32[400,512]{1,0:T(8,128)S(1)} custom-call(bf16[400,2560]{1,0:T(8,128)(2,1)S(1)} %bitcast.12, bf16[400,512]{1,0:T(8,128)(2,1)S(1)} %bitcast.18, bf16[400,512]{1,0:T(8,128)(2,1)S(1)} %get-tuple-element.31.next2, bf16[32,512]{1,0:T(8,128)(2,1)S(1)} %get-tuple-element.32.lists, f32[400,512]{1,0:T(8,128)S(1)} %get-tuple-element.33.part), custom_call_target="tpu_custom_call" | custom-call | flops 10000000000 | bytes 4194304 | tf_op jit(solution)/shard_map/pallas_call | solution.py:320
  30.7 0.0 collective-permute-done.6.sibling_lists
  30.7 0.0 collective-permute-done.8.core_row
  30.8 0.0 collective-permute-done.7.swapped_lists
  30.8 0.0 collective-permute-done.5.swapped
  30.8 3.2 %shard_map.92 = (bf16[400,512]{1,0:T(8,128)(2,1)S(1)}, f32[128,128]{1,0:T(8,128)S(1)}) custom-call(bf16[400,2560]{1,0:T(8,128)(2,1)S(1)} %bitcast.13, bf16[400,512]{1,0:T(8,128)(2,1)S(1)} %bitcast.19, bf16[400,512]{1,0:T(8,128)(2,1)S(1)} %collective-permute-done.sibling, bf16[400,512]{1,0:T(8,128)(2,1)S(1)} %collective-permute-done.5.swapped, ...), custom_call_target="tpu_custom_call" | custom-call | flops 3000000000 | bytes 4194304 | tf_op jit(solution)/shard_map/pallas_call | solution.py:322
  34.0 2.5 %collective-permute-start.9 = (bf16[400,512]{1,0:T(8,128)(2,1)S(1)}, bf16[400,512]{1,0:T(8,128)(2,1)S(1)}, u32[]{:S(2)}, u32[]{:S(2)}) collective-permute-start(bf16[400,512]{1,0:T(8,128)(2,1)S(1)} %get-tuple-element.34.own), channel_id=1, source_target_pairs={{0,1},{1,0},{2,3},{3,2},{4,5},{5,4},{6,7},{7,6},{8,9},{9,8},{10,11... | collective-permute-start | bytes 1228808 | tf_op jit(solution)/shard_map/ppermute | solution.py:326
  36.5 17.1 %all_to_all.11 = f32[128,1,128]{2,1,0:T(1,128)S(1)} all-to-all(f32[128,1,128]{2,1,0:T(1,128)S(1)} %bitcast.10), channel_id=1, replica_groups={{0,1,4,5,8,9,12,13,16,17,20,21,24,25,28,29,32,33,36,37,40,41,44,45,48,4..., dimensions={0} | all-to-all | bytes 131072 | tf_op jit(solution)/shard_map/all_to_all | solution.py:327
  53.6 0.0 collective-permute-done.9.other
  53.6 1.0 %shard_map.93 = (f32[400,512]{1,0:T(8,128)}, f32[1,1]{1,0:T(1,128)}) custom-call(bf16[400,512]{1,0:T(8,128)(2,1)S(1)} %get-tuple-element.34.own, bf16[400,512]{1,0:T(8,128)(2,1)S(1)} %collective-permute-done.9.other, f32[128,128]{1,0:T(8,128)S(1)} %bitcast.9), custom_call_target="tpu_custom_call" | custom-call | flops 1000000 | bytes 4194304 | tf_op jit(solution)/shard_map/pallas_call | solution.py:329
  (1 shorter events, 0.0 us)
Async XLA Ops:
  0.6 21.7 %collective-permute-start.3 = (bf16[400,512]{1,0:T(8,128)(2,1)}, bf16[400,512]{1,0:T(8,128)(2,1)S(1)}, u32[]{:S(2)}, u32[]{:S(2)}) collective-permute-start(bf16[400,512]{1,0:T(8,128)(2,1)} %bitcast.14), channel_id=1, source_target_pairs={{0,4},{2,6},{4,8},{6,10},{8,12},{10,14},{12,16},{14,18},{16,20},{1... | collective-permute-start | bytes 1228808 | tf_op jit(solution)/shard_map/ppermute | solution.py:275
  2.8 21.7 %collective-permute-start = (bf16[400,512]{1,0:T(8,128)(2,1)}, bf16[400,512]{1,0:T(8,128)(2,1)S(1)}, u32[]{:S(2)}, u32[]{:S(2)}) collective-permute-start(bf16[400,512]{1,0:T(8,128)(2,1)} %bitcast.15), channel_id=1, source_target_pairs={{0,2},{2,0},{4,6},{6,4},{8,10},{10,8},{12,14},{14,12},{16,18},{18,... | collective-permute-start | bytes 1228808 | tf_op jit(solution)/shard_map/ppermute | solution.py:279
  4.0 23.0 %collective-permute-start.1 = (bf16[400,512]{1,0:T(8,128)(2,1)}, bf16[400,512]{1,0:T(8,128)(2,1)S(1)}, u32[]{:S(2)}, u32[]{:S(2)}) collective-permute-start(bf16[400,512]{1,0:T(8,128)(2,1)} %bitcast.16), channel_id=1, source_target_pairs={{0,252},{2,254},{4,0},{6,2},{8,4},{10,6},{12,8},{14,10},{16,12},{1... | collective-permute-start | bytes 1228808 | tf_op jit(solution)/shard_map/ppermute | solution.py:275
  11.3 3.9 %copy-start = (bf16[2560,400]{0,1:T(8,128)(2,1)S(1)}, bf16[2560,400]{0,1:T(8,128)(2,1)}, u32[]{:S(2)}) copy-start(bf16[2560,400]{0,1:T(8,128)(2,1)} %param.8) | copy-start | bytes 6144004
  11.3 3.9 %copy-start.1 = (bf16[512,400]{0,1:T(8,128)(2,1)S(1)}, bf16[512,400]{0,1:T(8,128)(2,1)}, u32[]{:S(2)}) copy-start(bf16[512,400]{0,1:T(8,128)(2,1)} %param.7) | copy-start | bytes 1228804
  11.3 3.9 %copy-start.2 = (s32[3,512]{1,0:T(4,128)S(1)}, s32[3,512]{1,0:T(4,128)}, u32[]{:S(2)}) copy-start(s32[3,512]{1,0:T(4,128)} %rels.1) | copy-start | bytes 18436
  11.3 3.9 %copy-start.3 = (s32[3,512]{1,0:T(4,128)S(1)}, s32[3,512]{1,0:T(4,128)}, u32[]{:S(2)}) copy-start(s32[3,512]{1,0:T(4,128)} %heads.5) | copy-start | bytes 18436
  11.3 3.9 %copy-start.4 = (s32[3,512]{1,0:T(4,128)S(1)}, s32[3,512]{1,0:T(4,128)}, u32[]{:S(2)}) copy-start(s32[3,512]{1,0:T(4,128)} %tails.5) | copy-start | bytes 18436
  11.3 3.9 %copy-start.5 = (s32[3,2,256]{2,1,0:T(2,128)S(1)}, s32[3,2,256]{2,1,0:T(2,128)}, u32[]{:S(2)}) copy-start(s32[3,2,256]{2,1,0:T(2,128)} %negatives.1) | copy-start | bytes 18436
  11.3 3.9 %copy-start.6 = (s32[3,1]{0,1:T(1,128)S(1)}, s32[3,1]{0,1:T(1,128)}, u32[]{:S(2)}) copy-start(s32[3,1]{0,1:T(1,128)} %param.13) | copy-start | bytes 40
  12.9 14.1 %collective-permute-start.2 = (bf16[32,512]{1,0:T(8,128)(2,1)}, bf16[32,512]{1,0:T(8,128)(2,1)S(1)}, u32[]{:S(2)}, u32[]{:S(2)}) collective-permute-start(bf16[32,512]{1,0:T(8,128)(2,1)} %shard_map.86), channel_id=1, source_target_pairs={{0,252},{2,254},{4,0},{6,2},{8,4},{10,6},{12,8},{14,10},{16,12},{1... | collective-permute-start | bytes 98312 | tf_op jit(solution)/shard_map/ppermute | solution.py:275
  14.6 16.1 %collective-permute-start.6 = (bf16[32,512]{1,0:T(8,128)(2,1)}, bf16[32,512]{1,0:T(8,128)(2,1)S(1)}, u32[]{:S(2)}, u32[]{:S(2)}) collective-permute-start(bf16[32,512]{1,0:T(8,128)(2,1)} %shard_map.86), channel_id=1, source_target_pairs={{0,2},{2,0},{4,6},{6,4},{8,10},{10,8},{12,14},{14,12},{16,18},{18,... | collective-permute-start | bytes 98312 | tf_op jit(solution)/shard_map/ppermute | solution.py:279
  22.3 2.2 %collective-permute-start.4 = (bf16[400,512]{1,0:T(8,128)(2,1)S(1)}, bf16[400,512]{1,0:T(8,128)(2,1)S(1)}, u32[]{:S(2)}, u32[]{:S(2)}) collective-permute-start(bf16[400,512]{1,0:T(8,128)(2,1)S(1)} %collective-permute-done.3.prev2), channel_id=1, source_target_pairs={{0,2},{2,0},{4,6},{6,4},{8,10},{10,8},{12,14},{14,12},{16,18},{18,... | collective-permute-start | bytes 1228808 | tf_op jit(solution)/shard_map/ppermute | solution.py:279
  26.5 4.3 %collective-permute-start.8 = (f32[8,128]{1,0:T(8,128)S(1)}, f32[8,128]{1,0:T(8,128)S(1)}, u32[]{:S(2)}, u32[]{:S(2)}) collective-permute-start(f32[8,128]{1,0:T(8,128)S(1)} %get-tuple-element.30.row), channel_id=1, source_target_pairs={{0,2},{2,0},{4,6},{6,4},{8,10},{10,8},{12,14},{14,12},{16,18},{18,... | collective-permute-start | bytes 12296 | tf_op jit(solution)/shard_map/ppermute | solution.py:279
  27.1 3.7 %collective-permute-start.5 = (bf16[400,512]{1,0:T(8,128)(2,1)S(1)}, bf16[400,512]{1,0:T(8,128)(2,1)S(1)}, u32[]{:S(2)}, u32[]{:S(2)}) collective-permute-start(bf16[400,512]{1,0:T(8,128)(2,1)S(1)} %get-tuple-element.31.next2), channel_id=1, source_target_pairs={{0,2},{2,0},{4,6},{6,4},{8,10},{10,8},{12,14},{14,12},{16,18},{18,... | collective-permute-start | bytes 1228808 | tf_op jit(solution)/shard_map/ppermute | solution.py:279
  27.2 3.6 %collective-permute-start.7 = (bf16[32,512]{1,0:T(8,128)(2,1)S(1)}, bf16[32,512]{1,0:T(8,128)(2,1)S(1)}, u32[]{:S(2)}, u32[]{:S(2)}) collective-permute-start(bf16[32,512]{1,0:T(8,128)(2,1)S(1)} %get-tuple-element.32.lists), channel_id=1, source_target_pairs={{0,2},{2,0},{4,6},{6,4},{8,10},{10,8},{12,14},{14,12},{16,18},{18,... | collective-permute-start | bytes 98312 | tf_op jit(solution)/shard_map/ppermute | solution.py:279
  34.0 19.7 %collective-permute-start.9 = (bf16[400,512]{1,0:T(8,128)(2,1)S(1)}, bf16[400,512]{1,0:T(8,128)(2,1)S(1)}, u32[]{:S(2)}, u32[]{:S(2)}) collective-permute-start(bf16[400,512]{1,0:T(8,128)(2,1)S(1)} %get-tuple-element.34.own), channel_id=1, source_target_pairs={{0,1},{1,0},{2,3},{3,2},{4,5},{5,4},{6,7},{7,6},{8,9},{9,8},{10,11... | collective-permute-start | bytes 1228808 | tf_op jit(solution)/shard_map/ppermute | solution.py:326

commit v4 on v3

--- a/solution.py
+++ b/solution.py
@@ -67,15 +67,16 @@
 
 def softmax_terms(s_ref, log_ref, tail_row, q_ref):
     entities, edges = s_ref.shape
-    step = 32
+    step = 16384 // edges
     iota = lax.broadcasted_iota(jnp.int32, (step, edges), 0)
     top = jnp.full((8, edges), NEVER, F32)
     pos = jnp.zeros((8, edges), F32)
     for c in range(0, entities, step):
         s = s_ref[c:c + step, :]
         hit = jnp.where(iota == tail_row - c, s, 0.0)
-        first, second = log_ref[c:c + step, :128], log_ref[c:c + step, 128:]
-        log = jnp.concatenate([first, first, second, second], axis=1)
+        log = log_ref[c:c + step, :]
+        tiles = edges // log.shape[1]
+        log = jnp.concatenate([log[:, k // tiles * 128:k // tiles * 128 + 128] for k in range(edges // 128)], axis=1)
         s = s + log
         s_ref[c:c + step, :] = s
         for k in range(0, step, 8):
@@ -183,16 +184,25 @@
 
 def head_bucket(step, tail, q_in, r_in, log, heads, tails, live_groups, acc, hf, rf, qf, sf, qq):
     edges, (width, entities) = heads.shape[1], acc.shape
-    sf[...] = dot(tail[:width, :], q_in[...], TN)
-    loss, miss = softmax_terms(sf, log, tails[step:step + 1, :], qq)
-    live = live_row(live_groups[:, step:step + 1], edges)
-    hf[...] = dot(tail[:width, :], qq[...], NN)
+    half = edges // 2
+    groups = [slice(g * half, (g + 1) * half) for g in range(2)]
+    row = slice(step, step + 1)
+    for g in groups:
+        sf[:, g] = dot(tail[...], q_in[:, g], TN)
+    terms = [softmax_terms(sf.at[:, g], log.at[:, k * 128:(k + 1) * 128], tails[row, g], qq.at[:, g])
+             for k, g in enumerate(groups)]
+    live = live_row(live_groups[:, row], edges)
+    loss = jnp.concatenate([t[0] for t in terms], axis=1) * live
+    for g in groups:
+        hf[:, g] = dot(tail[...], qq[:, g], NN)
     rf[...] = r_in[...].astype(F32)
-    head_grad(hf, rf, miss * live * (1.0 / 256.0), qf)
-    high, low = split(qf[...])
-    head_hot = one_hot(heads[step:step + 1, :], entities)
-    acc[...] += dot(high, head_hot, NT) + dot(low, head_hot, NT)
-    return loss * live, live
+    for k, g in enumerate(groups):
+        head_grad(hf.at[:, g], rf.at[:, g], terms[k][1] * live[:, g] * (1.0 / 256.0), qf.at[:, g])
+    for g in groups:
+        high, low = split(qf[:, g])
+        head_hot = one_hot(heads[row, g], entities)
+        acc[...] += dot(high, head_hot, NT) + dot(low, head_hot, NT)
+    return loss, live
 
 
 def far_terms(step, rel, lists, r_out, log_out, hot):
@@ -213,7 +223,6 @@
 
 
 def heads2_kernel(prev2, q2, r2, log2, heads, tails, live_groups, part, sums, grad, sums_out, hf, rf, qf, sf, qq):
-    grad[...] = part[...]
     loss, live = head_bucket(2, prev2, q2, r2, log2, heads, tails, live_groups, grad, hf, rf, qf, sf, qq)
     sums_out[0:1, :] = sums[0:1, :] + loss
     sums_out[1:2, :] = sums[1:2, :] + live
@@ -221,7 +230,6 @@
 
 def heads1_kernel(sibling, swapped, q1, r1, log1, heads, tails, live_groups, part, sums, grad, row,
                   hf, rf, qf, sf, qq, prev1):
-    grad[...] = part[...]
     prev1[...] = jnp.where(lax.axis_index("blk") & 1 == 0, swapped[...], sibling[...])
     loss, live = head_bucket(1, prev1, q1, r1, log1, heads, tails, live_groups, grad, hf, rf, qf, sf, qq)
     loss_all = jnp.sum(sums[0:1, :] + loss, axis=1, keepdims=True)
@@ -235,7 +243,6 @@
 
 
 def tails2_kernel(rel, emb, next2, lists, part, grad, hot, hf, rf, qf, sf, qq, log):
-    grad[...] = part[...]
     far_terms(2, rel, lists, rf, log, hot)
     tail_bucket(2, emb, next2, lists, rf, log, grad, hf, qf, sf, qq)
 
@@ -308,16 +315,16 @@
         [hot] + work + [(logs, F32)], 20 * 10**9, [here] * 7)(emb, rel, *raw)
     own_lists = (heads, tails, live.T)
     swapped_prev = exchanged(prev2)
-    part, sums = kernel(heads2_kernel, [(grads, F32), ((8, edges), F32)], work, 8 * 10**9, [here] * 9)(
+    part, sums = kernel(heads2_kernel, [(grads, F32), ((8, edges), F32)], work, 8 * 10**9, [here] * 9, aliases={7: 0})(
         prev2, q2, r2, log2, *own_lists, part, sums)
-    part, row = kernel(heads1_kernel, [(grads, F32), (rows_of, F32)], work + [(big, BF16)], 3 * 10**9, [here] * 10)(
+    part, row = kernel(heads1_kernel, [(grads, F32), (rows_of, F32)], work + [(big, BF16)], 3 * 10**9, [here] * 10, aliases={8: 0})(
         sibling, swapped_prev, q1, r1, log1, *own_lists, part, sums)
     core_row = exchanged(row)
     next2, next2_lists = kernel(after_kernel, [(big, BF16), sent], [], 10**6, [here] * 3, aliases={0: 0, 1: 1})(
         next2, next2_lists, row)
     swapped_next = exchanged(next2)
     swapped_lists = exchanged(next2_lists)
-    (part,) = kernel(tails2_kernel, [(grads, F32)], [hot] + work + [(logs, F32)], 10 * 10**9, [here] * 5)(
+    (part,) = kernel(tails2_kernel, [(grads, F32)], [hot] + work + [(logs, F32)], 10 * 10**9, [here] * 5, aliases={4: 0})(
         rel, emb, next2, next2_lists, part)
     own, rows = kernel(
         tails1_kernel, [(grads, BF16), ((blocks, 128), F32)],

time: 54.8 us -> 54.6 us (level)
  transfers between devices with their start and end apart: 10 -> 10, of which waited for: 0 -> 0; matrix products, arithmetic and copies ran while one was open for 0% -> 0% of each run, Pallas kernels for 29% -> 28%
where the time goes in v4:
time: 54.6 us; the launch traced here: 54.5 us
  Pallas kernels  19.7 us (36%)
  blocking collectives  17.1 us (31%)
  starting transfers between devices  16.8 us (31%)
  between operations  0.8 us (1%)
    all_to_all x1, blocking collectives, per_device(): lax.all_to_all(rows, ('blk', 'rep'), 0, 0, tiled=True, axis_index_groups=...  17.1 us
    ppermute x3, starting transfers between devices, shifted(): return lax.ppermute(x, 'blk', [(i, (i + by) % peers) for i in range(peers)])  11.1 us
    pallas_call x1, Pallas kernels, per_device(): kernel(prepare_kernel, [(grads, F32), ((8, edges), F32)] + [(big, BF16)]...  7.03 us
    pallas_call x1, Pallas kernels, per_device(): kernel(tails1_kernel, [(grads, BF16), ((blocks, 128), F32)], [hot] + work...  3.19 us
    pallas_call x1, Pallas kernels, per_device(): kernel(tails2_kernel, [(grads, F32)], [hot] + work + [(logs, F32)], 10 *...  3.15 us
    ppermute x6, starting transfers between devices, exchanged(): lax.ppermute(x, 'blk', [(i, i ^ 1) for i in range(lax.axis_size('blk'))])  3.15 us
    ppermute x1, starting transfers between devices, per_device(): other = lax.ppermute(own, 'rep', [(0, 1), (1, 0)])  2.54 us
    pallas_call x1, Pallas kernels, per_device(): kernel(heads1_kernel, [(grads, F32), (rows_of, F32)], work + [(big, BF16)...  1.85 us
  transfers between devices with their start and end apart: 10, of which 0 were waited for; matrix products, arithmetic and copies ran while one was open for 0% of the time, Pallas kernels for 28%

profile of v4, /device:TPU:1, one launch (start us, length us, event | category | flops | bytes accessed | tf_op | source)
XLA Modules:
  0.0 54.5 jit_solution(15891730707205607401)
XLA Ops:
  0.6 2.2 %collective-permute-start.3 = (bf16[400,512]{1,0:T(8,128)(2,1)}, bf16[400,512]{1,0:T(8,128)(2,1)S(1)}, u32[]{:S(2)}, u32[]{:S(2)}) collective-permute-start(bf16[400,512]{1,0:T(8,128)(2,1)} %bitcast.14), channel_id=1, source_target_pairs={{0,4},{2,6},{4,8},{6,10},{8,12},{10,14},{12,16},{14,18},{16,20},{1... | collective-permute-start | bytes 1228808 | tf_op jit(solution)/shard_map/ppermute | solution.py:282
  2.8 1.2 %collective-permute-start = (bf16[400,512]{1,0:T(8,128)(2,1)}, bf16[400,512]{1,0:T(8,128)(2,1)S(1)}, u32[]{:S(2)}, u32[]{:S(2)}) collective-permute-start(bf16[400,512]{1,0:T(8,128)(2,1)} %bitcast.15), channel_id=1, source_target_pairs={{0,2},{2,0},{4,6},{6,4},{8,10},{10,8},{12,14},{14,12},{16,18},{18,... | collective-permute-start | bytes 1228808 | tf_op jit(solution)/shard_map/ppermute | solution.py:286
  4.0 7.2 %collective-permute-start.1 = (bf16[400,512]{1,0:T(8,128)(2,1)}, bf16[400,512]{1,0:T(8,128)(2,1)S(1)}, u32[]{:S(2)}, u32[]{:S(2)}) collective-permute-start(bf16[400,512]{1,0:T(8,128)(2,1)} %bitcast.16), channel_id=1, source_target_pairs={{0,252},{2,254},{4,0},{6,2},{8,4},{10,6},{12,8},{14,10},{16,12},{1... | collective-permute-start | bytes 1228808 | tf_op jit(solution)/shard_map/ppermute | solution.py:282
  11.3 0.0 copy-start
  11.3 0.0 copy-start.1
  11.3 0.0 copy-start.2
  11.3 0.0 copy-start.3
  11.3 0.0 copy-start.4
  11.3 0.0 copy-start.5
  11.3 0.0 copy-start.6
  11.3 1.6 %shard_map.86 = bf16[32,512]{1,0:T(8,128)(2,1)} custom-call(s32[3,512]{1,0:T(4,128)} %heads.5, s32[3,512]{1,0:T(4,128)} %tails.5, s32[3,512]{1,0:T(4,128)} %rels.1, s32[3,2,256]{2,1,0:T(2,128)} %negatives.1, s32[1,3]{1,0:T(1,128)} %bitcast.20), custom_call_target="tpu_custom_call" | custom-call | flops 2000000000 | bytes 4194304 | tf_op jit(solution)/shard_map/pallas_call | solution.py:305
  12.9 1.7 %collective-permute-start.2 = (bf16[32,512]{1,0:T(8,128)(2,1)}, bf16[32,512]{1,0:T(8,128)(2,1)S(1)}, u32[]{:S(2)}, u32[]{:S(2)}) collective-permute-start(bf16[32,512]{1,0:T(8,128)(2,1)} %shard_map.86), channel_id=1, source_target_pairs={{0,252},{2,254},{4,0},{6,2},{8,4},{10,6},{12,8},{14,10},{16,12},{1... | collective-permute-start | bytes 98312 | tf_op jit(solution)/shard_map/ppermute | solution.py:282
  14.6 0.6 %collective-permute-start.6 = (bf16[32,512]{1,0:T(8,128)(2,1)}, bf16[32,512]{1,0:T(8,128)(2,1)S(1)}, u32[]{:S(2)}, u32[]{:S(2)}) collective-permute-start(bf16[32,512]{1,0:T(8,128)(2,1)} %shard_map.86), channel_id=1, source_target_pairs={{0,2},{2,0},{4,6},{6,4},{8,10},{10,8},{12,14},{14,12},{16,18},{18,... | collective-permute-start | bytes 98312 | tf_op jit(solution)/shard_map/ppermute | solution.py:286
  15.2 0.0 copy-done
  15.2 0.0 copy-done.1
  15.2 0.0 copy-done.2
  15.2 0.0 copy-done.3
  15.2 0.0 copy-done.4
  15.2 0.0 copy-done.5
  15.2 0.0 copy-done.6
  15.3 7.0 %shard_map.87 = (f32[400,512]{1,0:T(8,128)S(1)}, f32[8,512]{1,0:T(8,128)S(1)}, bf16[400,512]{1,0:T(8,128)(2,1)S(1)}, bf16[400,512]{1,0:T(8,128)(2,1)S(1)}, bf16[...) custom-call(bf16[400,512]{1,0:T(8,128)(2,1)S(1)} %bitcast.17, ...), custom_call_target="tpu_custom_call" | custom-call | flops 20000000000 | bytes 4194304 | tf_op jit(solution)/shard_map/pallas_call | solution.py:312
  22.3 0.0 collective-permute-done.3.prev2
  22.3 0.3 collective-permute-start.4
  22.6 1.8 %shard_map.88 = (f32[400,512]{1,0:T(8,128)S(1)}, f32[8,512]{1,0:T(8,128)S(1)}) custom-call(bf16[400,512]{1,0:T(8,128)(2,1)S(1)} %collective-permute-done.3.prev2, bf16[400,512]{1,0:T(8,128)(2,1)S(1)} %get-tuple-element.23.q2, bf16[400,512]{1,0:T(8,128)(2,1)S(1)} %get-tuple-element.24.r2, ...), custom_call_target="tpu_custom_call", output_to_operand_aliasing={{0}: (7, {})} | custom-call | flops 8000000000 | bytes 4194304 | tf_op jit(solution)/shard_map/pallas_call | solution.py:318
  24.4 0.0 collective-permute-done.sibling
  24.4 0.0 collective-permute-done.4.swapped
  24.4 1.8 %shard_map.89 = (f32[400,512]{1,0:T(8,128)S(1)}, f32[8,128]{1,0:T(8,128)S(1)}) custom-call(bf16[400,512]{1,0:T(8,128)(2,1)S(1)} %collective-permute-done.sibling, bf16[400,512]{1,0:T(8,128)(2,1)S(1)} %collective-permute-done.4.swapped, bf16[400,512]{1,0:T(8,128)(2,1)S(1)} %get-tuple-element.20.q1, ...), custom_call_target="tpu_custom_call", output_to_operand_aliasing={{0}: (8, {})} | custom-call | flops 3000000000 | bytes 4194304 | tf_op jit(solution)/shard_map/pallas_call | solution.py:320
  26.3 0.6 %collective-permute-start.8 = (f32[8,128]{1,0:T(8,128)S(1)}, f32[8,128]{1,0:T(8,128)S(1)}, u32[]{:S(2)}, u32[]{:S(2)}) collective-permute-start(f32[8,128]{1,0:T(8,128)S(1)} %get-tuple-element.30.row), channel_id=1, source_target_pairs={{0,2},{2,0},{4,6},{6,4},{8,10},{10,8},{12,14},{14,12},{16,18},{18,... | collective-permute-start | bytes 12296 | tf_op jit(solution)/shard_map/ppermute | solution.py:286
  26.9 0.0 collective-permute-done.2.lists
  26.9 0.0 collective-permute-done.1.block
  26.9 0.1 collective-permute-start.5
  27.0 0.4 collective-permute-start.7
  27.4 3.2 %shard_map.91.part = f32[400,512]{1,0:T(8,128)S(1)} custom-call(bf16[400,2560]{1,0:T(8,128)(2,1)S(1)} %bitcast.12, bf16[400,512]{1,0:T(8,128)(2,1)S(1)} %bitcast.18, bf16[400,512]{1,0:T(8,128)(2,1)S(1)} %get-tuple-element.31.next2, bf16[32,512]{1,0:T(8,128)(2,1)S(1)} %get-tuple-element.32.lists, ...), custom_call_target="tpu_custom_call", output_to_operand_aliasing={{}: (4, {})} | custom-call | flops 10000000000 | bytes 4194304 | tf_op jit(solution)/shard_map/pallas_call | solution.py:327
  30.6 0.0 collective-permute-done.6.sibling_lists
  30.6 0.0 collective-permute-done.8.core_row
  30.6 0.0 collective-permute-done.7.swapped_lists
  30.6 0.0 collective-permute-done.5.swapped
  30.6 3.2 %shard_map.92 = (bf16[400,512]{1,0:T(8,128)(2,1)S(1)}, f32[128,128]{1,0:T(8,128)S(1)}) custom-call(bf16[400,2560]{1,0:T(8,128)(2,1)S(1)} %bitcast.13, bf16[400,512]{1,0:T(8,128)(2,1)S(1)} %bitcast.19, bf16[400,512]{1,0:T(8,128)(2,1)S(1)} %collective-permute-done.sibling, bf16[400,512]{1,0:T(8,128)(2,1)S(1)} %collective-permute-done.5.swapped, ...), custom_call_target="tpu_custom_call" | custom-call | flops 3000000000 | bytes 4194304 | tf_op jit(solution)/shard_map/pallas_call | solution.py:329
  33.8 2.5 %collective-permute-start.9 = (bf16[400,512]{1,0:T(8,128)(2,1)S(1)}, bf16[400,512]{1,0:T(8,128)(2,1)S(1)}, u32[]{:S(2)}, u32[]{:S(2)}) collective-permute-start(bf16[400,512]{1,0:T(8,128)(2,1)S(1)} %get-tuple-element.34.own), channel_id=1, source_target_pairs={{0,1},{1,0},{2,3},{3,2},{4,5},{5,4},{6,7},{7,6},{8,9},{9,8},{10,11... | collective-permute-start | bytes 1228808 | tf_op jit(solution)/shard_map/ppermute | solution.py:333
  36.3 17.1 %all_to_all.11 = f32[128,1,128]{2,1,0:T(1,128)S(1)} all-to-all(f32[128,1,128]{2,1,0:T(1,128)S(1)} %bitcast.10), channel_id=1, replica_groups={{0,1,4,5,8,9,12,13,16,17,20,21,24,25,28,29,32,33,36,37,40,41,44,45,48,4..., dimensions={0} | all-to-all | bytes 131072 | tf_op jit(solution)/shard_map/all_to_all | solution.py:334
  53.5 0.0 collective-permute-done.9.other
  53.5 1.0 %shard_map.93 = (f32[400,512]{1,0:T(8,128)}, f32[1,1]{1,0:T(1,128)}) custom-call(bf16[400,512]{1,0:T(8,128)(2,1)S(1)} %get-tuple-element.34.own, bf16[400,512]{1,0:T(8,128)(2,1)S(1)} %collective-permute-done.9.other, f32[128,128]{1,0:T(8,128)S(1)} %bitcast.9), custom_call_target="tpu_custom_call" | custom-call | flops 1000000 | bytes 4194304 | tf_op jit(solution)/shard_map/pallas_call | solution.py:336
  (1 shorter events, 0.0 us)
Async XLA Ops:
  0.6 21.7 %collective-permute-start.3 = (bf16[400,512]{1,0:T(8,128)(2,1)}, bf16[400,512]{1,0:T(8,128)(2,1)S(1)}, u32[]{:S(2)}, u32[]{:S(2)}) collective-permute-start(bf16[400,512]{1,0:T(8,128)(2,1)} %bitcast.14), channel_id=1, source_target_pairs={{0,4},{2,6},{4,8},{6,10},{8,12},{10,14},{12,16},{14,18},{16,20},{1... | collective-permute-start | bytes 1228808 | tf_op jit(solution)/shard_map/ppermute | solution.py:282
  2.8 21.6 %collective-permute-start = (bf16[400,512]{1,0:T(8,128)(2,1)}, bf16[400,512]{1,0:T(8,128)(2,1)S(1)}, u32[]{:S(2)}, u32[]{:S(2)}) collective-permute-start(bf16[400,512]{1,0:T(8,128)(2,1)} %bitcast.15), channel_id=1, source_target_pairs={{0,2},{2,0},{4,6},{6,4},{8,10},{10,8},{12,14},{14,12},{16,18},{18,... | collective-permute-start | bytes 1228808 | tf_op jit(solution)/shard_map/ppermute | solution.py:286
  4.0 22.8 %collective-permute-start.1 = (bf16[400,512]{1,0:T(8,128)(2,1)}, bf16[400,512]{1,0:T(8,128)(2,1)S(1)}, u32[]{:S(2)}, u32[]{:S(2)}) collective-permute-start(bf16[400,512]{1,0:T(8,128)(2,1)} %bitcast.16), channel_id=1, source_target_pairs={{0,252},{2,254},{4,0},{6,2},{8,4},{10,6},{12,8},{14,10},{16,12},{1... | collective-permute-start | bytes 1228808 | tf_op jit(solution)/shard_map/ppermute | solution.py:282
  11.3 3.9 %copy-start = (bf16[2560,400]{0,1:T(8,128)(2,1)S(1)}, bf16[2560,400]{0,1:T(8,128)(2,1)}, u32[]{:S(2)}) copy-start(bf16[2560,400]{0,1:T(8,128)(2,1)} %param.8) | copy-start | bytes 6144004
  11.3 3.9 %copy-start.1 = (bf16[512,400]{0,1:T(8,128)(2,1)S(1)}, bf16[512,400]{0,1:T(8,128)(2,1)}, u32[]{:S(2)}) copy-start(bf16[512,400]{0,1:T(8,128)(2,1)} %param.7) | copy-start | bytes 1228804
  11.3 3.9 %copy-start.2 = (s32[3,512]{1,0:T(4,128)S(1)}, s32[3,512]{1,0:T(4,128)}, u32[]{:S(2)}) copy-start(s32[3,512]{1,0:T(4,128)} %rels.1) | copy-start | bytes 18436
  11.3 3.9 %copy-start.3 = (s32[3,512]{1,0:T(4,128)S(1)}, s32[3,512]{1,0:T(4,128)}, u32[]{:S(2)}) copy-start(s32[3,512]{1,0:T(4,128)} %heads.5) | copy-start | bytes 18436
  11.3 3.9 %copy-start.4 = (s32[3,512]{1,0:T(4,128)S(1)}, s32[3,512]{1,0:T(4,128)}, u32[]{:S(2)}) copy-start(s32[3,512]{1,0:T(4,128)} %tails.5) | copy-start | bytes 18436
  11.3 3.9 %copy-start.5 = (s32[3,2,256]{2,1,0:T(2,128)S(1)}, s32[3,2,256]{2,1,0:T(2,128)}, u32[]{:S(2)}) copy-start(s32[3,2,256]{2,1,0:T(2,128)} %negatives.1) | copy-start | bytes 18436
  11.3 3.9 %copy-start.6 = (s32[3,1]{0,1:T(1,128)S(1)}, s32[3,1]{0,1:T(1,128)}, u32[]{:S(2)}) copy-start(s32[3,1]{0,1:T(1,128)} %param.13) | copy-start | bytes 40
  12.9 13.9 %collective-permute-start.2 = (bf16[32,512]{1,0:T(8,128)(2,1)}, bf16[32,512]{1,0:T(8,128)(2,1)S(1)}, u32[]{:S(2)}, u32[]{:S(2)}) collective-permute-start(bf16[32,512]{1,0:T(8,128)(2,1)} %shard_map.86), channel_id=1, source_target_pairs={{0,252},{2,254},{4,0},{6,2},{8,4},{10,6},{12,8},{14,10},{16,12},{1... | collective-permute-start | bytes 98312 | tf_op jit(solution)/shard_map/ppermute | solution.py:282
  14.6 15.9 %collective-permute-start.6 = (bf16[32,512]{1,0:T(8,128)(2,1)}, bf16[32,512]{1,0:T(8,128)(2,1)S(1)}, u32[]{:S(2)}, u32[]{:S(2)}) collective-permute-start(bf16[32,512]{1,0:T(8,128)(2,1)} %shard_map.86), channel_id=1, source_target_pairs={{0,2},{2,0},{4,6},{6,4},{8,10},{10,8},{12,14},{14,12},{16,18},{18,... | collective-permute-start | bytes 98312 | tf_op jit(solution)/shard_map/ppermute | solution.py:286
  22.3 2.1 %collective-permute-start.4 = (bf16[400,512]{1,0:T(8,128)(2,1)S(1)}, bf16[400,512]{1,0:T(8,128)(2,1)S(1)}, u32[]{:S(2)}, u32[]{:S(2)}) collective-permute-start(bf16[400,512]{1,0:T(8,128)(2,1)S(1)} %collective-permute-done.3.prev2), channel_id=1, source_target_pairs={{0,2},{2,0},{4,6},{6,4},{8,10},{10,8},{12,14},{14,12},{16,18},{18,... | collective-permute-start | bytes 1228808 | tf_op jit(solution)/shard_map/ppermute | solution.py:286
  26.3 4.3 %collective-permute-start.8 = (f32[8,128]{1,0:T(8,128)S(1)}, f32[8,128]{1,0:T(8,128)S(1)}, u32[]{:S(2)}, u32[]{:S(2)}) collective-permute-start(f32[8,128]{1,0:T(8,128)S(1)} %get-tuple-element.30.row), channel_id=1, source_target_pairs={{0,2},{2,0},{4,6},{6,4},{8,10},{10,8},{12,14},{14,12},{16,18},{18,... | collective-permute-start | bytes 12296 | tf_op jit(solution)/shard_map/ppermute | solution.py:286
  26.9 3.7 %collective-permute-start.5 = (bf16[400,512]{1,0:T(8,128)(2,1)S(1)}, bf16[400,512]{1,0:T(8,128)(2,1)S(1)}, u32[]{:S(2)}, u32[]{:S(2)}) collective-permute-start(bf16[400,512]{1,0:T(8,128)(2,1)S(1)} %get-tuple-element.31.next2), channel_id=1, source_target_pairs={{0,2},{2,0},{4,6},{6,4},{8,10},{10,8},{12,14},{14,12},{16,18},{18,... | collective-permute-start | bytes 1228808 | tf_op jit(solution)/shard_map/ppermute | solution.py:286
  27.0 3.6 %collective-permute-start.7 = (bf16[32,512]{1,0:T(8,128)(2,1)S(1)}, bf16[32,512]{1,0:T(8,128)(2,1)S(1)}, u32[]{:S(2)}, u32[]{:S(2)}) collective-permute-start(bf16[32,512]{1,0:T(8,128)(2,1)S(1)} %get-tuple-element.32.lists), channel_id=1, source_target_pairs={{0,2},{2,0},{4,6},{6,4},{8,10},{10,8},{12,14},{14,12},{16,18},{18,... | collective-permute-start | bytes 98312 | tf_op jit(solution)/shard_map/ppermute | solution.py:286
  33.8 19.7 %collective-permute-start.9 = (bf16[400,512]{1,0:T(8,128)(2,1)S(1)}, bf16[400,512]{1,0:T(8,128)(2,1)S(1)}, u32[]{:S(2)}, u32[]{:S(2)}) collective-permute-start(bf16[400,512]{1,0:T(8,128)(2,1)S(1)} %get-tuple-element.34.own), channel_id=1, source_target_pairs={{0,1},{1,0},{2,3},{3,2},{4,5},{5,4},{6,7},{7,6},{8,9},{9,8},{10,11... | collective-permute-start | bytes 1228808 | tf_op jit(solution)/shard_map/ppermute | solution.py:333

commit v5 on v4

--- a/solution.py
+++ b/solution.py
@@ -247,7 +247,7 @@
     tail_bucket(2, emb, next2, lists, rf, log, grad, hf, qf, sf, qq)
 
 
-def tails1_kernel(rel, emb, sibling, swapped, sibling_lists, swapped_lists, part, row, core_row, grad, rows,
+def tails1_kernel(rel, emb, sibling, swapped, sibling_lists, swapped_lists, part, row, grad,
                   hot, hf, rf, qf, sf, qq, acc, next1, lists, log):
     even = lax.axis_index("blk") & 1 == 0
     next1[...] = jnp.where(even, sibling[...], swapped[...])
@@ -256,7 +256,14 @@
     far_terms(1, rel, lists, rf, log, hot)
     tail_bucket(1, emb, next1, lists, rf, log, acc, hf, qf, sf, qq)
     grad[...] = acc[...].astype(BF16)
-    rows[...] = jnp.broadcast_to(row[0:1, :] + core_row[0:1, :], rows.shape)
+
+
+def add_kernel(row, other, out):
+    out[...] = row[...] + other[...]
+
+
+def rows_kernel(own, row, other, own_out, rows):
+    rows[...] = jnp.broadcast_to(row[0:1, :] + other[0:1, :], rows.shape)
 
 
 def finish_kernel(own, other, rows, grad, mean):
@@ -326,13 +333,17 @@
     swapped_lists = exchanged(next2_lists)
     (part,) = kernel(tails2_kernel, [(grads, F32)], [hot] + work + [(logs, F32)], 10 * 10**9, [here] * 5, aliases={4: 0})(
         rel, emb, next2, next2_lists, part)
-    own, rows = kernel(
-        tails1_kernel, [(grads, BF16), ((blocks, 128), F32)],
-        [hot] + work + [(grads, F32), (big, BF16), sent, (logs, F32)], 3 * 10**9, [here] * 9,
-    )(rel, emb, sibling, swapped_next, sibling_lists, swapped_lists, part, row, core_row)
+    (row,) = kernel(add_kernel, [(rows_of, F32)], [], 10**6, [here] * 2)(row, core_row)
+    rep_row = lax.ppermute(row, "rep", [(0, 1), (1, 0)])
+    (own,) = kernel(
+        tails1_kernel, [(grads, BF16)],
+        [hot] + work + [(grads, F32), (big, BF16), sent, (logs, F32)], 10 * 10**9, [here] * 8,
+    )(rel, emb, sibling, swapped_next, sibling_lists, swapped_lists, part, row)
+    own, rows = kernel(rows_kernel, [(grads, BF16), ((blocks // 2, 128), F32)], [], 10**6, [here] * 3, aliases={0: 0})(
+        own, row, rep_row)
     other = lax.ppermute(own, "rep", [(0, 1), (1, 0)])
-    rows = lax.all_to_all(rows, ("blk", "rep"), 0, 0, tiled=True,
-                          axis_index_groups=[[4 * i + 2 * k + r for i in range(blocks // 2) for r in (0, 1)] for k in (0, 1)])
+    rows = lax.all_to_all(rows, "blk", 0, 0, tiled=True,
+                          axis_index_groups=[[k + 2 * i for i in range(blocks // 2)] for k in (0, 1)])
     grad, mean = kernel(finish_kernel, [(grads, F32), ((1, 1), F32)], [], 10**6, [here] * 3)(own, other, rows)
     return grad.T, mean[0, 0]
 

time: 54.6 us -> 53.3 us (0.976)
  blocking collectives: 17.1 us -> 14.7 us
  starting transfers between devices: 16.8 us -> 17.6 us
    ppermute x0 -> x1, starting transfers between devices: none -> 2.57 us  [per_device(): rep_row = lax.ppermute(row, 'rep', [(0, 1), (1, 0)])]
    all_to_all x1, blocking collectives: 17.1 us -> 14.7 us  [per_device(): lax.all_to_all(rows, 'blk', 0, 0, tiled=True, axis_index_groups=[[k + 2 *...]
    ppermute x1, starting transfers between devices: 2.54 us -> 0.74 us  [per_device(): other = lax.ppermute(own, 'rep', [(0, 1), (1, 0)])]
    pallas_call x1 -> x3, Pallas kernels: 3.19 us -> 3.2 us  [the longest x1 3.19 us: per_device(): kernel(tails1_kernel, [(grads, BF16)], [hot] + work + [(grads, F32), (big...]
  transfers between devices with their start and end apart: 10 -> 11, of which waited for: 0 -> 0; matrix products, arithmetic and copies ran while one was open for 0% -> 0% of each run, Pallas kernels for 28% -> 35%
where the time goes in v5:
time: 53.3 us; the launch traced here: 52.8 us
  Pallas kernels  19.7 us (37%)
  starting transfers between devices  17.6 us (33%)
  blocking collectives  14.7 us (28%)
  between operations  0.8 us (2%)
    all_to_all x1, blocking collectives, per_device(): lax.all_to_all(rows, 'blk', 0, 0, tiled=True, axis_index_groups=[[k + 2 *...  14.7 us
    ppermute x3, starting transfers between devices, shifted(): return lax.ppermute(x, 'blk', [(i, (i + by) % peers) for i in range(peers)])  11.1 us
    pallas_call x1, Pallas kernels, per_device(): kernel(prepare_kernel, [(grads, F32), ((8, edges), F32)] + [(big, BF16)]...  7.01 us
    pallas_call x1, Pallas kernels, per_device(): kernel(tails1_kernel, [(grads, BF16)], [hot] + work + [(grads, F32), (big...  3.19 us
    pallas_call x1, Pallas kernels, per_device(): kernel(tails2_kernel, [(grads, F32)], [hot] + work + [(logs, F32)], 10 *...  3.16 us
    ppermute x6, starting transfers between devices, exchanged(): lax.ppermute(x, 'blk', [(i, i ^ 1) for i in range(lax.axis_size('blk'))])  3.16 us
    ppermute x1, starting transfers between devices, per_device(): rep_row = lax.ppermute(row, 'rep', [(0, 1), (1, 0)])  2.57 us
    pallas_call x1, Pallas kernels, per_device(): kernel(heads1_kernel, [(grads, F32), (rows_of, F32)], work + [(big, BF16)...  1.83 us
  transfers between devices with their start and end apart: 11, of which 0 were waited for; matrix products, arithmetic and copies ran while one was open for 0% of the time, Pallas kernels for 35%

profile of v5, /device:TPU:1, one launch (start us, length us, event | category | flops | bytes accessed | tf_op | source)
XLA Modules:
  0.0 52.8 jit_solution(6398737595704137746)
XLA Ops:
  0.6 2.2 %collective-permute-start.3 = (bf16[400,512]{1,0:T(8,128)(2,1)}, bf16[400,512]{1,0:T(8,128)(2,1)S(1)}, u32[]{:S(2)}, u32[]{:S(2)}) collective-permute-start(bf16[400,512]{1,0:T(8,128)(2,1)} %bitcast.14), channel_id=1, source_target_pairs={{0,4},{2,6},{4,8},{6,10},{8,12},{10,14},{12,16},{14,18},{16,20},{1... | collective-permute-start | bytes 1228808 | tf_op jit(solution)/shard_map/ppermute | solution.py:289
  2.8 1.2 %collective-permute-start = (bf16[400,512]{1,0:T(8,128)(2,1)}, bf16[400,512]{1,0:T(8,128)(2,1)S(1)}, u32[]{:S(2)}, u32[]{:S(2)}) collective-permute-start(bf16[400,512]{1,0:T(8,128)(2,1)} %bitcast.15), channel_id=1, source_target_pairs={{0,2},{2,0},{4,6},{6,4},{8,10},{10,8},{12,14},{14,12},{16,18},{18,... | collective-permute-start | bytes 1228808 | tf_op jit(solution)/shard_map/ppermute | solution.py:293
  4.0 7.2 %collective-permute-start.1 = (bf16[400,512]{1,0:T(8,128)(2,1)}, bf16[400,512]{1,0:T(8,128)(2,1)S(1)}, u32[]{:S(2)}, u32[]{:S(2)}) collective-permute-start(bf16[400,512]{1,0:T(8,128)(2,1)} %bitcast.16), channel_id=1, source_target_pairs={{0,252},{2,254},{4,0},{6,2},{8,4},{10,6},{12,8},{14,10},{16,12},{1... | collective-permute-start | bytes 1228808 | tf_op jit(solution)/shard_map/ppermute | solution.py:289
  11.3 0.0 copy-start
  11.3 0.0 copy-start.1
  11.3 0.0 copy-start.2
  11.3 0.0 copy-start.3
  11.3 0.0 copy-start.4
  11.3 0.0 copy-start.5
  11.3 0.0 copy-start.6
  11.3 1.6 %shard_map.86 = bf16[32,512]{1,0:T(8,128)(2,1)} custom-call(s32[3,512]{1,0:T(4,128)} %heads.5, s32[3,512]{1,0:T(4,128)} %tails.5, s32[3,512]{1,0:T(4,128)} %rels.1, s32[3,2,256]{2,1,0:T(2,128)} %negatives.1, s32[1,3]{1,0:T(1,128)} %bitcast.20), custom_call_target="tpu_custom_call" | custom-call | flops 2000000000 | bytes 4194304 | tf_op jit(solution)/shard_map/pallas_call | solution.py:312
  12.9 1.7 %collective-permute-start.2 = (bf16[32,512]{1,0:T(8,128)(2,1)}, bf16[32,512]{1,0:T(8,128)(2,1)S(1)}, u32[]{:S(2)}, u32[]{:S(2)}) collective-permute-start(bf16[32,512]{1,0:T(8,128)(2,1)} %shard_map.86), channel_id=1, source_target_pairs={{0,252},{2,254},{4,0},{6,2},{8,4},{10,6},{12,8},{14,10},{16,12},{1... | collective-permute-start | bytes 98312 | tf_op jit(solution)/shard_map/ppermute | solution.py:289
  14.6 0.6 %collective-permute-start.6 = (bf16[32,512]{1,0:T(8,128)(2,1)}, bf16[32,512]{1,0:T(8,128)(2,1)S(1)}, u32[]{:S(2)}, u32[]{:S(2)}) collective-permute-start(bf16[32,512]{1,0:T(8,128)(2,1)} %shard_map.86), channel_id=1, source_target_pairs={{0,2},{2,0},{4,6},{6,4},{8,10},{10,8},{12,14},{14,12},{16,18},{18,... | collective-permute-start | bytes 98312 | tf_op jit(solution)/shard_map/ppermute | solution.py:293
  15.2 0.0 copy-done
  15.2 0.0 copy-done.1
  15.2 0.0 copy-done.2
  15.2 0.0 copy-done.3
  15.2 0.0 copy-done.4
  15.2 0.0 copy-done.5
  15.2 0.0 copy-done.6
  15.3 7.0 %shard_map.87 = (f32[400,512]{1,0:T(8,128)S(1)}, f32[8,512]{1,0:T(8,128)S(1)}, bf16[400,512]{1,0:T(8,128)(2,1)S(1)}, bf16[400,512]{1,0:T(8,128)(2,1)S(1)}, bf16[...) custom-call(bf16[400,512]{1,0:T(8,128)(2,1)S(1)} %bitcast.17, ...), custom_call_target="tpu_custom_call" | custom-call | flops 20000000000 | bytes 4194304 | tf_op jit(solution)/shard_map/pallas_call | solution.py:319
  22.3 0.0 collective-permute-done.3.prev2
  22.3 0.3 collective-permute-start.4
  22.6 1.8 %shard_map.88 = (f32[400,512]{1,0:T(8,128)S(1)}, f32[8,512]{1,0:T(8,128)S(1)}) custom-call(bf16[400,512]{1,0:T(8,128)(2,1)S(1)} %collective-permute-done.3.prev2, bf16[400,512]{1,0:T(8,128)(2,1)S(1)} %get-tuple-element.23.q2, bf16[400,512]{1,0:T(8,128)(2,1)S(1)} %get-tuple-element.24.r2, ...), custom_call_target="tpu_custom_call", output_to_operand_aliasing={{0}: (7, {})} | custom-call | flops 8000000000 | bytes 4194304 | tf_op jit(solution)/shard_map/pallas_call | solution.py:325
  24.4 0.0 collective-permute-done.sibling
  24.4 0.0 collective-permute-done.4.swapped
  24.4 1.8 %shard_map.89 = (f32[400,512]{1,0:T(8,128)S(1)}, f32[8,128]{1,0:T(8,128)S(1)}) custom-call(bf16[400,512]{1,0:T(8,128)(2,1)S(1)} %collective-permute-done.sibling, bf16[400,512]{1,0:T(8,128)(2,1)S(1)} %collective-permute-done.4.swapped, bf16[400,512]{1,0:T(8,128)(2,1)S(1)} %get-tuple-element.20.q1, ...), custom_call_target="tpu_custom_call", output_to_operand_aliasing={{0}: (8, {})} | custom-call | flops 3000000000 | bytes 4194304 | tf_op jit(solution)/shard_map/pallas_call | solution.py:327
  26.3 0.6 %collective-permute-start.8 = (f32[8,128]{1,0:T(8,128)S(1)}, f32[8,128]{1,0:T(8,128)S(1)}, u32[]{:S(2)}, u32[]{:S(2)}) collective-permute-start(f32[8,128]{1,0:T(8,128)S(1)} %get-tuple-element.30.row), channel_id=1, source_target_pairs={{0,2},{2,0},{4,6},{6,4},{8,10},{10,8},{12,14},{14,12},{16,18},{18,... | collective-permute-start | bytes 12296 | tf_op jit(solution)/shard_map/ppermute | solution.py:293
  26.8 0.0 collective-permute-done.2.lists
  26.8 0.0 collective-permute-done.1.block
  26.9 0.1 collective-permute-start.5
  27.0 0.4 collective-permute-start.7
  27.4 3.2 %shard_map.91.part = f32[400,512]{1,0:T(8,128)S(1)} custom-call(bf16[400,2560]{1,0:T(8,128)(2,1)S(1)} %bitcast.12, bf16[400,512]{1,0:T(8,128)(2,1)S(1)} %bitcast.18, bf16[400,512]{1,0:T(8,128)(2,1)S(1)} %get-tuple-element.31.next2, bf16[32,512]{1,0:T(8,128)(2,1)S(1)} %get-tuple-element.32.lists, ...), custom_call_target="tpu_custom_call", output_to_operand_aliasing={{}: (4, {})} | custom-call | flops 10000000000 | bytes 4194304 | tf_op jit(solution)/shard_map/pallas_call | solution.py:334
  30.5 0.0 collective-permute-done.8.other
  30.6 2.6 %collective-permute-start.9 = (f32[8,128]{1,0:T(8,128)S(1)}, f32[8,128]{1,0:T(8,128)S(1)}, u32[]{:S(2)}, u32[]{:S(2)}) collective-permute-start(f32[8,128]{1,0:T(8,128)S(1)} %shard_map.92.row), channel_id=1, source_target_pairs={{0,1},{1,0},{2,3},{3,2},{4,5},{5,4},{6,7},{7,6},{8,9},{9,8},{10,11... | collective-permute-start | bytes 12296 | tf_op jit(solution)/shard_map/ppermute | solution.py:337
  33.1 0.0 collective-permute-done.6.sibling_lists
  33.1 0.0 collective-permute-done.7.swapped_lists
  33.1 0.0 collective-permute-done.5.swapped
  33.1 3.2 %shard_map.93.own = bf16[400,512]{1,0:T(8,128)(2,1)S(1)} custom-call(bf16[400,2560]{1,0:T(8,128)(2,1)S(1)} %bitcast.13, bf16[400,512]{1,0:T(8,128)(2,1)S(1)} %bitcast.19, bf16[400,512]{1,0:T(8,128)(2,1)S(1)} %collective-permute-done.sibling, bf16[400,512]{1,0:T(8,128)(2,1)S(1)} %collective-permute-done.5.swapped, ...), custom_call_target="tpu_custom_call" | custom-call | flops 10000000000 | bytes 4194304 | tf_op jit(solution)/shard_map/pallas_call | solution.py:338
  36.3 0.0 collective-permute-done.9.other
  36.4 0.7 %collective-permute-start.10 = (bf16[400,512]{1,0:T(8,128)(2,1)S(1)}, bf16[400,512]{1,0:T(8,128)(2,1)S(1)}, u32[]{:S(2)}, u32[]{:S(2)}) collective-permute-start(bf16[400,512]{1,0:T(8,128)(2,1)S(1)} %get-tuple-element.34.own), channel_id=1, source_target_pairs={{0,1},{1,0},{2,3},{3,2},{4,5},{5,4},{6,7},{7,6},{8,9},{9,8},{10,11... | collective-permute-start | bytes 1228808 | tf_op jit(solution)/shard_map/ppermute | solution.py:344
  37.1 14.7 %all_to_all.11 = f32[64,1,128]{2,1,0:T(1,128)S(1)} all-to-all(f32[64,1,128]{2,1,0:T(1,128)S(1)} %bitcast.10), channel_id=1, replica_groups={{0,4,8,12,16,20,24,28,32,36,40,44,48,52,56,60,64,68,72,76,80,84,88,92,9..., dimensions={0} | all-to-all | bytes 65536 | tf_op jit(solution)/shard_map/all_to_all | solution.py:345
  51.8 0.0 collective-permute-done.10.other
  51.8 1.0 %shard_map.95 = (f32[400,512]{1,0:T(8,128)}, f32[1,1]{1,0:T(1,128)}) custom-call(bf16[400,512]{1,0:T(8,128)(2,1)S(1)} %get-tuple-element.34.own, bf16[400,512]{1,0:T(8,128)(2,1)S(1)} %collective-permute-done.10.other, f32[64,128]{1,0:T(8,128)S(1)} %bitcast.9), custom_call_target="tpu_custom_call" | custom-call | flops 1000000 | bytes 4194304 | tf_op jit(solution)/shard_map/pallas_call | solution.py:347
  (3 shorter events, 0.0 us)
Async XLA Ops:
  0.6 21.6 %collective-permute-start.3 = (bf16[400,512]{1,0:T(8,128)(2,1)}, bf16[400,512]{1,0:T(8,128)(2,1)S(1)}, u32[]{:S(2)}, u32[]{:S(2)}) collective-permute-start(bf16[400,512]{1,0:T(8,128)(2,1)} %bitcast.14), channel_id=1, source_target_pairs={{0,4},{2,6},{4,8},{6,10},{8,12},{10,14},{12,16},{14,18},{16,20},{1... | collective-permute-start | bytes 1228808 | tf_op jit(solution)/shard_map/ppermute | solution.py:289
  2.8 21.6 %collective-permute-start = (bf16[400,512]{1,0:T(8,128)(2,1)}, bf16[400,512]{1,0:T(8,128)(2,1)S(1)}, u32[]{:S(2)}, u32[]{:S(2)}) collective-permute-start(bf16[400,512]{1,0:T(8,128)(2,1)} %bitcast.15), channel_id=1, source_target_pairs={{0,2},{2,0},{4,6},{6,4},{8,10},{10,8},{12,14},{14,12},{16,18},{18,... | collective-permute-start | bytes 1228808 | tf_op jit(solution)/shard_map/ppermute | solution.py:293
  4.0 22.8 %collective-permute-start.1 = (bf16[400,512]{1,0:T(8,128)(2,1)}, bf16[400,512]{1,0:T(8,128)(2,1)S(1)}, u32[]{:S(2)}, u32[]{:S(2)}) collective-permute-start(bf16[400,512]{1,0:T(8,128)(2,1)} %bitcast.16), channel_id=1, source_target_pairs={{0,252},{2,254},{4,0},{6,2},{8,4},{10,6},{12,8},{14,10},{16,12},{1... | collective-permute-start | bytes 1228808 | tf_op jit(solution)/shard_map/ppermute | solution.py:289
  11.3 3.9 %copy-start = (bf16[2560,400]{0,1:T(8,128)(2,1)S(1)}, bf16[2560,400]{0,1:T(8,128)(2,1)}, u32[]{:S(2)}) copy-start(bf16[2560,400]{0,1:T(8,128)(2,1)} %param.8) | copy-start | bytes 6144004
  11.3 3.9 %copy-start.1 = (bf16[512,400]{0,1:T(8,128)(2,1)S(1)}, bf16[512,400]{0,1:T(8,128)(2,1)}, u32[]{:S(2)}) copy-start(bf16[512,400]{0,1:T(8,128)(2,1)} %param.7) | copy-start | bytes 1228804
  11.3 3.9 %copy-start.2 = (s32[3,512]{1,0:T(4,128)S(1)}, s32[3,512]{1,0:T(4,128)}, u32[]{:S(2)}) copy-start(s32[3,512]{1,0:T(4,128)} %rels.1) | copy-start | bytes 18436
  11.3 3.9 %copy-start.3 = (s32[3,512]{1,0:T(4,128)S(1)}, s32[3,512]{1,0:T(4,128)}, u32[]{:S(2)}) copy-start(s32[3,512]{1,0:T(4,128)} %heads.5) | copy-start | bytes 18436
  11.3 3.9 %copy-start.4 = (s32[3,512]{1,0:T(4,128)S(1)}, s32[3,512]{1,0:T(4,128)}, u32[]{:S(2)}) copy-start(s32[3,512]{1,0:T(4,128)} %tails.5) | copy-start | bytes 18436
  11.3 3.9 %copy-start.5 = (s32[3,2,256]{2,1,0:T(2,128)S(1)}, s32[3,2,256]{2,1,0:T(2,128)}, u32[]{:S(2)}) copy-start(s32[3,2,256]{2,1,0:T(2,128)} %negatives.1) | copy-start | bytes 18436
  11.3 3.9 %copy-start.6 = (s32[3,1]{0,1:T(1,128)S(1)}, s32[3,1]{0,1:T(1,128)}, u32[]{:S(2)}) copy-start(s32[3,1]{0,1:T(1,128)} %param.13) | copy-start | bytes 40
  12.9 13.9 %collective-permute-start.2 = (bf16[32,512]{1,0:T(8,128)(2,1)}, bf16[32,512]{1,0:T(8,128)(2,1)S(1)}, u32[]{:S(2)}, u32[]{:S(2)}) collective-permute-start(bf16[32,512]{1,0:T(8,128)(2,1)} %shard_map.86), channel_id=1, source_target_pairs={{0,252},{2,254},{4,0},{6,2},{8,4},{10,6},{12,8},{14,10},{16,12},{1... | collective-permute-start | bytes 98312 | tf_op jit(solution)/shard_map/ppermute | solution.py:289
  14.6 18.5 %collective-permute-start.6 = (bf16[32,512]{1,0:T(8,128)(2,1)}, bf16[32,512]{1,0:T(8,128)(2,1)S(1)}, u32[]{:S(2)}, u32[]{:S(2)}) collective-permute-start(bf16[32,512]{1,0:T(8,128)(2,1)} %shard_map.86), channel_id=1, source_target_pairs={{0,2},{2,0},{4,6},{6,4},{8,10},{10,8},{12,14},{14,12},{16,18},{18,... | collective-permute-start | bytes 98312 | tf_op jit(solution)/shard_map/ppermute | solution.py:293
  22.3 2.1 %collective-permute-start.4 = (bf16[400,512]{1,0:T(8,128)(2,1)S(1)}, bf16[400,512]{1,0:T(8,128)(2,1)S(1)}, u32[]{:S(2)}, u32[]{:S(2)}) collective-permute-start(bf16[400,512]{1,0:T(8,128)(2,1)S(1)} %collective-permute-done.3.prev2), channel_id=1, source_target_pairs={{0,2},{2,0},{4,6},{6,4},{8,10},{10,8},{12,14},{14,12},{16,18},{18,... | collective-permute-start | bytes 1228808 | tf_op jit(solution)/shard_map/ppermute | solution.py:293
  26.3 4.3 %collective-permute-start.8 = (f32[8,128]{1,0:T(8,128)S(1)}, f32[8,128]{1,0:T(8,128)S(1)}, u32[]{:S(2)}, u32[]{:S(2)}) collective-permute-start(f32[8,128]{1,0:T(8,128)S(1)} %get-tuple-element.30.row), channel_id=1, source_target_pairs={{0,2},{2,0},{4,6},{6,4},{8,10},{10,8},{12,14},{14,12},{16,18},{18,... | collective-permute-start | bytes 12296 | tf_op jit(solution)/shard_map/ppermute | solution.py:293
  26.9 6.3 %collective-permute-start.5 = (bf16[400,512]{1,0:T(8,128)(2,1)S(1)}, bf16[400,512]{1,0:T(8,128)(2,1)S(1)}, u32[]{:S(2)}, u32[]{:S(2)}) collective-permute-start(bf16[400,512]{1,0:T(8,128)(2,1)S(1)} %get-tuple-element.31.next2), channel_id=1, source_target_pairs={{0,2},{2,0},{4,6},{6,4},{8,10},{10,8},{12,14},{14,12},{16,18},{18,... | collective-permute-start | bytes 1228808 | tf_op jit(solution)/shard_map/ppermute | solution.py:293
  27.0 6.2 %collective-permute-start.7 = (bf16[32,512]{1,0:T(8,128)(2,1)S(1)}, bf16[32,512]{1,0:T(8,128)(2,1)S(1)}, u32[]{:S(2)}, u32[]{:S(2)}) collective-permute-start(bf16[32,512]{1,0:T(8,128)(2,1)S(1)} %get-tuple-element.32.lists), channel_id=1, source_target_pairs={{0,2},{2,0},{4,6},{6,4},{8,10},{10,8},{12,14},{14,12},{16,18},{18,... | collective-permute-start | bytes 98312 | tf_op jit(solution)/shard_map/ppermute | solution.py:293
  30.6 5.8 %collective-permute-start.9 = (f32[8,128]{1,0:T(8,128)S(1)}, f32[8,128]{1,0:T(8,128)S(1)}, u32[]{:S(2)}, u32[]{:S(2)}) collective-permute-start(f32[8,128]{1,0:T(8,128)S(1)} %shard_map.92.row), channel_id=1, source_target_pairs={{0,1},{1,0},{2,3},{3,2},{4,5},{5,4},{6,7},{7,6},{8,9},{9,8},{10,11... | collective-permute-start | bytes 12296 | tf_op jit(solution)/shard_map/ppermute | solution.py:337
  36.4 15.5 %collective-permute-start.10 = (bf16[400,512]{1,0:T(8,128)(2,1)S(1)}, bf16[400,512]{1,0:T(8,128)(2,1)S(1)}, u32[]{:S(2)}, u32[]{:S(2)}) collective-permute-start(bf16[400,512]{1,0:T(8,128)(2,1)S(1)} %get-tuple-element.34.own), channel_id=1, source_target_pairs={{0,1},{1,0},{2,3},{3,2},{4,5},{5,4},{6,7},{7,6},{8,9},{9,8},{10,11... | collective-permute-start | bytes 1228808 | tf_op jit(solution)/shard_map/ppermute | solution.py:344

commit v6 on v5

--- a/solution.py
+++ b/solution.py
@@ -228,9 +228,7 @@
     sums_out[1:2, :] = sums[1:2, :] + live
 
 
-def heads1_kernel(sibling, swapped, q1, r1, log1, heads, tails, live_groups, part, sums, grad, row,
-                  hf, rf, qf, sf, qq, prev1):
-    prev1[...] = jnp.where(lax.axis_index("blk") & 1 == 0, swapped[...], sibling[...])
+def heads1_kernel(prev1, q1, r1, log1, heads, tails, live_groups, part, sums, grad, row, hf, rf, qf, sf, qq):
     loss, live = head_bucket(1, prev1, q1, r1, log1, heads, tails, live_groups, grad, hf, rf, qf, sf, qq)
     loss_all = jnp.sum(sums[0:1, :] + loss, axis=1, keepdims=True)
     live_all = jnp.sum(sums[1:2, :] + live, axis=1, keepdims=True)
@@ -238,8 +236,14 @@
     row[...] = jnp.where(lane == 0, loss_all, jnp.where(lane == 1, live_all, 0.0))
 
 
-def after_kernel(block, lists, row, block_out, lists_out):
-    pass
+def choose_kernel(emb, prev2, passed):
+    passed[...] = jnp.where(lax.axis_index("blk") & 1 == 0, emb[...], prev2[...])
+
+
+def after_kernel(block, lists, emb, own_lists, row, block_out, lists_out, passed, passed_lists):
+    even = lax.axis_index("blk") & 1 == 0
+    passed[...] = jnp.where(even, block[...], emb[...])
+    passed_lists[...] = jnp.where(even, lists[...], own_lists[...])
 
 
 def tails2_kernel(rel, emb, next2, lists, part, grad, hot, hf, rf, qf, sf, qq, log):
@@ -247,11 +251,7 @@
     tail_bucket(2, emb, next2, lists, rf, log, grad, hf, qf, sf, qq)
 
 
-def tails1_kernel(rel, emb, sibling, swapped, sibling_lists, swapped_lists, part, row, grad,
-                  hot, hf, rf, qf, sf, qq, acc, next1, lists, log):
-    even = lax.axis_index("blk") & 1 == 0
-    next1[...] = jnp.where(even, sibling[...], swapped[...])
-    lists[...] = jnp.where(even, sibling_lists[...], swapped_lists[...])
+def tails1_kernel(rel, emb, next1, lists, part, row, grad, hot, hf, rf, qf, sf, qq, acc, log):
     acc[...] = part[...]
     far_terms(1, rel, lists, rf, log, hot)
     tail_bucket(1, emb, next1, lists, rf, log, acc, hf, qf, sf, qq)
@@ -307,7 +307,6 @@
     raw = (heads, tails, rels, negatives, live.T)
     prev2 = shifted(emb, 2)
     next2 = shifted(emb, -2)
-    sibling = exchanged(emb)
     sent = ((EXTRA, edges), BF16)
     (lists,) = kernel(
         pack_kernel, [sent],
@@ -315,30 +314,31 @@
         2 * 10**9, [pltpu.HBM] * len(raw), 56,
     )(*raw)
     next2_lists = shifted(lists, -2)
-    sibling_lists = exchanged(lists)
     part, sums, q1, q2, r1, r2, log1, log2 = kernel(
         prepare_kernel,
         [(grads, F32), ((8, edges), F32)] + [(big, BF16)] * 4 + [(logs, F32)] * 2,
         [hot] + work + [(logs, F32)], 20 * 10**9, [here] * 7)(emb, rel, *raw)
     own_lists = (heads, tails, live.T)
-    swapped_prev = exchanged(prev2)
+    (passed,) = kernel(choose_kernel, [(big, BF16)], [], 10**6, [here] * 2)(emb, prev2)
+    prev1 = exchanged(passed)
     part, sums = kernel(heads2_kernel, [(grads, F32), ((8, edges), F32)], work, 8 * 10**9, [here] * 9, aliases={7: 0})(
         prev2, q2, r2, log2, *own_lists, part, sums)
-    part, row = kernel(heads1_kernel, [(grads, F32), (rows_of, F32)], work + [(big, BF16)], 3 * 10**9, [here] * 10, aliases={8: 0})(
-        sibling, swapped_prev, q1, r1, log1, *own_lists, part, sums)
+    part, row = kernel(heads1_kernel, [(grads, F32), (rows_of, F32)], work, 3 * 10**9, [here] * 9, aliases={7: 0})(
+        prev1, q1, r1, log1, *own_lists, part, sums)
     core_row = exchanged(row)
-    next2, next2_lists = kernel(after_kernel, [(big, BF16), sent], [], 10**6, [here] * 3, aliases={0: 0, 1: 1})(
-        next2, next2_lists, row)
-    swapped_next = exchanged(next2)
-    swapped_lists = exchanged(next2_lists)
+    next2, next2_lists, passed, passed_lists = kernel(
+        after_kernel, [(big, BF16), sent] * 2, [], 10**6, [here] * 5, aliases={0: 0, 1: 1})(
+        next2, next2_lists, emb, lists, row)
+    next1 = exchanged(passed)
+    lists1 = exchanged(passed_lists)
     (part,) = kernel(tails2_kernel, [(grads, F32)], [hot] + work + [(logs, F32)], 10 * 10**9, [here] * 5, aliases={4: 0})(
         rel, emb, next2, next2_lists, part)
     (row,) = kernel(add_kernel, [(rows_of, F32)], [], 10**6, [here] * 2)(row, core_row)
     rep_row = lax.ppermute(row, "rep", [(0, 1), (1, 0)])
     (own,) = kernel(
         tails1_kernel, [(grads, BF16)],
-        [hot] + work + [(grads, F32), (big, BF16), sent, (logs, F32)], 10 * 10**9, [here] * 8,
-    )(rel, emb, sibling, swapped_next, sibling_lists, swapped_lists, part, row)
+        [hot] + work + [(grads, F32), (logs, F32)], 10 * 10**9, [here] * 6,
+    )(rel, emb, next1, lists1, part, row)
     own, rows = kernel(rows_kernel, [(grads, BF16), ((blocks // 2, 128), F32)], [], 10**6, [here] * 3, aliases={0: 0})(
         own, row, rep_row)
     other = lax.ppermute(own, "rep", [(0, 1), (1, 0)])

time: 53.3 us -> 53.3 us (level)
    ppermute x6 -> x4, starting transfers between devices: 3.16 us -> 2.55 us  [exchanged(): lax.ppermute(x, 'blk', [(i, i ^ 1) for i in range(lax.axis_size('blk'))])]
    pallas_call x3 -> x4, Pallas kernels: 5.02 us -> 5.08 us  [the longest x1 3.15 us: per_device(): kernel(tails1_kernel, [(grads, BF16)], [hot] + work + [(grads, F32), (log...]
  transfers between devices with their start and end apart: 11 -> 9, of which waited for: 0 -> 0; matrix products, arithmetic and copies ran while one was open for 0% -> 0% of each run, Pallas kernels for 35% -> 36%
where the time goes in v6:
time: 53.3 us; the launch traced here: 52.6 us
  Pallas kernels  19.7 us (37%)
  starting transfers between devices  17.3 us (32%)
  blocking collectives  14.7 us (28%)
  between operations  0.83 us (2%)
    all_to_all x1, blocking collectives, per_device(): lax.all_to_all(rows, 'blk', 0, 0, tiled=True, axis_index_groups=[[k + 2 *...  14.7 us
    ppermute x3, starting transfers between devices, shifted(): return lax.ppermute(x, 'blk', [(i, (i + by) % peers) for i in range(peers)])  11.4 us
    pallas_call x1, Pallas kernels, per_device(): kernel(prepare_kernel, [(grads, F32), ((8, edges), F32)] + [(big, BF16)]...  7.01 us
    pallas_call x1, Pallas kernels, per_device(): kernel(tails2_kernel, [(grads, F32)], [hot] + work + [(logs, F32)], 10 *...  3.16 us
    pallas_call x1, Pallas kernels, per_device(): kernel(tails1_kernel, [(grads, BF16)], [hot] + work + [(grads, F32), (log...  3.15 us
    ppermute x4, starting transfers between devices, exchanged(): lax.ppermute(x, 'blk', [(i, i ^ 1) for i in range(lax.axis_size('blk'))])  2.55 us
    ppermute x1, starting transfers between devices, per_device(): rep_row = lax.ppermute(row, 'rep', [(0, 1), (1, 0)])  2.53 us
    pallas_call x1, Pallas kernels, per_device(): kernel(heads1_kernel, [(grads, F32), (rows_of, F32)], work, 3 * 10 ** 9,...  1.82 us
  transfers between devices with their start and end apart: 9, of which 0 were waited for; matrix products, arithmetic and copies ran while one was open for 0% of the time, Pallas kernels for 36%

profile of v6, /device:TPU:1, one launch (start us, length us, event | category | flops | bytes accessed | tf_op | source)
XLA Modules:
  0.0 52.6 jit_solution(180736080940246229)
XLA Ops:
  0.6 2.2 %collective-permute-start.2 = (bf16[400,512]{1,0:T(8,128)(2,1)}, bf16[400,512]{1,0:T(8,128)(2,1)S(1)}, u32[]{:S(2)}, u32[]{:S(2)}) collective-permute-start(bf16[400,512]{1,0:T(8,128)(2,1)} %bitcast.9), channel_id=1, source_target_pairs={{0,4},{2,6},{4,8},{6,10},{8,12},{10,14},{12,16},{14,18},{16,20},{1... | collective-permute-start | bytes 1228808 | tf_op jit(solution)/shard_map/ppermute | solution.py:289
  2.8 7.7 %collective-permute-start = (bf16[400,512]{1,0:T(8,128)(2,1)}, bf16[400,512]{1,0:T(8,128)(2,1)S(1)}, u32[]{:S(2)}, u32[]{:S(2)}) collective-permute-start(bf16[400,512]{1,0:T(8,128)(2,1)} %bitcast.10), channel_id=1, source_target_pairs={{0,252},{2,254},{4,0},{6,2},{8,4},{10,6},{12,8},{14,10},{16,12},{1... | collective-permute-start | bytes 1228808 | tf_op jit(solution)/shard_map/ppermute | solution.py:289
  10.6 0.0 copy-start
  10.6 0.0 copy-start.2
  10.6 0.0 copy-start.3
  10.6 0.0 copy-start.4
  10.6 0.0 copy-start.5
  10.6 0.0 copy-start.6
  10.6 0.0 copy-start.7
  10.6 1.6 %shard_map.86.own_lists = bf16[32,512]{1,0:T(8,128)(2,1)} custom-call(s32[3,512]{1,0:T(4,128)} %heads.5, s32[3,512]{1,0:T(4,128)} %tails.5, s32[3,512]{1,0:T(4,128)} %rels.1, s32[3,2,256]{2,1,0:T(2,128)} %negatives.1, s32[1,3]{1,0:T(1,128)} %bitcast.21), custom_call_target="tpu_custom_call" | custom-call | flops 2000000000 | bytes 4194304 | tf_op jit(solution)/shard_map/pallas_call | solution.py:311
  12.2 1.5 %collective-permute-start.1 = (bf16[32,512]{1,0:T(8,128)(2,1)}, bf16[32,512]{1,0:T(8,128)(2,1)S(1)}, u32[]{:S(2)}, u32[]{:S(2)}) collective-permute-start(bf16[32,512]{1,0:T(8,128)(2,1)} %shard_map.86.own_lists), channel_id=1, source_target_pairs={{0,252},{2,254},{4,0},{6,2},{8,4},{10,6},{12,8},{14,10},{16,12},{1... | collective-permute-start | bytes 98312 | tf_op jit(solution)/shard_map/ppermute | solution.py:289
  13.7 0.0 copy-done
  13.7 0.0 copy-done.2
  13.7 0.0 copy-done.3
  13.7 0.0 copy-done.4
  13.7 0.0 copy-done.5
  13.7 0.0 copy-done.6
  13.7 0.0 copy-done.7
  13.7 7.0 %shard_map.88 = (f32[400,512]{1,0:T(8,128)S(1)}, f32[8,512]{1,0:T(8,128)S(1)}, bf16[400,512]{1,0:T(8,128)(2,1)S(1)}, bf16[400,512]{1,0:T(8,128)(2,1)S(1)}, bf16[...) custom-call(bf16[400,512]{1,0:T(8,128)(2,1)S(1)} %bitcast.11, ...), custom_call_target="tpu_custom_call" | custom-call | flops 20000000000 | bytes 4194304 | tf_op jit(solution)/shard_map/pallas_call | solution.py:317
  20.8 0.0 collective-permute-done.2.prev2
  20.8 1.6 %collective-permute-start.3 = (bf16[400,512]{1,0:T(8,128)(2,1)S(1)}, bf16[400,512]{1,0:T(8,128)(2,1)S(1)}, u32[]{:S(2)}, u32[]{:S(2)}) collective-permute-start(bf16[400,512]{1,0:T(8,128)(2,1)S(1)} %shard_map.87), channel_id=1, source_target_pairs={{0,2},{2,0},{4,6},{6,4},{8,10},{10,8},{12,14},{14,12},{16,18},{18,... | collective-permute-start | bytes 1228808 | tf_op jit(solution)/shard_map/ppermute | solution.py:293
  22.4 1.8 %shard_map.89 = (f32[400,512]{1,0:T(8,128)S(1)}, f32[8,512]{1,0:T(8,128)S(1)}) custom-call(bf16[400,512]{1,0:T(8,128)(2,1)S(1)} %collective-permute-done.2.prev2, bf16[400,512]{1,0:T(8,128)(2,1)S(1)} %get-tuple-element.25.q2, bf16[400,512]{1,0:T(8,128)(2,1)S(1)} %get-tuple-element.26.r2, ...), custom_call_target="tpu_custom_call", output_to_operand_aliasing={{0}: (7, {})} | custom-call | flops 8000000000 | bytes 4194304 | tf_op jit(solution)/shard_map/pallas_call | solution.py:324
  24.2 0.0 collective-permute-done.3.prev1
  24.3 0.0 copy-start.1
  24.3 1.8 %shard_map.90 = (f32[400,512]{1,0:T(8,128)S(1)}, f32[8,128]{1,0:T(8,128)S(1)}) custom-call(bf16[400,512]{1,0:T(8,128)(2,1)S(1)} %collective-permute-done.3.prev1, bf16[400,512]{1,0:T(8,128)(2,1)S(1)} %get-tuple-element.22.q1, bf16[400,512]{1,0:T(8,128)(2,1)S(1)} %get-tuple-element.23.r1, ...), custom_call_target="tpu_custom_call", output_to_operand_aliasing={{0}: (7, {})} | custom-call | flops 3000000000 | bytes 4194304 | tf_op jit(solution)/shard_map/pallas_call | solution.py:326
  26.1 0.1 collective-permute-start.6
  26.2 0.0 collective-permute-done.1.lists
  26.2 0.0 collective-permute-done.block
  26.2 0.0 copy-done.1
  26.2 0.1 shard_map.91
  26.3 0.7 %collective-permute-start.4 = (bf16[400,512]{1,0:T(8,128)(2,1)S(1)}, bf16[400,512]{1,0:T(8,128)(2,1)S(1)}, u32[]{:S(2)}, u32[]{:S(2)}) collective-permute-start(bf16[400,512]{1,0:T(8,128)(2,1)S(1)} %get-tuple-element.33), channel_id=1, source_target_pairs={{0,2},{2,0},{4,6},{6,4},{8,10},{10,8},{12,14},{14,12},{16,18},{18,... | collective-permute-start | bytes 1228808 | tf_op jit(solution)/shard_map/ppermute | solution.py:293
  27.0 0.1 collective-permute-start.5
  27.1 3.2 %shard_map.92.part = f32[400,512]{1,0:T(8,128)S(1)} custom-call(bf16[400,2560]{1,0:T(8,128)(2,1)S(1)} %bitcast.19, bf16[400,512]{1,0:T(8,128)(2,1)S(1)} %bitcast.14, bf16[400,512]{1,0:T(8,128)(2,1)S(1)} %get-tuple-element.35.next2, bf16[32,512]{1,0:T(8,128)(2,1)S(1)} %get-tuple-element.36.lists, ...), custom_call_target="tpu_custom_call", output_to_operand_aliasing={{}: (4, {})} | custom-call | flops 10000000000 | bytes 4194304 | tf_op jit(solution)/shard_map/pallas_call | solution.py:334
  30.3 0.0 collective-permute-done.6.other
  30.3 2.5 %collective-permute-start.7 = (f32[8,128]{1,0:T(8,128)S(1)}, f32[8,128]{1,0:T(8,128)S(1)}, u32[]{:S(2)}, u32[]{:S(2)}) collective-permute-start(f32[8,128]{1,0:T(8,128)S(1)} %shard_map.93.row), channel_id=1, source_target_pairs={{0,1},{1,0},{2,3},{3,2},{4,5},{5,4},{6,7},{7,6},{8,9},{9,8},{10,11... | collective-permute-start | bytes 12296 | tf_op jit(solution)/shard_map/ppermute | solution.py:337
  32.9 0.0 collective-permute-done.5.lists
  32.9 0.0 collective-permute-done.4.next1
  32.9 3.2 %shard_map.94.own = bf16[400,512]{1,0:T(8,128)(2,1)S(1)} custom-call(bf16[400,2560]{1,0:T(8,128)(2,1)S(1)} %bitcast.20, bf16[400,512]{1,0:T(8,128)(2,1)S(1)} %bitcast.15, bf16[400,512]{1,0:T(8,128)(2,1)S(1)} %collective-permute-done.4.next1, bf16[32,512]{1,0:T(8,128)(2,1)S(1)} %collective-permute-done.5.lists, f32[400,512]{1,0:T(8,128)S(1)} %shard_map.92.part, ...), custom_call_target="tpu_custom_call" | custom-call | flops 10000000000 | bytes 4194304 | tf_op jit(solution)/shard_map/pallas_call | solution.py:338
  36.0 0.0 collective-permute-done.7.other
  36.0 0.8 %collective-permute-start.8 = (bf16[400,512]{1,0:T(8,128)(2,1)S(1)}, bf16[400,512]{1,0:T(8,128)(2,1)S(1)}, u32[]{:S(2)}, u32[]{:S(2)}) collective-permute-start(bf16[400,512]{1,0:T(8,128)(2,1)S(1)} %get-tuple-element.38.own), channel_id=1, source_target_pairs={{0,1},{1,0},{2,3},{3,2},{4,5},{5,4},{6,7},{7,6},{8,9},{9,8},{10,11... | collective-permute-start | bytes 1228808 | tf_op jit(solution)/shard_map/ppermute | solution.py:344
  36.8 14.7 %all_to_all.11 = f32[64,1,128]{2,1,0:T(1,128)S(1)} all-to-all(f32[64,1,128]{2,1,0:T(1,128)S(1)} %bitcast.17), channel_id=1, replica_groups={{0,4,8,12,16,20,24,28,32,36,40,44,48,52,56,60,64,68,72,76,80,84,88,92,9..., dimensions={0} | all-to-all | bytes 65536 | tf_op jit(solution)/shard_map/all_to_all | solution.py:345
  51.5 0.0 collective-permute-done.8.other
  51.5 1.0 %shard_map.96 = (f32[400,512]{1,0:T(8,128)}, f32[1,1]{1,0:T(1,128)}) custom-call(bf16[400,512]{1,0:T(8,128)(2,1)S(1)} %get-tuple-element.38.own, bf16[400,512]{1,0:T(8,128)(2,1)S(1)} %collective-permute-done.8.other, f32[64,128]{1,0:T(8,128)S(1)} %bitcast.16), custom_call_target="tpu_custom_call" | custom-call | flops 1000000 | bytes 4194304 | tf_op jit(solution)/shard_map/pallas_call | solution.py:347
  (3 shorter events, 0.1 us)
Async XLA Ops:
  0.6 20.1 %collective-permute-start.2 = (bf16[400,512]{1,0:T(8,128)(2,1)}, bf16[400,512]{1,0:T(8,128)(2,1)S(1)}, u32[]{:S(2)}, u32[]{:S(2)}) collective-permute-start(bf16[400,512]{1,0:T(8,128)(2,1)} %bitcast.9), channel_id=1, source_target_pairs={{0,4},{2,6},{4,8},{6,10},{8,12},{10,14},{12,16},{14,18},{16,20},{1... | collective-permute-start | bytes 1228808 | tf_op jit(solution)/shard_map/ppermute | solution.py:289
  2.8 23.4 %collective-permute-start = (bf16[400,512]{1,0:T(8,128)(2,1)}, bf16[400,512]{1,0:T(8,128)(2,1)S(1)}, u32[]{:S(2)}, u32[]{:S(2)}) collective-permute-start(bf16[400,512]{1,0:T(8,128)(2,1)} %bitcast.10), channel_id=1, source_target_pairs={{0,252},{2,254},{4,0},{6,2},{8,4},{10,6},{12,8},{14,10},{16,12},{1... | collective-permute-start | bytes 1228808 | tf_op jit(solution)/shard_map/ppermute | solution.py:289
  10.6 3.1 %copy-start = (bf16[512,400]{0,1:T(8,128)(2,1)S(1)}, bf16[512,400]{0,1:T(8,128)(2,1)}, u32[]{:S(2)}) copy-start(bf16[512,400]{0,1:T(8,128)(2,1)} %param.7) | copy-start | bytes 1228804
  10.6 3.1 %copy-start.2 = (bf16[2560,400]{0,1:T(8,128)(2,1)S(1)}, bf16[2560,400]{0,1:T(8,128)(2,1)}, u32[]{:S(2)}) copy-start(bf16[2560,400]{0,1:T(8,128)(2,1)} %param.8) | copy-start | bytes 6144004
  10.6 3.1 %copy-start.3 = (s32[3,512]{1,0:T(4,128)S(1)}, s32[3,512]{1,0:T(4,128)}, u32[]{:S(2)}) copy-start(s32[3,512]{1,0:T(4,128)} %rels.1) | copy-start | bytes 18436
  10.6 3.1 %copy-start.4 = (s32[3,512]{1,0:T(4,128)S(1)}, s32[3,512]{1,0:T(4,128)}, u32[]{:S(2)}) copy-start(s32[3,512]{1,0:T(4,128)} %heads.5) | copy-start | bytes 18436
  10.6 3.1 %copy-start.5 = (s32[3,512]{1,0:T(4,128)S(1)}, s32[3,512]{1,0:T(4,128)}, u32[]{:S(2)}) copy-start(s32[3,512]{1,0:T(4,128)} %tails.5) | copy-start | bytes 18436
  10.6 3.1 %copy-start.6 = (s32[3,2,256]{2,1,0:T(2,128)S(1)}, s32[3,2,256]{2,1,0:T(2,128)}, u32[]{:S(2)}) copy-start(s32[3,2,256]{2,1,0:T(2,128)} %negatives.1) | copy-start | bytes 18436
  10.6 3.1 %copy-start.7 = (s32[3,1]{0,1:T(1,128)S(1)}, s32[3,1]{0,1:T(1,128)}, u32[]{:S(2)}) copy-start(s32[3,1]{0,1:T(1,128)} %param.13) | copy-start | bytes 40
  12.2 14.0 %collective-permute-start.1 = (bf16[32,512]{1,0:T(8,128)(2,1)}, bf16[32,512]{1,0:T(8,128)(2,1)S(1)}, u32[]{:S(2)}, u32[]{:S(2)}) collective-permute-start(bf16[32,512]{1,0:T(8,128)(2,1)} %shard_map.86.own_lists), channel_id=1, source_target_pairs={{0,252},{2,254},{4,0},{6,2},{8,4},{10,6},{12,8},{14,10},{16,12},{1... | collective-permute-start | bytes 98312 | tf_op jit(solution)/shard_map/ppermute | solution.py:289
  20.8 3.4 %collective-permute-start.3 = (bf16[400,512]{1,0:T(8,128)(2,1)S(1)}, bf16[400,512]{1,0:T(8,128)(2,1)S(1)}, u32[]{:S(2)}, u32[]{:S(2)}) collective-permute-start(bf16[400,512]{1,0:T(8,128)(2,1)S(1)} %shard_map.87), channel_id=1, source_target_pairs={{0,2},{2,0},{4,6},{6,4},{8,10},{10,8},{12,14},{14,12},{16,18},{18,... | collective-permute-start | bytes 1228808 | tf_op jit(solution)/shard_map/ppermute | solution.py:293
  24.3 2.0 %copy-start.1 = (bf16[32,512]{1,0:T(8,128)(2,1)S(1)}, bf16[32,512]{1,0:T(8,128)(2,1)}, u32[]{:S(2)}) copy-start(bf16[32,512]{1,0:T(8,128)(2,1)} %shard_map.86.own_lists) | copy-start | bytes 98308
  26.1 4.2 %collective-permute-start.6 = (f32[8,128]{1,0:T(8,128)S(1)}, f32[8,128]{1,0:T(8,128)S(1)}, u32[]{:S(2)}, u32[]{:S(2)}) collective-permute-start(f32[8,128]{1,0:T(8,128)S(1)} %get-tuple-element.32.row), channel_id=1, source_target_pairs={{0,2},{2,0},{4,6},{6,4},{8,10},{10,8},{12,14},{14,12},{16,18},{18,... | collective-permute-start | bytes 12296 | tf_op jit(solution)/shard_map/ppermute | solution.py:293
  26.3 6.6 %collective-permute-start.4 = (bf16[400,512]{1,0:T(8,128)(2,1)S(1)}, bf16[400,512]{1,0:T(8,128)(2,1)S(1)}, u32[]{:S(2)}, u32[]{:S(2)}) collective-permute-start(bf16[400,512]{1,0:T(8,128)(2,1)S(1)} %get-tuple-element.33), channel_id=1, source_target_pairs={{0,2},{2,0},{4,6},{6,4},{8,10},{10,8},{12,14},{14,12},{16,18},{18,... | collective-permute-start | bytes 1228808 | tf_op jit(solution)/shard_map/ppermute | solution.py:293
  27.0 5.8 %collective-permute-start.5 = (bf16[32,512]{1,0:T(8,128)(2,1)S(1)}, bf16[32,512]{1,0:T(8,128)(2,1)S(1)}, u32[]{:S(2)}, u32[]{:S(2)}) collective-permute-start(bf16[32,512]{1,0:T(8,128)(2,1)S(1)} %get-tuple-element.34), channel_id=1, source_target_pairs={{0,2},{2,0},{4,6},{6,4},{8,10},{10,8},{12,14},{14,12},{16,18},{18,... | collective-permute-start | bytes 98312 | tf_op jit(solution)/shard_map/ppermute | solution.py:293
  30.3 5.7 %collective-permute-start.7 = (f32[8,128]{1,0:T(8,128)S(1)}, f32[8,128]{1,0:T(8,128)S(1)}, u32[]{:S(2)}, u32[]{:S(2)}) collective-permute-start(f32[8,128]{1,0:T(8,128)S(1)} %shard_map.93.row), channel_id=1, source_target_pairs={{0,1},{1,0},{2,3},{3,2},{4,5},{5,4},{6,7},{7,6},{8,9},{9,8},{10,11... | collective-permute-start | bytes 12296 | tf_op jit(solution)/shard_map/ppermute | solution.py:337
  36.0 15.5 %collective-permute-start.8 = (bf16[400,512]{1,0:T(8,128)(2,1)S(1)}, bf16[400,512]{1,0:T(8,128)(2,1)S(1)}, u32[]{:S(2)}, u32[]{:S(2)}) collective-permute-start(bf16[400,512]{1,0:T(8,128)(2,1)S(1)} %get-tuple-element.38.own), channel_id=1, source_target_pairs={{0,1},{1,0},{2,3},{3,2},{4,5},{5,4},{6,7},{7,6},{8,9},{9,8},{10,11... | collective-permute-start | bytes 1228808 | tf_op jit(solution)/shard_map/ppermute | solution.py:344

commit v7 on v6

--- a/solution.py
+++ b/solution.py
@@ -334,16 +334,16 @@
     (part,) = kernel(tails2_kernel, [(grads, F32)], [hot] + work + [(logs, F32)], 10 * 10**9, [here] * 5, aliases={4: 0})(
         rel, emb, next2, next2_lists, part)
     (row,) = kernel(add_kernel, [(rows_of, F32)], [], 10**6, [here] * 2)(row, core_row)
-    rep_row = lax.ppermute(row, "rep", [(0, 1), (1, 0)])
+    half_row = shifted(row, blocks // 2)
     (own,) = kernel(
         tails1_kernel, [(grads, BF16)],
         [hot] + work + [(grads, F32), (logs, F32)], 10 * 10**9, [here] * 6,
     )(rel, emb, next1, lists1, part, row)
     own, rows = kernel(rows_kernel, [(grads, BF16), ((blocks // 2, 128), F32)], [], 10**6, [here] * 3, aliases={0: 0})(
-        own, row, rep_row)
+        own, row, half_row)
     other = lax.ppermute(own, "rep", [(0, 1), (1, 0)])
-    rows = lax.all_to_all(rows, "blk", 0, 0, tiled=True,
-                          axis_index_groups=[[k + 2 * i for i in range(blocks // 2)] for k in (0, 1)])
+    rows = lax.all_to_all(rows, ("blk", "rep"), 0, 0, tiled=True, axis_index_groups=[
+        [h * blocks + 4 * i + 2 * k + r for i in range(blocks // 4) for r in (0, 1)] for h in (0, 1) for k in (0, 1)])
     grad, mean = kernel(finish_kernel, [(grads, F32), ((1, 1), F32)], [], 10**6, [here] * 3)(own, other, rows)
     return grad.T, mean[0, 0]
 

time: 53.3 us -> 54.1 us (1.015); the launches traced: 52.6 us -> 54 us
  blocking collectives: 14.7 us -> 16.2 us
    ppermute x1 -> x0, starting transfers between devices: 2.53 us -> none  [per_device(): rep_row = lax.ppermute(row, 'rep', [(0, 1), (1, 0)])]
    ppermute x1, starting transfers between devices: 0.78 us -> 2.83 us  [per_device(): other = lax.ppermute(own, 'rep', [(0, 1), (1, 0)])]
    all_to_all x1, blocking collectives: 14.7 us -> 16.2 us  [per_device(): lax.all_to_all(rows, ('blk', 'rep'), 0, 0, tiled=True, axis_index_groups=...]
    ppermute x3 -> x4, starting transfers between devices: 11.4 us -> 11.7 us  [shifted(): return lax.ppermute(x, 'blk', [(i, (i + by) % peers) for i in range(peers)])]
  transfers between devices with their start and end apart: 9 -> 9, of which waited for: 0 -> 0; matrix products, arithmetic and copies ran while one was open for 0% -> 0% of each run, Pallas kernels for 36% -> 35%
where the time goes in v7:
time: 54.1 us; the launch traced here: 54 us
  Pallas kernels  19.7 us (36%)
  starting transfers between devices  17.1 us (32%)
  blocking collectives  16.2 us (30%)
  between operations  0.83 us (2%)
    all_to_all x1, blocking collectives, per_device(): lax.all_to_all(rows, ('blk', 'rep'), 0, 0, tiled=True, axis_index_groups=...  16.2 us
    ppermute x4, starting transfers between devices, shifted(): return lax.ppermute(x, 'blk', [(i, (i + by) % peers) for i in range(peers)])  11.7 us
    pallas_call x1, Pallas kernels, per_device(): kernel(prepare_kernel, [(grads, F32), ((8, edges), F32)] + [(big, BF16)]...  7.01 us
    pallas_call x1, Pallas kernels, per_device(): kernel(tails2_kernel, [(grads, F32)], [hot] + work + [(logs, F32)], 10 *...  3.16 us
    pallas_call x1, Pallas kernels, per_device(): kernel(tails1_kernel, [(grads, BF16)], [hot] + work + [(grads, F32), (log...  3.16 us
    ppermute x1, starting transfers between devices, per_device(): other = lax.ppermute(own, 'rep', [(0, 1), (1, 0)])  2.83 us
    ppermute x4, starting transfers between devices, exchanged(): lax.ppermute(x, 'blk', [(i, i ^ 1) for i in range(lax.axis_size('blk'))])  2.55 us
    pallas_call x1, Pallas kernels, per_device(): kernel(heads1_kernel, [(grads, F32), (rows_of, F32)], work, 3 * 10 ** 9,...  1.82 us
  transfers between devices with their start and end apart: 9, of which 0 were waited for; matrix products, arithmetic and copies ran while one was open for 0% of the time, Pallas kernels for 35%

profile of v7, /device:TPU:1, one launch (start us, length us, event | category | flops | bytes accessed | tf_op | source)
XLA Modules:
  0.0 54.0 jit_solution(1973562847408264943)
XLA Ops:
  0.6 2.2 %collective-permute-start.2 = (bf16[400,512]{1,0:T(8,128)(2,1)}, bf16[400,512]{1,0:T(8,128)(2,1)S(1)}, u32[]{:S(2)}, u32[]{:S(2)}) collective-permute-start(bf16[400,512]{1,0:T(8,128)(2,1)} %bitcast.9), channel_id=1, source_target_pairs={{0,4},{2,6},{4,8},{6,10},{8,12},{10,14},{12,16},{14,18},{16,20},{1... | collective-permute-start | bytes 1228808 | tf_op jit(solution)/shard_map/ppermute | solution.py:289
  2.8 7.7 %collective-permute-start = (bf16[400,512]{1,0:T(8,128)(2,1)}, bf16[400,512]{1,0:T(8,128)(2,1)S(1)}, u32[]{:S(2)}, u32[]{:S(2)}) collective-permute-start(bf16[400,512]{1,0:T(8,128)(2,1)} %bitcast.10), channel_id=1, source_target_pairs={{0,252},{2,254},{4,0},{6,2},{8,4},{10,6},{12,8},{14,10},{16,12},{1... | collective-permute-start | bytes 1228808 | tf_op jit(solution)/shard_map/ppermute | solution.py:289
  10.6 0.0 copy-start
  10.6 0.0 copy-start.2
  10.6 0.0 copy-start.3
  10.6 0.0 copy-start.4
  10.6 0.0 copy-start.5
  10.6 0.0 copy-start.6
  10.6 0.0 copy-start.7
  10.6 1.6 %shard_map.86.own_lists = bf16[32,512]{1,0:T(8,128)(2,1)} custom-call(s32[3,512]{1,0:T(4,128)} %heads.5, s32[3,512]{1,0:T(4,128)} %tails.5, s32[3,512]{1,0:T(4,128)} %rels.1, s32[3,2,256]{2,1,0:T(2,128)} %negatives.1, s32[1,3]{1,0:T(1,128)} %bitcast.21), custom_call_target="tpu_custom_call" | custom-call | flops 2000000000 | bytes 4194304 | tf_op jit(solution)/shard_map/pallas_call | solution.py:311
  12.2 1.5 %collective-permute-start.1 = (bf16[32,512]{1,0:T(8,128)(2,1)}, bf16[32,512]{1,0:T(8,128)(2,1)S(1)}, u32[]{:S(2)}, u32[]{:S(2)}) collective-permute-start(bf16[32,512]{1,0:T(8,128)(2,1)} %shard_map.86.own_lists), channel_id=1, source_target_pairs={{0,252},{2,254},{4,0},{6,2},{8,4},{10,6},{12,8},{14,10},{16,12},{1... | collective-permute-start | bytes 98312 | tf_op jit(solution)/shard_map/ppermute | solution.py:289
  13.7 0.0 copy-done
  13.7 0.0 copy-done.2
  13.7 0.0 copy-done.3
  13.7 0.0 copy-done.4
  13.7 0.0 copy-done.5
  13.7 0.0 copy-done.6
  13.7 0.0 copy-done.7
  13.7 7.0 %shard_map.88 = (f32[400,512]{1,0:T(8,128)S(1)}, f32[8,512]{1,0:T(8,128)S(1)}, bf16[400,512]{1,0:T(8,128)(2,1)S(1)}, bf16[400,512]{1,0:T(8,128)(2,1)S(1)}, bf16[...) custom-call(bf16[400,512]{1,0:T(8,128)(2,1)S(1)} %bitcast.11, ...), custom_call_target="tpu_custom_call" | custom-call | flops 20000000000 | bytes 4194304 | tf_op jit(solution)/shard_map/pallas_call | solution.py:317
  20.8 0.0 collective-permute-done.2.prev2
  20.8 1.6 %collective-permute-start.3 = (bf16[400,512]{1,0:T(8,128)(2,1)S(1)}, bf16[400,512]{1,0:T(8,128)(2,1)S(1)}, u32[]{:S(2)}, u32[]{:S(2)}) collective-permute-start(bf16[400,512]{1,0:T(8,128)(2,1)S(1)} %shard_map.87), channel_id=1, source_target_pairs={{0,2},{2,0},{4,6},{6,4},{8,10},{10,8},{12,14},{14,12},{16,18},{18,... | collective-permute-start | bytes 1228808 | tf_op jit(solution)/shard_map/ppermute | solution.py:293
  22.4 1.8 %shard_map.89 = (f32[400,512]{1,0:T(8,128)S(1)}, f32[8,512]{1,0:T(8,128)S(1)}) custom-call(bf16[400,512]{1,0:T(8,128)(2,1)S(1)} %collective-permute-done.2.prev2, bf16[400,512]{1,0:T(8,128)(2,1)S(1)} %get-tuple-element.25.q2, bf16[400,512]{1,0:T(8,128)(2,1)S(1)} %get-tuple-element.26.r2, ...), custom_call_target="tpu_custom_call", output_to_operand_aliasing={{0}: (7, {})} | custom-call | flops 8000000000 | bytes 4194304 | tf_op jit(solution)/shard_map/pallas_call | solution.py:324
  24.2 0.0 collective-permute-done.3.prev1
  24.3 0.0 copy-start.1
  24.3 1.8 %shard_map.90 = (f32[400,512]{1,0:T(8,128)S(1)}, f32[8,128]{1,0:T(8,128)S(1)}) custom-call(bf16[400,512]{1,0:T(8,128)(2,1)S(1)} %collective-permute-done.3.prev1, bf16[400,512]{1,0:T(8,128)(2,1)S(1)} %get-tuple-element.22.q1, bf16[400,512]{1,0:T(8,128)(2,1)S(1)} %get-tuple-element.23.r1, ...), custom_call_target="tpu_custom_call", output_to_operand_aliasing={{0}: (7, {})} | custom-call | flops 3000000000 | bytes 4194304 | tf_op jit(solution)/shard_map/pallas_call | solution.py:326
  26.1 0.1 collective-permute-start.6
  26.2 0.0 collective-permute-done.1.lists
  26.2 0.0 collective-permute-done.block
  26.2 0.0 copy-done.1
  26.2 0.1 shard_map.91
  26.3 0.7 %collective-permute-start.4 = (bf16[400,512]{1,0:T(8,128)(2,1)S(1)}, bf16[400,512]{1,0:T(8,128)(2,1)S(1)}, u32[]{:S(2)}, u32[]{:S(2)}) collective-permute-start(bf16[400,512]{1,0:T(8,128)(2,1)S(1)} %get-tuple-element.33), channel_id=1, source_target_pairs={{0,2},{2,0},{4,6},{6,4},{8,10},{10,8},{12,14},{14,12},{16,18},{18,... | collective-permute-start | bytes 1228808 | tf_op jit(solution)/shard_map/ppermute | solution.py:293
  27.0 0.1 collective-permute-start.5
  27.1 3.2 %shard_map.92.part = f32[400,512]{1,0:T(8,128)S(1)} custom-call(bf16[400,2560]{1,0:T(8,128)(2,1)S(1)} %bitcast.19, bf16[400,512]{1,0:T(8,128)(2,1)S(1)} %bitcast.14, bf16[400,512]{1,0:T(8,128)(2,1)S(1)} %get-tuple-element.35.next2, bf16[32,512]{1,0:T(8,128)(2,1)S(1)} %get-tuple-element.36.lists, ...), custom_call_target="tpu_custom_call", output_to_operand_aliasing={{}: (4, {})} | custom-call | flops 10000000000 | bytes 4194304 | tf_op jit(solution)/shard_map/pallas_call | solution.py:334
  30.3 0.0 collective-permute-done.6.other
  30.3 0.3 collective-permute-start.7
  30.7 0.0 collective-permute-done.5.lists
  30.7 0.0 collective-permute-done.4.next1
  30.7 3.2 %shard_map.94.own = bf16[400,512]{1,0:T(8,128)(2,1)S(1)} custom-call(bf16[400,2560]{1,0:T(8,128)(2,1)S(1)} %bitcast.20, bf16[400,512]{1,0:T(8,128)(2,1)S(1)} %bitcast.15, bf16[400,512]{1,0:T(8,128)(2,1)S(1)} %collective-permute-done.4.next1, bf16[32,512]{1,0:T(8,128)(2,1)S(1)} %collective-permute-done.5.lists, f32[400,512]{1,0:T(8,128)S(1)} %shard_map.92.part, ...), custom_call_target="tpu_custom_call" | custom-call | flops 10000000000 | bytes 4194304 | tf_op jit(solution)/shard_map/pallas_call | solution.py:338
  33.8 0.0 collective-permute-done.7.other
  33.9 2.8 %collective-permute-start.8 = (bf16[400,512]{1,0:T(8,128)(2,1)S(1)}, bf16[400,512]{1,0:T(8,128)(2,1)S(1)}, u32[]{:S(2)}, u32[]{:S(2)}) collective-permute-start(bf16[400,512]{1,0:T(8,128)(2,1)S(1)} %get-tuple-element.38.own), channel_id=1, source_target_pairs={{0,1},{1,0},{2,3},{3,2},{4,5},{5,4},{6,7},{7,6},{8,9},{9,8},{10,11... | collective-permute-start | bytes 1228808 | tf_op jit(solution)/shard_map/ppermute | solution.py:344
  36.7 16.2 %all_to_all.11 = f32[64,1,128]{2,1,0:T(1,128)S(1)} all-to-all(f32[64,1,128]{2,1,0:T(1,128)S(1)} %bitcast.17), channel_id=1, replica_groups={{0,1,4,5,8,9,12,13,16,17,20,21,24,25,28,29,32,33,36,37,40,41,44,45,48,4..., dimensions={0} | all-to-all | bytes 65536 | tf_op jit(solution)/shard_map/all_to_all | solution.py:345
  52.9 0.0 collective-permute-done.8.other
  52.9 1.0 %shard_map.96 = (f32[400,512]{1,0:T(8,128)}, f32[1,1]{1,0:T(1,128)}) custom-call(bf16[400,512]{1,0:T(8,128)(2,1)S(1)} %get-tuple-element.38.own, bf16[400,512]{1,0:T(8,128)(2,1)S(1)} %collective-permute-done.8.other, f32[64,128]{1,0:T(8,128)S(1)} %bitcast.16), custom_call_target="tpu_custom_call" | custom-call | flops 1000000 | bytes 4194304 | tf_op jit(solution)/shard_map/pallas_call | solution.py:347
  (3 shorter events, 0.1 us)
Async XLA Ops:
  0.6 20.1 %collective-permute-start.2 = (bf16[400,512]{1,0:T(8,128)(2,1)}, bf16[400,512]{1,0:T(8,128)(2,1)S(1)}, u32[]{:S(2)}, u32[]{:S(2)}) collective-permute-start(bf16[400,512]{1,0:T(8,128)(2,1)} %bitcast.9), channel_id=1, source_target_pairs={{0,4},{2,6},{4,8},{6,10},{8,12},{10,14},{12,16},{14,18},{16,20},{1... | collective-permute-start | bytes 1228808 | tf_op jit(solution)/shard_map/ppermute | solution.py:289
  2.8 23.4 %collective-permute-start = (bf16[400,512]{1,0:T(8,128)(2,1)}, bf16[400,512]{1,0:T(8,128)(2,1)S(1)}, u32[]{:S(2)}, u32[]{:S(2)}) collective-permute-start(bf16[400,512]{1,0:T(8,128)(2,1)} %bitcast.10), channel_id=1, source_target_pairs={{0,252},{2,254},{4,0},{6,2},{8,4},{10,6},{12,8},{14,10},{16,12},{1... | collective-permute-start | bytes 1228808 | tf_op jit(solution)/shard_map/ppermute | solution.py:289
  10.6 3.1 %copy-start = (bf16[512,400]{0,1:T(8,128)(2,1)S(1)}, bf16[512,400]{0,1:T(8,128)(2,1)}, u32[]{:S(2)}) copy-start(bf16[512,400]{0,1:T(8,128)(2,1)} %param.7) | copy-start | bytes 1228804
  10.6 3.1 %copy-start.2 = (bf16[2560,400]{0,1:T(8,128)(2,1)S(1)}, bf16[2560,400]{0,1:T(8,128)(2,1)}, u32[]{:S(2)}) copy-start(bf16[2560,400]{0,1:T(8,128)(2,1)} %param.8) | copy-start | bytes 6144004
  10.6 3.1 %copy-start.3 = (s32[3,512]{1,0:T(4,128)S(1)}, s32[3,512]{1,0:T(4,128)}, u32[]{:S(2)}) copy-start(s32[3,512]{1,0:T(4,128)} %rels.1) | copy-start | bytes 18436
  10.6 3.1 %copy-start.4 = (s32[3,512]{1,0:T(4,128)S(1)}, s32[3,512]{1,0:T(4,128)}, u32[]{:S(2)}) copy-start(s32[3,512]{1,0:T(4,128)} %heads.5) | copy-start | bytes 18436
  10.6 3.1 %copy-start.5 = (s32[3,512]{1,0:T(4,128)S(1)}, s32[3,512]{1,0:T(4,128)}, u32[]{:S(2)}) copy-start(s32[3,512]{1,0:T(4,128)} %tails.5) | copy-start | bytes 18436
  10.6 3.1 %copy-start.6 = (s32[3,2,256]{2,1,0:T(2,128)S(1)}, s32[3,2,256]{2,1,0:T(2,128)}, u32[]{:S(2)}) copy-start(s32[3,2,256]{2,1,0:T(2,128)} %negatives.1) | copy-start | bytes 18436
  10.6 3.1 %copy-start.7 = (s32[3,1]{0,1:T(1,128)S(1)}, s32[3,1]{0,1:T(1,128)}, u32[]{:S(2)}) copy-start(s32[3,1]{0,1:T(1,128)} %param.13) | copy-start | bytes 40
  12.2 14.0 %collective-permute-start.1 = (bf16[32,512]{1,0:T(8,128)(2,1)}, bf16[32,512]{1,0:T(8,128)(2,1)S(1)}, u32[]{:S(2)}, u32[]{:S(2)}) collective-permute-start(bf16[32,512]{1,0:T(8,128)(2,1)} %shard_map.86.own_lists), channel_id=1, source_target_pairs={{0,252},{2,254},{4,0},{6,2},{8,4},{10,6},{12,8},{14,10},{16,12},{1... | collective-permute-start | bytes 98312 | tf_op jit(solution)/shard_map/ppermute | solution.py:289
  20.8 3.4 %collective-permute-start.3 = (bf16[400,512]{1,0:T(8,128)(2,1)S(1)}, bf16[400,512]{1,0:T(8,128)(2,1)S(1)}, u32[]{:S(2)}, u32[]{:S(2)}) collective-permute-start(bf16[400,512]{1,0:T(8,128)(2,1)S(1)} %shard_map.87), channel_id=1, source_target_pairs={{0,2},{2,0},{4,6},{6,4},{8,10},{10,8},{12,14},{14,12},{16,18},{18,... | collective-permute-start | bytes 1228808 | tf_op jit(solution)/shard_map/ppermute | solution.py:293
  24.3 2.0 %copy-start.1 = (bf16[32,512]{1,0:T(8,128)(2,1)S(1)}, bf16[32,512]{1,0:T(8,128)(2,1)}, u32[]{:S(2)}) copy-start(bf16[32,512]{1,0:T(8,128)(2,1)} %shard_map.86.own_lists) | copy-start | bytes 98308
  26.1 4.2 %collective-permute-start.6 = (f32[8,128]{1,0:T(8,128)S(1)}, f32[8,128]{1,0:T(8,128)S(1)}, u32[]{:S(2)}, u32[]{:S(2)}) collective-permute-start(f32[8,128]{1,0:T(8,128)S(1)} %get-tuple-element.32.row), channel_id=1, source_target_pairs={{0,2},{2,0},{4,6},{6,4},{8,10},{10,8},{12,14},{14,12},{16,18},{18,... | collective-permute-start | bytes 12296 | tf_op jit(solution)/shard_map/ppermute | solution.py:293
  26.3 4.4 %collective-permute-start.4 = (bf16[400,512]{1,0:T(8,128)(2,1)S(1)}, bf16[400,512]{1,0:T(8,128)(2,1)S(1)}, u32[]{:S(2)}, u32[]{:S(2)}) collective-permute-start(bf16[400,512]{1,0:T(8,128)(2,1)S(1)} %get-tuple-element.33), channel_id=1, source_target_pairs={{0,2},{2,0},{4,6},{6,4},{8,10},{10,8},{12,14},{14,12},{16,18},{18,... | collective-permute-start | bytes 1228808 | tf_op jit(solution)/shard_map/ppermute | solution.py:293
  27.0 3.6 %collective-permute-start.5 = (bf16[32,512]{1,0:T(8,128)(2,1)S(1)}, bf16[32,512]{1,0:T(8,128)(2,1)S(1)}, u32[]{:S(2)}, u32[]{:S(2)}) collective-permute-start(bf16[32,512]{1,0:T(8,128)(2,1)S(1)} %get-tuple-element.34), channel_id=1, source_target_pairs={{0,2},{2,0},{4,6},{6,4},{8,10},{10,8},{12,14},{14,12},{16,18},{18,... | collective-permute-start | bytes 98312 | tf_op jit(solution)/shard_map/ppermute | solution.py:293
  30.3 3.5 %collective-permute-start.7 = (f32[8,128]{1,0:T(8,128)S(1)}, f32[8,128]{1,0:T(8,128)S(1)}, u32[]{:S(2)}, u32[]{:S(2)}) collective-permute-start(f32[8,128]{1,0:T(8,128)S(1)} %shard_map.93.row), channel_id=1, source_target_pairs={{0,128},{2,130},{4,132},{6,134},{8,136},{10,138},{12,140},{14,142}... | collective-permute-start | bytes 12296 | tf_op jit(solution)/shard_map/ppermute | solution.py:289
  33.9 19.1 %collective-permute-start.8 = (bf16[400,512]{1,0:T(8,128)(2,1)S(1)}, bf16[400,512]{1,0:T(8,128)(2,1)S(1)}, u32[]{:S(2)}, u32[]{:S(2)}) collective-permute-start(bf16[400,512]{1,0:T(8,128)(2,1)S(1)} %get-tuple-element.38.own), channel_id=1, source_target_pairs={{0,1},{1,0},{2,3},{3,2},{4,5},{5,4},{6,7},{7,6},{8,9},{9,8},{10,11... | collective-permute-start | bytes 1228808 | tf_op jit(solution)/shard_map/ppermute | solution.py:344

commit v8 on v6

--- a/solution.py
+++ b/solution.py
@@ -210,7 +210,7 @@
     log_counts(halves(unpacked(lists, NEGS, step)), log_out.shape[0], log_out)
 
 
-def tail_bucket(step, emb, head, lists, rf, log, acc, hf, qf, sf, qq):
+def tail_bucket(step, emb, head, lists, rf, log, hf, qf, sf, qq):
     entities, edges = emb.shape[1], lists.shape[1]
     hf[...] = dot(head[...], one_hot(unpacked(lists, HEADS, step), entities), NN)
     make_query(hf, rf, qf)
@@ -219,7 +219,7 @@
     loss, miss = softmax_terms(sf, log, unpacked(lists, TAILS, step), qq)
     scale = miss * live_row(live_counts(lists, step), edges) * (1.0 / 256.0)
     high, low = split(q.astype(F32) * scale)
-    acc[...] += dot(high, qq[...], NT) + dot(low, qq[...], NT)
+    return dot(high, qq[...], NT) + dot(low, qq[...], NT)
 
 
 def heads2_kernel(prev2, q2, r2, log2, heads, tails, live_groups, part, sums, grad, sums_out, hf, rf, qf, sf, qq):
@@ -248,14 +248,13 @@
 
 def tails2_kernel(rel, emb, next2, lists, part, grad, hot, hf, rf, qf, sf, qq, log):
     far_terms(2, rel, lists, rf, log, hot)
-    tail_bucket(2, emb, next2, lists, rf, log, grad, hf, qf, sf, qq)
-
-
-def tails1_kernel(rel, emb, next1, lists, part, row, grad, hot, hf, rf, qf, sf, qq, acc, log):
-    acc[...] = part[...]
+    grad[...] += tail_bucket(2, emb, next2, lists, rf, log, hf, qf, sf, qq)
+
+
+def tails1_kernel(rel, emb, next1, lists, part, row, grad, hot, hf, rf, qf, sf, qq, log):
     far_terms(1, rel, lists, rf, log, hot)
-    tail_bucket(1, emb, next1, lists, rf, log, acc, hf, qf, sf, qq)
-    grad[...] = acc[...].astype(BF16)
+    own = tail_bucket(1, emb, next1, lists, rf, log, hf, qf, sf, qq)
+    grad[...] = (part[...] + own).astype(BF16)
 
 
 def add_kernel(row, other, out):
@@ -337,7 +336,7 @@
     rep_row = lax.ppermute(row, "rep", [(0, 1), (1, 0)])
     (own,) = kernel(
         tails1_kernel, [(grads, BF16)],
-        [hot] + work + [(grads, F32), (logs, F32)], 10 * 10**9, [here] * 6,
+        [hot] + work + [(logs, F32)], 10 * 10**9, [here] * 6,
     )(rel, emb, next1, lists1, part, row)
     own, rows = kernel(rows_kernel, [(grads, BF16), ((blocks // 2, 128), F32)], [], 10**6, [here] * 3, aliases={0: 0})(
         own, row, rep_row)

time: 53.3 us -> 53.3 us (level)
  no operation moved by 1% of the time
where the time goes in v8:
time: 53.3 us; the launch traced here: 52.6 us
  Pallas kernels  19.7 us (37%)
  starting transfers between devices  17.3 us (32%)
  blocking collectives  14.7 us (28%)
  between operations  0.83 us (2%)
    all_to_all x1, blocking collectives, per_device(): lax.all_to_all(rows, 'blk', 0, 0, tiled=True, axis_index_groups=[[k + 2 *...  14.7 us
    ppermute x3, starting transfers between devices, shifted(): return lax.ppermute(x, 'blk', [(i, (i + by) % peers) for i in range(peers)])  11.4 us
    pallas_call x1, Pallas kernels, per_device(): kernel(prepare_kernel, [(grads, F32), ((8, edges), F32)] + [(big, BF16)]...  7.01 us
    pallas_call x1, Pallas kernels, per_device(): kernel(tails2_kernel, [(grads, F32)], [hot] + work + [(logs, F32)], 10 *...  3.16 us
    pallas_call x1, Pallas kernels, per_device(): kernel(tails1_kernel, [(grads, BF16)], [hot] + work + [(logs, F32)], 10 *...  3.15 us
    ppermute x4, starting transfers between devices, exchanged(): lax.ppermute(x, 'blk', [(i, i ^ 1) for i in range(lax.axis_size('blk'))])  2.55 us
    ppermute x1, starting transfers between devices, per_device(): rep_row = lax.ppermute(row, 'rep', [(0, 1), (1, 0)])  2.53 us
    pallas_call x1, Pallas kernels, per_device(): kernel(heads1_kernel, [(grads, F32), (rows_of, F32)], work, 3 * 10 ** 9,...  1.82 us
  transfers between devices with their start and end apart: 9, of which 0 were waited for; matrix products, arithmetic and copies ran while one was open for 0% of the time, Pallas kernels for 36%

profile of v8, /device:TPU:1, one launch (start us, length us, event | category | flops | bytes accessed | tf_op | source)
XLA Modules:
  0.0 52.6 jit_solution(7077527788501376275)
XLA Ops:
  0.6 2.2 %collective-permute-start.2 = (bf16[400,512]{1,0:T(8,128)(2,1)}, bf16[400,512]{1,0:T(8,128)(2,1)S(1)}, u32[]{:S(2)}, u32[]{:S(2)}) collective-permute-start(bf16[400,512]{1,0:T(8,128)(2,1)} %bitcast.9), channel_id=1, source_target_pairs={{0,4},{2,6},{4,8},{6,10},{8,12},{10,14},{12,16},{14,18},{16,20},{1... | collective-permute-start | bytes 1228808 | tf_op jit(solution)/shard_map/ppermute | solution.py:288
  2.8 7.7 %collective-permute-start = (bf16[400,512]{1,0:T(8,128)(2,1)}, bf16[400,512]{1,0:T(8,128)(2,1)S(1)}, u32[]{:S(2)}, u32[]{:S(2)}) collective-permute-start(bf16[400,512]{1,0:T(8,128)(2,1)} %bitcast.10), channel_id=1, source_target_pairs={{0,252},{2,254},{4,0},{6,2},{8,4},{10,6},{12,8},{14,10},{16,12},{1... | collective-permute-start | bytes 1228808 | tf_op jit(solution)/shard_map/ppermute | solution.py:288
  10.6 0.0 copy-start
  10.6 0.0 copy-start.2
  10.6 0.0 copy-start.3
  10.6 0.0 copy-start.4
  10.6 0.0 copy-start.5
  10.6 0.0 copy-start.6
  10.6 0.0 copy-start.7
  10.6 1.6 %shard_map.86.own_lists = bf16[32,512]{1,0:T(8,128)(2,1)} custom-call(s32[3,512]{1,0:T(4,128)} %heads.5, s32[3,512]{1,0:T(4,128)} %tails.5, s32[3,512]{1,0:T(4,128)} %rels.1, s32[3,2,256]{2,1,0:T(2,128)} %negatives.1, s32[1,3]{1,0:T(1,128)} %bitcast.21), custom_call_target="tpu_custom_call" | custom-call | flops 2000000000 | bytes 4194304 | tf_op jit(solution)/shard_map/pallas_call | solution.py:310
  12.2 1.5 %collective-permute-start.1 = (bf16[32,512]{1,0:T(8,128)(2,1)}, bf16[32,512]{1,0:T(8,128)(2,1)S(1)}, u32[]{:S(2)}, u32[]{:S(2)}) collective-permute-start(bf16[32,512]{1,0:T(8,128)(2,1)} %shard_map.86.own_lists), channel_id=1, source_target_pairs={{0,252},{2,254},{4,0},{6,2},{8,4},{10,6},{12,8},{14,10},{16,12},{1... | collective-permute-start | bytes 98312 | tf_op jit(solution)/shard_map/ppermute | solution.py:288
  13.7 0.0 copy-done
  13.7 0.0 copy-done.2
  13.7 0.0 copy-done.3
  13.7 0.0 copy-done.4
  13.7 0.0 copy-done.5
  13.7 0.0 copy-done.6
  13.7 0.0 copy-done.7
  13.7 7.0 %shard_map.88 = (f32[400,512]{1,0:T(8,128)S(1)}, f32[8,512]{1,0:T(8,128)S(1)}, bf16[400,512]{1,0:T(8,128)(2,1)S(1)}, bf16[400,512]{1,0:T(8,128)(2,1)S(1)}, bf16[...) custom-call(bf16[400,512]{1,0:T(8,128)(2,1)S(1)} %bitcast.11, ...), custom_call_target="tpu_custom_call" | custom-call | flops 20000000000 | bytes 4194304 | tf_op jit(solution)/shard_map/pallas_call | solution.py:316
  20.8 0.0 collective-permute-done.2.prev2
  20.8 1.6 %collective-permute-start.3 = (bf16[400,512]{1,0:T(8,128)(2,1)S(1)}, bf16[400,512]{1,0:T(8,128)(2,1)S(1)}, u32[]{:S(2)}, u32[]{:S(2)}) collective-permute-start(bf16[400,512]{1,0:T(8,128)(2,1)S(1)} %shard_map.87), channel_id=1, source_target_pairs={{0,2},{2,0},{4,6},{6,4},{8,10},{10,8},{12,14},{14,12},{16,18},{18,... | collective-permute-start | bytes 1228808 | tf_op jit(solution)/shard_map/ppermute | solution.py:292
  22.4 1.8 %shard_map.89 = (f32[400,512]{1,0:T(8,128)S(1)}, f32[8,512]{1,0:T(8,128)S(1)}) custom-call(bf16[400,512]{1,0:T(8,128)(2,1)S(1)} %collective-permute-done.2.prev2, bf16[400,512]{1,0:T(8,128)(2,1)S(1)} %get-tuple-element.25.q2, bf16[400,512]{1,0:T(8,128)(2,1)S(1)} %get-tuple-element.26.r2, ...), custom_call_target="tpu_custom_call", output_to_operand_aliasing={{0}: (7, {})} | custom-call | flops 8000000000 | bytes 4194304 | tf_op jit(solution)/shard_map/pallas_call | solution.py:323
  24.2 0.0 collective-permute-done.3.prev1
  24.3 0.0 copy-start.1
  24.3 1.8 %shard_map.90 = (f32[400,512]{1,0:T(8,128)S(1)}, f32[8,128]{1,0:T(8,128)S(1)}) custom-call(bf16[400,512]{1,0:T(8,128)(2,1)S(1)} %collective-permute-done.3.prev1, bf16[400,512]{1,0:T(8,128)(2,1)S(1)} %get-tuple-element.22.q1, bf16[400,512]{1,0:T(8,128)(2,1)S(1)} %get-tuple-element.23.r1, ...), custom_call_target="tpu_custom_call", output_to_operand_aliasing={{0}: (7, {})} | custom-call | flops 3000000000 | bytes 4194304 | tf_op jit(solution)/shard_map/pallas_call | solution.py:325
  26.1 0.1 collective-permute-start.6
  26.2 0.0 collective-permute-done.1.lists
  26.2 0.0 collective-permute-done.block
  26.2 0.0 copy-done.1
  26.2 0.1 shard_map.91
  26.3 0.7 %collective-permute-start.4 = (bf16[400,512]{1,0:T(8,128)(2,1)S(1)}, bf16[400,512]{1,0:T(8,128)(2,1)S(1)}, u32[]{:S(2)}, u32[]{:S(2)}) collective-permute-start(bf16[400,512]{1,0:T(8,128)(2,1)S(1)} %get-tuple-element.33), channel_id=1, source_target_pairs={{0,2},{2,0},{4,6},{6,4},{8,10},{10,8},{12,14},{14,12},{16,18},{18,... | collective-permute-start | bytes 1228808 | tf_op jit(solution)/shard_map/ppermute | solution.py:292
  27.0 0.1 collective-permute-start.5
  27.1 3.2 %shard_map.92.part = f32[400,512]{1,0:T(8,128)S(1)} custom-call(bf16[400,2560]{1,0:T(8,128)(2,1)S(1)} %bitcast.19, bf16[400,512]{1,0:T(8,128)(2,1)S(1)} %bitcast.14, bf16[400,512]{1,0:T(8,128)(2,1)S(1)} %get-tuple-element.35.next2, bf16[32,512]{1,0:T(8,128)(2,1)S(1)} %get-tuple-element.36.lists, ...), custom_call_target="tpu_custom_call", output_to_operand_aliasing={{}: (4, {})} | custom-call | flops 10000000000 | bytes 4194304 | tf_op jit(solution)/shard_map/pallas_call | solution.py:333
  30.3 0.0 collective-permute-done.6.other
  30.3 2.5 %collective-permute-start.7 = (f32[8,128]{1,0:T(8,128)S(1)}, f32[8,128]{1,0:T(8,128)S(1)}, u32[]{:S(2)}, u32[]{:S(2)}) collective-permute-start(f32[8,128]{1,0:T(8,128)S(1)} %shard_map.93.row), channel_id=1, source_target_pairs={{0,1},{1,0},{2,3},{3,2},{4,5},{5,4},{6,7},{7,6},{8,9},{9,8},{10,11... | collective-permute-start | bytes 12296 | tf_op jit(solution)/shard_map/ppermute | solution.py:336
  32.9 0.0 collective-permute-done.5.lists
  32.9 0.0 collective-permute-done.4.next1
  32.9 3.2 %shard_map.94.own = bf16[400,512]{1,0:T(8,128)(2,1)S(1)} custom-call(bf16[400,2560]{1,0:T(8,128)(2,1)S(1)} %bitcast.20, bf16[400,512]{1,0:T(8,128)(2,1)S(1)} %bitcast.15, bf16[400,512]{1,0:T(8,128)(2,1)S(1)} %collective-permute-done.4.next1, bf16[32,512]{1,0:T(8,128)(2,1)S(1)} %collective-permute-done.5.lists, f32[400,512]{1,0:T(8,128)S(1)} %shard_map.92.part, ...), custom_call_target="tpu_custom_call" | custom-call | flops 10000000000 | bytes 4194304 | tf_op jit(solution)/shard_map/pallas_call | solution.py:337
  36.0 0.0 collective-permute-done.7.other
  36.0 0.8 %collective-permute-start.8 = (bf16[400,512]{1,0:T(8,128)(2,1)S(1)}, bf16[400,512]{1,0:T(8,128)(2,1)S(1)}, u32[]{:S(2)}, u32[]{:S(2)}) collective-permute-start(bf16[400,512]{1,0:T(8,128)(2,1)S(1)} %get-tuple-element.38.own), channel_id=1, source_target_pairs={{0,1},{1,0},{2,3},{3,2},{4,5},{5,4},{6,7},{7,6},{8,9},{9,8},{10,11... | collective-permute-start | bytes 1228808 | tf_op jit(solution)/shard_map/ppermute | solution.py:343
  36.8 14.7 %all_to_all.11 = f32[64,1,128]{2,1,0:T(1,128)S(1)} all-to-all(f32[64,1,128]{2,1,0:T(1,128)S(1)} %bitcast.17), channel_id=1, replica_groups={{0,4,8,12,16,20,24,28,32,36,40,44,48,52,56,60,64,68,72,76,80,84,88,92,9..., dimensions={0} | all-to-all | bytes 65536 | tf_op jit(solution)/shard_map/all_to_all | solution.py:344
  51.5 0.0 collective-permute-done.8.other
  51.5 1.0 %shard_map.96 = (f32[400,512]{1,0:T(8,128)}, f32[1,1]{1,0:T(1,128)}) custom-call(bf16[400,512]{1,0:T(8,128)(2,1)S(1)} %get-tuple-element.38.own, bf16[400,512]{1,0:T(8,128)(2,1)S(1)} %collective-permute-done.8.other, f32[64,128]{1,0:T(8,128)S(1)} %bitcast.16), custom_call_target="tpu_custom_call" | custom-call | flops 1000000 | bytes 4194304 | tf_op jit(solution)/shard_map/pallas_call | solution.py:346
  (3 shorter events, 0.1 us)
Async XLA Ops:
  0.6 20.1 %collective-permute-start.2 = (bf16[400,512]{1,0:T(8,128)(2,1)}, bf16[400,512]{1,0:T(8,128)(2,1)S(1)}, u32[]{:S(2)}, u32[]{:S(2)}) collective-permute-start(bf16[400,512]{1,0:T(8,128)(2,1)} %bitcast.9), channel_id=1, source_target_pairs={{0,4},{2,6},{4,8},{6,10},{8,12},{10,14},{12,16},{14,18},{16,20},{1... | collective-permute-start | bytes 1228808 | tf_op jit(solution)/shard_map/ppermute | solution.py:288
  2.8 23.4 %collective-permute-start = (bf16[400,512]{1,0:T(8,128)(2,1)}, bf16[400,512]{1,0:T(8,128)(2,1)S(1)}, u32[]{:S(2)}, u32[]{:S(2)}) collective-permute-start(bf16[400,512]{1,0:T(8,128)(2,1)} %bitcast.10), channel_id=1, source_target_pairs={{0,252},{2,254},{4,0},{6,2},{8,4},{10,6},{12,8},{14,10},{16,12},{1... | collective-permute-start | bytes 1228808 | tf_op jit(solution)/shard_map/ppermute | solution.py:288
  10.6 3.1 %copy-start = (bf16[512,400]{0,1:T(8,128)(2,1)S(1)}, bf16[512,400]{0,1:T(8,128)(2,1)}, u32[]{:S(2)}) copy-start(bf16[512,400]{0,1:T(8,128)(2,1)} %param.7) | copy-start | bytes 1228804
  10.6 3.1 %copy-start.2 = (bf16[2560,400]{0,1:T(8,128)(2,1)S(1)}, bf16[2560,400]{0,1:T(8,128)(2,1)}, u32[]{:S(2)}) copy-start(bf16[2560,400]{0,1:T(8,128)(2,1)} %param.8) | copy-start | bytes 6144004
  10.6 3.1 %copy-start.3 = (s32[3,512]{1,0:T(4,128)S(1)}, s32[3,512]{1,0:T(4,128)}, u32[]{:S(2)}) copy-start(s32[3,512]{1,0:T(4,128)} %rels.1) | copy-start | bytes 18436
  10.6 3.1 %copy-start.4 = (s32[3,512]{1,0:T(4,128)S(1)}, s32[3,512]{1,0:T(4,128)}, u32[]{:S(2)}) copy-start(s32[3,512]{1,0:T(4,128)} %heads.5) | copy-start | bytes 18436
  10.6 3.1 %copy-start.5 = (s32[3,512]{1,0:T(4,128)S(1)}, s32[3,512]{1,0:T(4,128)}, u32[]{:S(2)}) copy-start(s32[3,512]{1,0:T(4,128)} %tails.5) | copy-start | bytes 18436
  10.6 3.1 %copy-start.6 = (s32[3,2,256]{2,1,0:T(2,128)S(1)}, s32[3,2,256]{2,1,0:T(2,128)}, u32[]{:S(2)}) copy-start(s32[3,2,256]{2,1,0:T(2,128)} %negatives.1) | copy-start | bytes 18436
  10.6 3.1 %copy-start.7 = (s32[3,1]{0,1:T(1,128)S(1)}, s32[3,1]{0,1:T(1,128)}, u32[]{:S(2)}) copy-start(s32[3,1]{0,1:T(1,128)} %param.13) | copy-start | bytes 40
  12.2 14.0 %collective-permute-start.1 = (bf16[32,512]{1,0:T(8,128)(2,1)}, bf16[32,512]{1,0:T(8,128)(2,1)S(1)}, u32[]{:S(2)}, u32[]{:S(2)}) collective-permute-start(bf16[32,512]{1,0:T(8,128)(2,1)} %shard_map.86.own_lists), channel_id=1, source_target_pairs={{0,252},{2,254},{4,0},{6,2},{8,4},{10,6},{12,8},{14,10},{16,12},{1... | collective-permute-start | bytes 98312 | tf_op jit(solution)/shard_map/ppermute | solution.py:288
  20.8 3.4 %collective-permute-start.3 = (bf16[400,512]{1,0:T(8,128)(2,1)S(1)}, bf16[400,512]{1,0:T(8,128)(2,1)S(1)}, u32[]{:S(2)}, u32[]{:S(2)}) collective-permute-start(bf16[400,512]{1,0:T(8,128)(2,1)S(1)} %shard_map.87), channel_id=1, source_target_pairs={{0,2},{2,0},{4,6},{6,4},{8,10},{10,8},{12,14},{14,12},{16,18},{18,... | collective-permute-start | bytes 1228808 | tf_op jit(solution)/shard_map/ppermute | solution.py:292
  24.3 2.0 %copy-start.1 = (bf16[32,512]{1,0:T(8,128)(2,1)S(1)}, bf16[32,512]{1,0:T(8,128)(2,1)}, u32[]{:S(2)}) copy-start(bf16[32,512]{1,0:T(8,128)(2,1)} %shard_map.86.own_lists) | copy-start | bytes 98308
  26.1 4.2 %collective-permute-start.6 = (f32[8,128]{1,0:T(8,128)S(1)}, f32[8,128]{1,0:T(8,128)S(1)}, u32[]{:S(2)}, u32[]{:S(2)}) collective-permute-start(f32[8,128]{1,0:T(8,128)S(1)} %get-tuple-element.32.row), channel_id=1, source_target_pairs={{0,2},{2,0},{4,6},{6,4},{8,10},{10,8},{12,14},{14,12},{16,18},{18,... | collective-permute-start | bytes 12296 | tf_op jit(solution)/shard_map/ppermute | solution.py:292
  26.3 6.6 %collective-permute-start.4 = (bf16[400,512]{1,0:T(8,128)(2,1)S(1)}, bf16[400,512]{1,0:T(8,128)(2,1)S(1)}, u32[]{:S(2)}, u32[]{:S(2)}) collective-permute-start(bf16[400,512]{1,0:T(8,128)(2,1)S(1)} %get-tuple-element.33), channel_id=1, source_target_pairs={{0,2},{2,0},{4,6},{6,4},{8,10},{10,8},{12,14},{14,12},{16,18},{18,... | collective-permute-start | bytes 1228808 | tf_op jit(solution)/shard_map/ppermute | solution.py:292
  27.0 5.8 %collective-permute-start.5 = (bf16[32,512]{1,0:T(8,128)(2,1)S(1)}, bf16[32,512]{1,0:T(8,128)(2,1)S(1)}, u32[]{:S(2)}, u32[]{:S(2)}) collective-permute-start(bf16[32,512]{1,0:T(8,128)(2,1)S(1)} %get-tuple-element.34), channel_id=1, source_target_pairs={{0,2},{2,0},{4,6},{6,4},{8,10},{10,8},{12,14},{14,12},{16,18},{18,... | collective-permute-start | bytes 98312 | tf_op jit(solution)/shard_map/ppermute | solution.py:292
  30.3 5.7 %collective-permute-start.7 = (f32[8,128]{1,0:T(8,128)S(1)}, f32[8,128]{1,0:T(8,128)S(1)}, u32[]{:S(2)}, u32[]{:S(2)}) collective-permute-start(f32[8,128]{1,0:T(8,128)S(1)} %shard_map.93.row), channel_id=1, source_target_pairs={{0,1},{1,0},{2,3},{3,2},{4,5},{5,4},{6,7},{7,6},{8,9},{9,8},{10,11... | collective-permute-start | bytes 12296 | tf_op jit(solution)/shard_map/ppermute | solution.py:336
  36.0 15.5 %collective-permute-start.8 = (bf16[400,512]{1,0:T(8,128)(2,1)S(1)}, bf16[400,512]{1,0:T(8,128)(2,1)S(1)}, u32[]{:S(2)}, u32[]{:S(2)}) collective-permute-start(bf16[400,512]{1,0:T(8,128)(2,1)S(1)} %get-tuple-element.38.own), channel_id=1, source_target_pairs={{0,1},{1,0},{2,3},{3,2},{4,5},{5,4},{6,7},{7,6},{8,9},{9,8},{10,11... | collective-permute-start | bytes 1228808 | tf_op jit(solution)/shard_map/ppermute | solution.py:343
